TPU v7x, 32 devices: a whole 2x2x4 slice. The times are simulated.
32 devices in a mesh: groups: 2 (over x), tensor: 8 (over z, y), section: 2 (over core).
Axes of the slice: x: 2, y: 2, z: 4, core: 2. Of those that a mesh axis runs over, the one named last changes fastest.
Arguments:
- prompt_states: bfloat16 [4, 512, 8192], P(('groups', 'section'), 'tensor'), parts along dimension 0
- decode_states: bfloat16 [4, 32, 8192], P(('groups', 'section'), 'tensor'), parts along dimension 0
- norm_gain: bfloat16 [8192], replicated, may hold values from 0.099609375 to 1.8984375
- w_query: bfloat16 [8192, 4096], P(None, 'tensor'), may hold values from -0.0625 to 0.0625
- w_keyvalue: bfloat16 [8192, 2048], P(None, 'tensor'), may hold values from -0.0625 to 0.0625
- w_output: bfloat16 [4096, 8192], P('tensor'), may hold values from -0.09375 to 0.09375
- cache_pages: bfloat16 [4, 512, 16, 2048], P(('groups', 'section'), 'tensor'), parts along dimension 0
- page_table: int32 [4, 32, 16], P(('groups', 'section'), 'tensor'), parts along dimension 0, may hold values from 0 to 63, as said below
- cache_len: int32 [4, 32], P(('groups', 'section')), parts along dimension 0, may hold values from 1 to 252, as said below
- dest_rank: int32 [4, 4], P('groups'), parts along dimension 0, may hold values from 0 to 7, as said below
- dest_page: int32 [4, 4, 8], P('groups'), parts along dimension 0, may hold values from 0 to 63, as said below
Outputs:
- layer_outputs: bfloat16 [4, 4, 32, 8192], P(None, ('groups', 'section'), 'tensor'), parts along dimension 1
There are 2 independent parts, one for each index of `groups`. A program takes and returns all parts, laid end to end along the dimension named above; an argument that names none is the same for every part. Nothing has to cross between parts.
Inputs may be any that keep to these rules, and one draw needn't show every extreme that they name: `page_table`: each device's table names each of its 64 local pages exactly once. `cache_len`: a request that receives a prompt has that prompt's length, 128 or fewer, and in each half one prompt has length 128; 252 is reached in every draw. `dest_rank`: distinct within a half. `dest_page`: the first 8 entries of the page table of one request of the receiving device.
All inputs are finite; a program needn't handle non-finite values.
Results may differ from a plain program's by a relative error of at most 0.03.
Values may be sent and summed in bfloat16 or wider, within the bound.
No kernel may reach another device: no remote copies, remote signals or barrier semaphores. Data moves between devices by JAX's collectives and lax.ppermute only.
A program may use at most 128 MiB of HBM per device.

v0:
```python
import jax
import jax.numpy as jnp
from jax import lax
from jax.sharding import PartitionSpec as P

HD = 128
PLEN = 128
STEPS = 4


EPS = 1e-05
ROPE_BASE = 500000.0


def from_behind(value, axis, steps):
    count = lax.axis_size(axis)
    pairs = [(source, (source + steps) % count) for source in range(count)]
    return lax.ppermute(value, axis, pairs)


def normalize(rows, gain):
    values = rows.astype(jnp.float32)
    square = jnp.mean(values * values, axis=-1, keepdims=True)
    return (values * lax.rsqrt(square + EPS) * gain.astype(jnp.float32)).astype(jnp.bfloat16)


def rotate(values, positions, head_dim):
    half_dim = head_dim // 2
    freqs = ROPE_BASE ** (-(jnp.arange(half_dim, dtype=jnp.float32) * 2.0 / head_dim))
    angles = positions.astype(jnp.float32)[:, None] * freqs[None, :]
    cosine = jnp.cos(angles)[:, None, :]
    sine = jnp.sin(angles)[:, None, :]
    first = values[..., :half_dim]
    second = values[..., half_dim:]
    return jnp.concatenate(
        [first * cosine - second * sine, second * cosine + first * sine], axis=-1
    )


def rotate_keys(values, positions, first_col, head_dim):
    count_rows, columns = values.shape
    blocks = values.reshape(count_rows, columns // head_dim, head_dim)
    turned = rotate(blocks, positions, head_dim)
    block_index = first_col // head_dim + jnp.arange(columns // head_dim, dtype=jnp.int32)
    is_key = (block_index % 2 == 0)[None, :, None]
    return jnp.where(is_key, turned, blocks).reshape(count_rows, columns)


def attend(query, cache, positions, head_dim):
    count_rows, span, width = cache.shape
    kv_heads = width // (2 * head_dim)
    all_heads = query.shape[1] // head_dim
    paired = cache.reshape(count_rows, span, kv_heads, 2, head_dim)
    keys = paired[:, :, :, 0, :]
    values = paired[:, :, :, 1, :]
    grouped = query.reshape(count_rows, kv_heads, all_heads // kv_heads, head_dim)
    scores = jnp.einsum(
        "rhgd,rlhd->rhgl", grouped, keys, preferred_element_type=jnp.float32
    ) * head_dim ** (-0.5)
    visible = jnp.arange(span, dtype=jnp.int32)[None, :] <= positions[:, None]
    scores = jnp.where(visible[:, None, None, :], scores, -1e30)
    top = jnp.max(scores, axis=-1, keepdims=True)
    weights = jnp.exp(scores - top)
    weights = (weights / jnp.sum(weights, axis=-1, keepdims=True)).astype(jnp.bfloat16)
    mixed = jnp.einsum("rhgl,rlhd->rhgd", weights, values, preferred_element_type=jnp.float32)
    return mixed.astype(jnp.bfloat16).reshape(count_rows, all_heads * head_dim)


def on_device(
    prompt_states,
    decode_states,
    norm_gain,
    w_query,
    w_keyvalue,
    w_output,
    cache_pages,
    page_table,
    cache_len,
    dest_rank,
    dest_page,
):
    tensor_rank = lax.axis_index("tensor")
    section_rank = lax.axis_index("section")
    ntensor = lax.axis_size("tensor")
    kv_cols = w_keyvalue.shape[1]
    q_cols = w_query.shape[1]
    first_kv = tensor_rank * kv_cols
    prompts = dest_rank.shape[1]
    page_pool = cache_pages[0]
    page_size = page_pool.shape[1]
    kv_width = page_pool.shape[2]
    own_table = page_table[0]
    group_lens = cache_len[0]
    requests_dev = decode_states.shape[1]
    anchor = (section_rank + 1) % 2
    piece = lax.all_gather(prompt_states[0], "tensor", axis=0, tiled=True)
    normed = normalize(piece, norm_gain)
    values = jnp.dot(normed, w_keyvalue, preferred_element_type=jnp.float32)
    positions = jnp.arange(piece.shape[0], dtype=jnp.int32) % PLEN
    prompt_kv = rotate_keys(values, positions, first_kv, HD).astype(jnp.bfloat16)
    targets = lax.dynamic_index_in_dim(dest_rank, section_rank, 0, keepdims=False)
    select = (jnp.arange(ntensor, dtype=jnp.int32)[:, None] == targets[None, :]).astype(
        jnp.bfloat16
    )
    flat = prompt_kv.reshape(prompts, -1)
    routed = jnp.dot(select, flat, preferred_element_type=jnp.float32).astype(jnp.bfloat16)
    columns = lax.all_to_all(
        routed.reshape(ntensor, PLEN, prompt_kv.shape[1]),
        "tensor",
        split_axis=0,
        concat_axis=2,
        tiled=True,
    )
    arrived = from_behind(columns, "section", 1)
    sources = lax.dynamic_index_in_dim(dest_rank, anchor, 0, keepdims=False)
    matched = sources == tensor_rank
    found = jnp.any(matched)
    source_pages = lax.dynamic_index_in_dim(dest_page, anchor, 0, keepdims=False)
    landing = jnp.sum(jnp.where(matched[:, None], source_pages, 0), axis=0)
    incoming = arrived.reshape(-1, page_size, kv_width)
    page_pool = page_pool.at[landing].set(jnp.where(found, incoming, page_pool[landing]))
    own_lens = lax.dynamic_slice_in_dim(group_lens, tensor_rank * requests_dev, requests_dev)
    outputs = []
    everyone = lax.all_gather(decode_states[0], "tensor", axis=0, tiled=True)
    for iteration in range(STEPS):
        project_positions = group_lens + iteration
        project_normed = normalize(everyone, norm_gain)
        project_query = jnp.dot(project_normed, w_query, preferred_element_type=jnp.float32)
        project_query = rotate(
            project_query.reshape(everyone.shape[0], -1, HD), project_positions, HD
        ).reshape(everyone.shape[0], -1)
        project_keyvalue = rotate_keys(
            jnp.dot(project_normed, w_keyvalue, preferred_element_type=jnp.float32),
            project_positions,
            first_kv,
            HD,
        )
        projected = jnp.concatenate(
            [project_query.astype(jnp.bfloat16), project_keyvalue.astype(jnp.bfloat16)], axis=1
        )
        pool_now = page_pool
        parcels = projected.reshape(ntensor, requests_dev, -1)
        owned = lax.all_to_all(parcels, "tensor", split_axis=0, concat_axis=2, tiled=True)
        owned = owned.reshape(requests_dev, ntensor, -1)
        query = owned[:, :, :q_cols].reshape(requests_dev, -1)
        keyvalue = owned[:, :, q_cols:].reshape(requests_dev, -1)
        decode_positions = own_lens + iteration
        write_page = jnp.take_along_axis(
            own_table, (decode_positions // page_size)[:, None], axis=1
        )[:, 0]
        pool_now = pool_now.at[write_page, decode_positions % page_size].set(keyvalue)
        cache = pool_now[own_table].reshape(requests_dev, -1, kv_width)
        mixed = attend(query, cache, decode_positions, HD)
        returned = lax.all_to_all(
            mixed.reshape(requests_dev, ntensor, q_cols),
            "tensor",
            split_axis=1,
            concat_axis=0,
            tiled=True,
        )
        head_rows = returned.reshape(-1, q_cols)
        page_pool = pool_now
        partial_value = jnp.dot(head_rows, w_output, preferred_element_type=jnp.float32)
        total = lax.psum(partial_value.astype(jnp.bfloat16), "tensor").astype(jnp.float32)
        everyone = (everyone.astype(jnp.float32) + total).astype(jnp.bfloat16)
        outputs.append(lax.dynamic_slice_in_dim(everyone, tensor_rank * requests_dev, requests_dev))
    return jnp.stack(outputs)[:, None]


def solution(mesh):
    in_specs = (
        P(("groups", "section"), "tensor", None),
        P(("groups", "section"), "tensor", None),
        P(),
        P(None, "tensor"),
        P(None, "tensor"),
        P("tensor", None),
        P(("groups", "section"), "tensor", None, None),
        P(("groups", "section"), "tensor", None),
        P(("groups", "section"), None),
        P("groups", None),
        P("groups", None, None),
    )
    out_specs = P(None, ("groups", "section"), "tensor", None)
    return jax.shard_map(
        on_device, mesh=mesh, in_specs=in_specs, out_specs=out_specs, check_vma=False
    )
```

profile of v0, /device:TPU:0, one launch (start us, length us, event | category | flops | bytes accessed | tf_op | source)
XLA Modules:
  0.0 719.7 jit_solution(800605762207158727)
XLA Ops:
  6.6 4.8 copy.184
  13.7 38.8 %all-gather = bf16[1,32,8192]{2,0,1:T(2,128)(2,1)S(1)} all-gather(bf16[1,4,8192]{2,0,1:T(2,128)(2,1)S(1)} %copy.83), channel_id=2, replica_groups=mesh['groups'=2,'tensor'=8,'section'=2] {'tensor'}, dimensions={1}, use_global_device_ids=true | all-gather | bytes 589824 | tf_op jit(solution)/shard_map/all_gather | solution.py:124
  53.2 3.2 fusion.55
  57.8 5.0 fusion.57
  62.8 84.1 %all-gather.4.cloned.1.call-done = bf16[1,512,8192]{2,1,0:T(8,128)(2,1)} async-done(((bf16[1,64,8192]{2,1,0:T(8,128)(2,1)}), bf16[1,512,8192]{2,1,0:T(8,128)(2,1)}) %all-gather.4.cloned.1.call-update) | async-done | bytes 8388624 | tf_op jit(solution)/shard_map/all_gather | solution.py:96
  146.9 5.3 fusion.4
  152.2 6.3 fusion.7
  160.2 3.5 all-to-all-start.1
  169.0 9.0 %all-to-all-done.1 = bf16[8,128,256]{2,1,0:T(8,128)(2,1)S(1)} async-done(((bf16[8,128,256]{2,1,0:T(8,128)(2,1)}), bf16[8,128,256]{2,1,0:T(8,128)(2,1)S(1)}, u32[]{:S(2)}, u32[]{:S(2)}) %all-to-all-start.1) | async-done | bytes 524320 | tf_op jit(solution)/shard_map/all_to_all | solution.py:107
  178.0 3.6 all-to-all-start
  182.3 6.1 all-to-all-done
  194.3 5.0 gather_fusion.1
  199.2 7.7 %reshape_reshape.37 = bf16[4,256,8,2,128]{4,3,2,1,0:T(2,128)(2,1)} reshape(bf16[64,16,2048]{2,1,0:T(8,128)(2,1)} %gather_fusion.1) | data formatting | bytes 8388608 | tf_op jit(solution)/shard_map/reshape;reshape | solution.py:53
  206.9 9.8 %fusion.111 = (bf16[4,256,8,1,128]{4,3,2,1,0:T(2,128)(2,1)S(1)}, bf16[4,256,8,1,128]{4,3,2,1,0:T(2,128)(2,1)}) fusion(bf16[4,256,8,2,128]{4,3,2,1,0:T(2,128)(2,1)} %reshape_reshape.37), kind=kLoop, calls=%fused_computation.291 | loop fusion | bytes 8388608 | tf_op jit(solution)/shard_map/slice | solution.py:54
  220.6 9.1 %all_to_all.138 = bf16[4,8,512]{2,0,1:T(4,128)(2,1)S(1)} all-to-all(bf16[4,8,512]{2,0,1:T(4,128)(2,1)S(1)} %copy.92), channel_id=1, replica_groups=mesh['groups'=2,'tensor'=8,'section'=2] {'tensor'}, dimensions={1} | all-to-all | bytes 65536 | tf_op jit(solution)/shard_map/all_to_all | solution.py:154
  229.7 5.7 convolution_convert_fusion.4
  235.5 69.9 %all-reduce.5.cloned.1.call-done = bf16[32,8192]{1,0:T(8,128)(2,1)} async-done(((bf16[32,8192]{1,0:T(8,128)(2,1)}), bf16[32,8192]{1,0:T(8,128)(2,1)}) %all-reduce.5.cloned.1.call-update) | async-done | bytes 524304 | tf_op jit(solution)/shard_map/psum | solution.py:164
  306.8 3.1 fusion.63
  309.8 5.0 fusion.65
  316.0 3.8 all-to-all-start.3
  319.9 6.7 all-to-all-done.3
  329.0 5.0 gather_fusion.2
  334.0 7.7 %reshape_reshape.40 = bf16[4,256,8,2,128]{4,3,2,1,0:T(2,128)(2,1)} reshape(bf16[64,16,2048]{2,1,0:T(8,128)(2,1)} %gather_fusion.2) | data formatting | bytes 8388608 | tf_op jit(solution)/shard_map/reshape;reshape | solution.py:53
  341.7 9.8 %fusion.110 = (bf16[4,256,8,1,128]{4,3,2,1,0:T(2,128)(2,1)S(1)}, bf16[4,256,8,1,128]{4,3,2,1,0:T(2,128)(2,1)}) fusion(bf16[4,256,8,2,128]{4,3,2,1,0:T(2,128)(2,1)} %reshape_reshape.40), kind=kLoop, calls=%fused_computation.290 | loop fusion | bytes 8388608 | tf_op jit(solution)/shard_map/slice | solution.py:54
  352.3 2.9 fusion.37
  355.3 9.3 %all_to_all.139 = bf16[4,8,512]{2,0,1:T(4,128)(2,1)S(1)} all-to-all(bf16[4,8,512]{2,0,1:T(4,128)(2,1)S(1)} %copy.96), channel_id=1, replica_groups=mesh['groups'=2,'tensor'=8,'section'=2] {'tensor'}, dimensions={1} | all-to-all | bytes 65536 | tf_op jit(solution)/shard_map/all_to_all | solution.py:154
  364.6 5.7 convolution_convert_fusion.3
  370.4 69.9 %all-reduce.7.cloned.1.call-done = bf16[32,8192]{1,0:T(8,128)(2,1)} async-done(((bf16[32,8192]{1,0:T(8,128)(2,1)}), bf16[32,8192]{1,0:T(8,128)(2,1)}) %all-reduce.7.cloned.1.call-update) | async-done | bytes 524304 | tf_op jit(solution)/shard_map/psum | solution.py:164
  441.7 3.1 fusion.59
  444.7 5.0 fusion.61
  450.3 10.4 %all_to_all.140 = bf16[8,4,768]{2,1,0:T(4,128)(2,1)S(1)} all-to-all(bf16[8,4,768]{2,1,0:T(4,128)(2,1)S(1)} %pad_maximum_fusion.3), channel_id=1, replica_groups=mesh['groups'=2,'tensor'=8,'section'=2] {'tensor'}, dimensions={0} | all-to-all | bytes 98304 | tf_op jit(solution)/shard_map/all_to_all | solution.py:143
  463.1 5.0 gather_fusion.3
  468.1 7.7 %reshape_reshape.43 = bf16[4,256,8,2,128]{4,3,2,1,0:T(2,128)(2,1)} reshape(bf16[64,16,2048]{2,1,0:T(8,128)(2,1)} %gather_fusion.3) | data formatting | bytes 8388608 | tf_op jit(solution)/shard_map/reshape;reshape | solution.py:53
  475.8 9.8 %fusion.109 = (bf16[4,256,8,1,128]{4,3,2,1,0:T(2,128)(2,1)S(1)}, bf16[4,256,8,1,128]{4,3,2,1,0:T(2,128)(2,1)}) fusion(bf16[4,256,8,2,128]{4,3,2,1,0:T(2,128)(2,1)} %reshape_reshape.43), kind=kLoop, calls=%fused_computation.289 | loop fusion | bytes 8388608 | tf_op jit(solution)/shard_map/slice | solution.py:54
  489.5 9.1 %all_to_all.141 = bf16[4,8,512]{2,0,1:T(4,128)(2,1)S(1)} all-to-all(bf16[4,8,512]{2,0,1:T(4,128)(2,1)S(1)} %copy.100), channel_id=1, replica_groups=mesh['groups'=2,'tensor'=8,'section'=2] {'tensor'}, dimensions={1} | all-to-all | bytes 65536 | tf_op jit(solution)/shard_map/all_to_all | solution.py:154
  498.5 5.7 convolution_convert_fusion.2
  504.4 69.9 %all-reduce.9.cloned.1.call-done = bf16[32,8192]{1,0:T(8,128)(2,1)} async-done(((bf16[32,8192]{1,0:T(8,128)(2,1)}), bf16[32,8192]{1,0:T(8,128)(2,1)}) %all-reduce.9.cloned.1.call-update) | async-done | bytes 524304 | tf_op jit(solution)/shard_map/psum | solution.py:164
  575.6 3.1 fusion.53
  578.7 5.0 fusion.54
  584.9 4.1 all-to-all-start.7
  589.0 6.7 all-to-all-done.7
  598.1 4.9 gather_fusion.4
  603.0 7.7 %reshape_reshape.46 = bf16[4,256,8,2,128]{4,3,2,1,0:T(2,128)(2,1)} reshape(bf16[64,16,2048]{2,1,0:T(8,128)(2,1)} %gather_fusion.4) | data formatting | bytes 8388608 | tf_op jit(solution)/shard_map/reshape;reshape | solution.py:53
  610.7 9.9 %fusion.108 = (bf16[4,256,8,1,128]{4,3,2,1,0:T(2,128)(2,1)S(1)}, bf16[4,256,8,1,128]{4,3,2,1,0:T(2,128)(2,1)}) fusion(bf16[4,256,8,2,128]{4,3,2,1,0:T(2,128)(2,1)} %reshape_reshape.46), kind=kLoop, calls=%fused_computation.288 | loop fusion | bytes 8388608 | tf_op jit(solution)/shard_map/slice | solution.py:54
  625.1 3.3 all-to-all-start.8
  628.6 6.4 all-to-all-done.8
  635.1 5.7 convolution_convert_fusion.1
  640.9 69.9 %all-reduce.11.cloned.1.call-done = bf16[32,8192]{1,0:T(8,128)(2,1)} async-done(((bf16[32,8192]{1,0:T(8,128)(2,1)}), bf16[32,8192]{1,0:T(8,128)(2,1)}) %all-reduce.11.cloned.1.call-update) | async-done | bytes 524304 | tf_op jit(solution)/shard_map/psum | solution.py:164
  (167 shorter events, 47.2 us)
Async XLA Ops:
  6.5 7.0 copy-start.2
  6.5 7.0 copy-start.3
  6.5 5.0 copy-start
  6.5 4.9 copy-start.4
  6.5 140.3 %all-gather.4.cloned.1.call-start = ((), (), s32[]{:S(2)}) async-start(), calls=%async_computation.13 | async-start | bytes 9437184 | tf_op jit(solution)/shard_map/all_gather | solution.py:96
  12.9 43.6 %copy-start.6 = (s32[2,4]{1,0:T(2,128)S(1)}, s32[2,4]{1,0:T(2,128)}, u32[]{:S(2)}) copy-start(s32[2,4]{1,0:T(2,128)} %param.22) | copy-start | bytes 100
  146.9 5.3 copy-start.1
  158.4 7.0 copy-start.5
  160.2 17.8 %all-to-all-start.1 = ((bf16[8,128,256]{2,1,0:T(8,128)(2,1)}), bf16[8,128,256]{2,1,0:T(8,128)(2,1)S(1)}, u32[]{:S(2)}, u32[]{:S(2)}) async-start(bf16[8,128,256]{2,1,0:T(8,128)(2,1)} %copy.87), calls=%async_computation.1 | async-start | bytes 1048576 | tf_op jit(solution)/shard_map/all_to_all | solution.py:107
  178.0 10.4 %all-to-all-start = ((bf16[8,4,768]{2,1,0:T(4,128)(2,1)}), bf16[8,4,768]{2,1,0:T(4,128)(2,1)S(1)}, u32[]{:S(2)}, u32[]{:S(2)}) async-start(bf16[8,4,768]{2,1,0:T(4,128)(2,1)} %pad_maximum_fusion.1), calls=%async_computation | async-start | bytes 98304 | tf_op jit(solution)/shard_map/all_to_all | solution.py:143
  181.6 123.8 %all-reduce.5.cloned.1.call-start = ((), (), s32[]{:S(2)}) async-start(), calls=%async_computation.9 | async-start | bytes 1048576 | tf_op jit(solution)/shard_map/psum | solution.py:164
  182.1 6.4 collective-permute-start
  316.0 10.6 %all-to-all-start.3 = ((bf16[8,4,768]{2,1,0:T(4,128)(2,1)}), bf16[8,4,768]{2,1,0:T(4,128)(2,1)S(1)}, u32[]{:S(2)}, u32[]{:S(2)}) async-start(bf16[8,4,768]{2,1,0:T(4,128)(2,1)} %pad_maximum_fusion.2), calls=%async_computation.3 | async-start | bytes 98304 | tf_op jit(solution)/shard_map/all_to_all | solution.py:143
  319.8 120.5 %all-reduce.7.cloned.1.call-start = ((), (), s32[]{:S(2)}) async-start(), calls=%async_computation.10 | async-start | bytes 1048576 | tf_op jit(solution)/shard_map/psum | solution.py:164
  370.4 203.9 %all-reduce.9.cloned.1.call-start = ((), (), s32[]{:S(2)}) async-start(), calls=%async_computation.11 | async-start | bytes 1048576 | tf_op jit(solution)/shard_map/psum | solution.py:164
  584.9 10.9 %all-to-all-start.7 = ((bf16[8,4,768]{2,1,0:T(4,128)(2,1)}), bf16[8,4,768]{2,1,0:T(4,128)(2,1)S(1)}, u32[]{:S(2)}, u32[]{:S(2)}) async-start(bf16[8,4,768]{2,1,0:T(4,128)(2,1)} %pad_maximum_fusion.4), calls=%async_computation.7 | async-start | bytes 98304 | tf_op jit(solution)/shard_map/all_to_all | solution.py:143
  625.1 10.0 %all-to-all-start.8 = ((bf16[4,8,512]{2,0,1:T(4,128)(2,1)}), bf16[4,8,512]{2,0,1:T(4,128)(2,1)S(1)}, u32[]{:S(2)}, u32[]{:S(2)}) async-start(bf16[4,8,512]{2,0,1:T(4,128)(2,1)} %copy.104), calls=%async_computation.8 | async-start | bytes 65536 | tf_op jit(solution)/shard_map/all_to_all | solution.py:154
  628.5 82.4 %all-reduce.11.cloned.1.call-start = ((), (), s32[]{:S(2)}) async-start(), calls=%async_computation.12 | async-start | bytes 1048576 | tf_op jit(solution)/shard_map/psum | solution.py:164
Sparse Core Ops, SparseCore 0:
  11.5 135.3 all-gather.3
  235.6 69.7 all-reduce.4
  370.5 69.7 all-reduce.6
  504.4 69.8 all-reduce.8
  641.0 69.7 all-reduce.10
where the time goes:
time: 730 us; the launch traced here: 720 us
  waiting for transfers between devices  399 us (55%)
  local copies, waits for them, and re-layouts  115 us (16%)
  blocking collectives  76.6 us (10%)
  matrix products  76.5 us (10%)
  other arithmetic  19.4 us (3%)
  starting transfers between devices  18.8 us (3%)
  between operations  14.4 us (2%)
    psum x4, waiting for transfers between devices, on_device(): lax.psum(partial_value.astype(jnp.bfloat16), 'tensor').astype(jnp.float32)  280 us
    all_gather x1, waiting for transfers between devices, on_device(): piece = lax.all_gather(prompt_states[0], 'tensor', axis=0, tiled=True)  84.1 us
    slice x4, local copies, waits for them, and re-layouts, attend(): keys = paired[:, :, :, 0, :]  39.2 us
    all_gather x1, blocking collectives, on_device(): everyone = lax.all_gather(decode_states[0], 'tensor', axis=0, tiled=True)  38.8 us
    another operation x4, local copies, waits for them, and re-layouts, attend(): paired = cache.reshape(count_rows, span, kv_heads, 2, head_dim)  30.8 us
    all_to_all x3, blocking collectives, on_device(): lax.all_to_all(mixed.reshape(requests_dev, ntensor, q_cols), 'tensor', sp...  27.4 us
    dot_general x4, matrix products, on_device(): jnp.dot(head_rows, w_output, preferred_element_type=jnp.float32)  23 us
    dot_general x4, matrix products, on_device(): jnp.dot(project_normed, w_query, preferred_element_type=jnp.float32)  20 us
  transfers between devices with their start and end apart: 11, of which 10 were waited for; matrix products, arithmetic and copies ran while one was open for 3% of the time, Pallas kernels for 0%

commit v1 on v0

v1 whole, which is shorter than its diff:
```python
import functools

import jax
import jax.numpy as jnp
from jax import lax
from jax.experimental import pallas as pl
from jax.experimental.pallas import tpu as pltpu
from jax.sharding import PartitionSpec as P

HD = 128
PLEN = 128
STEPS = 4
EPS = 1e-05
ROPE_BASE = 500000.0
LANES = 8
CHUNKS = 8
VMEM_LIMIT = 44 * 1024 * 1024


def ring_order(count):
    if count == 8:
        return [0, 2, 4, 6, 7, 5, 3, 1]
    return list(range(count))


def ring_shift(value, steps):
    count = lax.axis_size("tensor")
    order = ring_order(count)
    pairs = [(order[i], order[(i + steps) % count]) for i in range(count)]
    return lax.ppermute(value, "tensor", pairs)


def swap_xor(value, mask):
    count = lax.axis_size("tensor")
    return lax.ppermute(value, "tensor", [(s, s ^ mask) for s in range(count)])


def rope_tables(positions):
    half_dim = HD // 2
    freqs = ROPE_BASE ** (-(jnp.arange(half_dim, dtype=jnp.float32) * 2.0 / HD))
    angles = positions.astype(jnp.float32)[:, None] * freqs[None, :]
    cosine = jnp.cos(angles)
    sine = jnp.sin(angles)
    return (
        jnp.concatenate([cosine, cosine], axis=1),
        jnp.concatenate([-sine, sine], axis=1),
    )


def whole():
    return pl.BlockSpec(memory_space=pltpu.VMEM)


def normed_rows(values, gain):
    square = jnp.mean(values * values, axis=-1, keepdims=True)
    return values * lax.rsqrt(square + EPS) * gain


def prepare_kernel(prompt_ref, decode_ref, info_ref, gain_ref, first_ref, second_ref):
    half = first_ref.shape[0]
    gain = gain_ref[...].astype(jnp.float32)
    first_ref[...] = normed_rows(prompt_ref[:half, :].astype(jnp.float32), gain).astype(jnp.bfloat16)
    later = normed_rows(prompt_ref[half:, :].astype(jnp.float32), gain)
    states = normed_rows(decode_ref[...].astype(jnp.float32), gain)
    second_ref[...] = jnp.concatenate(
        [later, states, info_ref[...].astype(jnp.float32)], axis=0
    ).astype(jnp.bfloat16)


def prepare(prompts, decodes, info, gain):
    tokens, width = prompts.shape
    half = tokens // 2
    extra = decodes.shape[0] + info.shape[0]
    return pl.pallas_call(
        prepare_kernel,
        out_shape=(
            jax.ShapeDtypeStruct((half, width), jnp.bfloat16),
            jax.ShapeDtypeStruct((half + extra, width), jnp.bfloat16),
        ),
        in_specs=[whole()] * 4,
        out_specs=(whole(), whole()),
        compiler_params=pltpu.CompilerParams(vmem_limit_bytes=VMEM_LIMIT),
        name="prepare",
    )(prompts, decodes, info, gain)


def parcels_kernel(heads, table_ref, pool_ref, out_ref, held, load_sem, store_sem):
    pages = held.shape[0]
    width = out_ref.shape[-1]

    def load(index):
        return pltpu.make_async_copy(pool_ref.at[table_ref[index]], held.at[index], load_sem.at[index])

    for index in range(pages):
        load(index).start()
    for index in range(pages):
        load(index).wait()
    stores = []
    for target, head in enumerate(heads):
        copy = pltpu.make_async_copy(
            held.at[:, :, pl.ds(head * width, width)], out_ref.at[target], store_sem.at[target]
        )
        copy.start()
        stores.append(copy)
    for copy in stores:
        copy.wait()


def make_parcels(table, pool, heads, width):
    pages, rows, _ = pool.shape
    return pl.pallas_call(
        functools.partial(parcels_kernel, heads),
        out_shape=jax.ShapeDtypeStruct((len(heads), pages, rows, width), jnp.bfloat16),
        in_specs=[pl.BlockSpec(memory_space=pltpu.SMEM), pl.BlockSpec(memory_space=pl.ANY)],
        out_specs=pl.BlockSpec(memory_space=pl.ANY),
        scratch_shapes=[
            pltpu.VMEM(pool.shape, jnp.bfloat16),
            pltpu.SemaphoreType.DMA((pages,)),
            pltpu.SemaphoreType.DMA((len(heads),)),
        ],
        compiler_params=pltpu.CompilerParams(vmem_limit_bytes=VMEM_LIMIT),
        name="parcels",
    )(table, pool)


def patch_kernel(rows, request_ref, offset_ref, arrived_ref, _cache_in, cache_ref, sems):
    copies = []
    for piece in range(arrived_ref.shape[0] // rows):
        offset = pl.multiple_of(offset_ref[piece], rows)
        copy = pltpu.make_async_copy(
            arrived_ref.at[pl.ds(piece * rows, rows), :],
            cache_ref.at[request_ref[piece], pl.ds(offset, rows), :],
            sems.at[piece],
        )
        copy.start()
        copies.append(copy)
    for copy in copies:
        copy.wait()


def patch(requests, offsets, arrived, cache, rows):
    return pl.pallas_call(
        functools.partial(patch_kernel, rows),
        out_shape=jax.ShapeDtypeStruct(cache.shape, cache.dtype),
        in_specs=[
            pl.BlockSpec(memory_space=pltpu.SMEM),
            pl.BlockSpec(memory_space=pltpu.SMEM),
            pl.BlockSpec(memory_space=pl.ANY),
            pl.BlockSpec(memory_space=pl.ANY),
        ],
        out_specs=pl.BlockSpec(memory_space=pl.ANY),
        scratch_shapes=[pltpu.SemaphoreType.DMA((arrived.shape[0] // rows,))],
        input_output_aliases={3: 0},
        compiler_params=pltpu.CompilerParams(vmem_limit_bytes=VMEM_LIMIT),
        name="patch",
    )(requests, offsets, arrived, cache)


def turn(values, cosine, sine):
    return values * cosine + pltpu.roll(values, HD // 2, 1) * sine


def step_kernel(
    blocks,
    earlier,
    *refs,
):
    x_refs = refs[:blocks]
    refs = refs[blocks:]
    order_ref, wq, wkv, wo, cache, mask_ref, cos_ref, sin_ref = refs[:8]
    refs = refs[8:]
    new_refs = refs[:earlier]
    out_ref, fresh_ref = refs[earlier : earlier + 2]
    (x_rows, wq_s, wkv_s, wo_s, cache_s, q_s, score_s, mix_s, new_s, sems) = refs[earlier + 2 :]
    each, width = x_refs[0].shape
    count = blocks * each
    q_cols = wq_s.shape[1]
    heads = q_cols // HD
    depth = width // CHUNKS
    group = count // CHUNKS

    loads = []
    for c in range(CHUNKS):
        span = pl.ds(c * depth, depth)
        loads.append(pltpu.make_async_copy(wq.at[span, :], wq_s.at[span, :], sems.at[0, c]))
        loads.append(pltpu.make_async_copy(wkv.at[span, :], wkv_s.at[span, :], sems.at[1, c]))
    for c in range(CHUNKS):
        span = pl.ds(c * group, group)
        loads.append(pltpu.make_async_copy(cache.at[span], cache_s.at[span], sems.at[2, c]))
    for c in range(CHUNKS):
        span = pl.ds(c * depth, depth)
        loads.append(pltpu.make_async_copy(wo.at[:, span], wo_s.at[:, span], sems.at[3, c]))
    for copy in loads:
        copy.start()

    for k in range(blocks):
        x_rows[k * each : (k + 1) * each, :] = x_refs[k][...].astype(jnp.float32)
    order = order_ref[...]
    q_s[...] = jnp.zeros_like(q_s)

    query = jnp.zeros((count, q_cols), jnp.float32)
    keyvalue = jnp.zeros((count, 2 * HD), jnp.float32)
    for c in range(CHUNKS):
        span = slice(c * depth, (c + 1) * depth)
        x = jnp.dot(
            order, x_rows[:, span].astype(jnp.bfloat16), preferred_element_type=jnp.float32
        ).astype(jnp.bfloat16)
        loads[2 * c].wait()
        query += jnp.dot(x, wq_s[span, :], preferred_element_type=jnp.float32)
        loads[2 * c + 1].wait()
        keyvalue += jnp.dot(x, wkv_s[span, :], preferred_element_type=jnp.float32)

    cosine = cos_ref[...]
    sine = sin_ref[...]
    key = turn(keyvalue[:, :HD], cosine, sine).astype(jnp.bfloat16)
    value = keyvalue[:, HD:].astype(jnp.bfloat16)
    fresh_ref[:, :HD] = key
    fresh_ref[:, HD:] = value
    for j in range(heads):
        turned = turn(query[:, j * HD : (j + 1) * HD], cosine, sine).astype(jnp.bfloat16)
        lane = pl.ds(j, count, LANES)
        q_s[lane, :] = turned.astype(jnp.float32)
        for t in range(earlier):
            new_s[t, 0, lane, :] = new_refs[t][:, :HD].astype(jnp.float32)
            new_s[t, 1, lane, :] = new_refs[t][:, HD:].astype(jnp.float32)
        new_s[earlier, 0, lane, :] = key.astype(jnp.float32)
        new_s[earlier, 1, lane, :] = value.astype(jnp.float32)
    for j in range(heads, LANES):
        lane = pl.ds(j, count, LANES)
        for t in range(earlier + 1):
            for part in range(2):
                new_s[t, part, lane, :] = jnp.zeros((count, HD), jnp.float32)

    base = 2 * CHUNKS
    for r in range(count):
        if r % group == 0:
            loads[base + r // group].wait()
        rows = slice(r * LANES, (r + 1) * LANES)
        score_s[rows, :] = lax.dot_general(
            q_s[rows, :].astype(jnp.bfloat16),
            cache_s[r, :, :HD],
            (((1,), (1,)), ((), ())),
            preferred_element_type=jnp.float32,
        )

    scale = HD**-0.5
    span = score_s.shape[1]
    scores = score_s[...].reshape(count, LANES, span) * scale + mask_ref[...]
    queries = q_s[...]
    fresh_scores = [
        (jnp.sum(queries * new_s[t, 0], axis=-1, keepdims=True) * scale).reshape(count, LANES, 1)
        for t in range(earlier + 1)
    ]
    top = jnp.max(scores, axis=-1, keepdims=True)
    for s in fresh_scores:
        top = jnp.maximum(top, s)
    weights = jnp.exp(scores - top)
    fresh_weights = [jnp.exp(s - top) for s in fresh_scores]
    total = jnp.sum(weights, axis=-1, keepdims=True)
    for w in fresh_weights:
        total = total + w
    score_s[...] = (weights / total).reshape(count * LANES, span)
    fresh_weights = [
        (w / total).reshape(count * LANES, 1).astype(jnp.bfloat16).astype(jnp.float32)
        for w in fresh_weights
    ]
    for r in range(count):
        rows = slice(r * LANES, (r + 1) * LANES)
        mix_s[rows, :] = jnp.dot(
            score_s[rows, :].astype(jnp.bfloat16),
            cache_s[r, :, HD:],
            preferred_element_type=jnp.float32,
        )
    mixed = mix_s[...]
    for t in range(earlier + 1):
        mixed = mixed + fresh_weights[t] * new_s[t, 1]
    mix_s[...] = mixed
    columns = jnp.concatenate(
        [mix_s[pl.ds(j, count, LANES), :].astype(jnp.bfloat16) for j in range(heads)], axis=1
    )

    base = 3 * CHUNKS
    for c in range(CHUNKS):
        span = slice(c * depth, (c + 1) * depth)
        loads[base + c].wait()
        part = jnp.dot(columns, wo_s[:, span], preferred_element_type=jnp.float32)
        for d in range(blocks):
            out_ref[d, :, span] = part[d * each : (d + 1) * each, :].astype(jnp.bfloat16)


def step(x_blocks, order, wq, wkv, wo, cache, mask, cosine, sine, earlier):
    blocks = len(x_blocks)
    each, width = x_blocks[0].shape
    count = blocks * each
    span = cache.shape[1]
    anywhere = pl.BlockSpec(memory_space=pl.ANY)
    q_cols = wq.shape[1]
    return pl.pallas_call(
        functools.partial(step_kernel, blocks, len(earlier)),
        out_shape=(
            jax.ShapeDtypeStruct((blocks, each, width), jnp.bfloat16),
            jax.ShapeDtypeStruct((count, 2 * HD), jnp.bfloat16),
        ),
        in_specs=[whole()] * (blocks + 1) + [anywhere] * 4 + [whole()] * (3 + len(earlier)),
        out_specs=(whole(), whole()),
        scratch_shapes=[
            pltpu.VMEM((count, width), jnp.float32),
            pltpu.VMEM(wq.shape, jnp.bfloat16),
            pltpu.VMEM(wkv.shape, jnp.bfloat16),
            pltpu.VMEM(wo.shape, jnp.bfloat16),
            pltpu.VMEM(cache.shape, jnp.bfloat16),
            pltpu.VMEM((count * LANES, HD), jnp.float32),
            pltpu.VMEM((count * LANES, span), jnp.float32),
            pltpu.VMEM((count * LANES, HD), jnp.float32),
            pltpu.VMEM((len(earlier) + 1, 2, count * LANES, HD), jnp.float32),
            pltpu.SemaphoreType.DMA((4, CHUNKS)),
        ],
        compiler_params=pltpu.CompilerParams(vmem_limit_bytes=VMEM_LIMIT),
        cost_estimate=pl.CostEstimate(
            flops=2 * count * width * (2 * q_cols + 2 * HD),
            bytes_accessed=2 * (2 * wq.size + wkv.size + cache.size),
            transcendentals=count * LANES * span,
        ),
        name="decode_step",
    )(*x_blocks, order, wq, wkv, wo, cache, mask, cosine, sine, *earlier)


def settle_kernel(parts_ref, state_ref, gain_ref, next_ref, normed_ref):
    total = parts_ref[0].astype(jnp.float32)
    for d in range(1, parts_ref.shape[0]):
        total = total + parts_ref[d].astype(jnp.float32)
    state = (state_ref[...].astype(jnp.float32) + total).astype(jnp.bfloat16)
    next_ref[...] = state
    gain = gain_ref[...].astype(jnp.float32)
    normed_ref[...] = normed_rows(state.astype(jnp.float32), gain).astype(jnp.bfloat16)


def settle(parts, state, gain):
    shape = jax.ShapeDtypeStruct(state.shape, jnp.bfloat16)
    return pl.pallas_call(
        settle_kernel,
        out_shape=(shape, shape),
        in_specs=[whole()] * 3,
        out_specs=(whole(), whole()),
        compiler_params=pltpu.CompilerParams(vmem_limit_bytes=VMEM_LIMIT),
        name="settle",
    )(parts, state, gain)


def on_device(
    prompt_states,
    decode_states,
    norm_gain,
    w_query,
    w_keyvalue,
    w_output,
    cache_pages,
    page_table,
    cache_len,
    dest_rank,
    dest_page,
):
    rank = lax.axis_index("tensor")
    section = lax.axis_index("section")
    count = lax.axis_size("tensor")
    pool = cache_pages[0]
    page_size, kv_width = pool.shape[1:]
    own_table = page_table[0]
    lengths = cache_len[0]
    each, width = decode_states.shape[1:]
    tokens = prompt_states.shape[1]
    q_cols = w_query.shape[1]
    kv_heads = kv_width // (2 * HD)
    shared = count // kv_heads if count > kv_heads else 1
    gain = norm_gain[None, :]

    if w_keyvalue.shape[1] < 2 * HD:
        other = swap_xor(w_keyvalue, 1)
        is_key = rank % 2 == 0
        w_kv = jnp.concatenate(
            [jnp.where(is_key, w_keyvalue, other), jnp.where(is_key, other, w_keyvalue)], axis=1
        )
    else:
        w_kv = w_keyvalue

    heads = tuple(target // shared for target in range(count))
    parcels = make_parcels(own_table.reshape(-1), pool, heads, 2 * HD)
    span = own_table.shape[1] * page_size
    cache = lax.all_to_all(
        parcels.reshape(count, each * span, 2 * HD), "tensor", split_axis=0, concat_axis=0, tiled=True
    ).reshape(count * each, span, 2 * HD)

    info = jnp.zeros((LANES - each, width), jnp.bfloat16)
    info = info.at[0, :each].set(own_table[:, 0].astype(jnp.bfloat16))
    first, second = prepare(prompt_states[0], decode_states[0], info, gain)
    order = ring_order(count)
    place = jnp.array([order.index(r) for r in range(count)], jnp.int32)[rank]
    ring = jnp.array(order, jnp.int32)
    half = tokens // 2
    arrivals = [(rank, 0, first), (rank, 1, second)]
    going = [[first, first], [second, second]]
    for hop in range(1, count // 2 + 1):
        for piece in range(2):
            for way in range(2):
                if hop == count // 2 and piece != way:
                    continue
                sign = 1 if way == 0 else -1
                going[piece][way] = ring_shift(going[piece][way], sign)
                source = ring[(place - sign * hop) % count]
                arrivals.append((source, piece, going[piece][way]))
    products = [
        jnp.dot(rows, w_kv, preferred_element_type=jnp.float32)[:half] for _, _, rows in arrivals
    ]
    starts = jnp.stack([source * tokens + piece * half for source, piece, _ in arrivals])
    row_index = (starts[:, None] + jnp.arange(half, dtype=jnp.int32)[None, :]).reshape(-1)
    cosine, sine = rope_tables(row_index % PLEN)
    values = jnp.concatenate(products, axis=0)
    keys = values[:, :HD]
    keys = keys * cosine + jnp.roll(keys, HD // 2, axis=1) * sine
    prompt_kv = jnp.concatenate([keys, values[:, HD:]], axis=1).astype(jnp.bfloat16)
    sections = lax.axis_size("section")
    arrived = lax.ppermute(prompt_kv, "section", [(s, (s + 1) % sections) for s in range(sections)])

    seconds = [(source, rows) for source, piece, rows in arrivals if piece == 1]
    sources = jnp.stack([source for source, _ in seconds])
    first_pages = jnp.stack([rows[half + each, :each] for _, rows in seconds]).astype(jnp.int32)
    anchor = (section + 1) % sections
    targets = lax.dynamic_index_in_dim(dest_rank, anchor, 0, keepdims=False)
    landing = lax.dynamic_index_in_dim(dest_page, anchor, 0, keepdims=False)[:, 0]
    here = (sources[None, :, None] == targets[:, None, None]) & (
        first_pages[None] == landing[:, None, None]
    )
    numbers = sources[:, None] * each + jnp.arange(each, dtype=jnp.int32)[None, :]
    receivers = jnp.sum(jnp.where(here, numbers[None], 0), axis=(1, 2))
    cache = patch(receivers[starts // PLEN], starts % PLEN, arrived, cache, half)

    visible = jnp.arange(span, dtype=jnp.int32)[None, :] < lengths[:, None]
    mask = jnp.where(visible, 0.0, -1e30).astype(jnp.float32)[:, None, :]
    state = decode_states[0]
    blocks = [rows[half : half + each] for _, rows in seconds]
    outputs = []
    earlier = []
    for iteration in range(STEPS):
        rows_of = (sources[:, None] * each + jnp.arange(each, dtype=jnp.int32)[None, :]).reshape(-1)
        chosen = (jnp.arange(count * each, dtype=jnp.int32)[:, None] == rows_of[None, :]).astype(
            jnp.bfloat16
        )
        cosine, sine = rope_tables(lengths + iteration)
        parts, fresh = step(
            blocks, chosen, w_query, w_kv, w_output, cache, mask, cosine, sine, earlier
        )
        earlier.append(fresh)
        parts = lax.all_to_all(parts, "tensor", split_axis=0, concat_axis=0, tiled=True)
        state, normed = settle(parts, state, gain)
        outputs.append(state)
        if iteration + 1 < STEPS:
            blocks = [normed] + [swap_xor(normed, mask_bits) for mask_bits in range(1, count)]
            sources = rank ^ jnp.arange(count, dtype=jnp.int32)
    return jnp.stack(outputs)[:, None]


def solution(mesh):
    in_specs = (
        P(("groups", "section"), "tensor", None),
        P(("groups", "section"), "tensor", None),
        P(),
        P(None, "tensor"),
        P(None, "tensor"),
        P("tensor", None),
        P(("groups", "section"), "tensor", None, None),
        P(("groups", "section"), "tensor", None),
        P(("groups", "section"), None),
        P("groups", None),
        P("groups", None, None),
    )
    out_specs = P(None, ("groups", "section"), "tensor", None)
    return jax.shard_map(
        on_device, mesh=mesh, in_specs=in_specs, out_specs=out_specs, check_vma=False
    )
```

time: 730 us -> 365 us (0.50); the launches traced: 720 us -> 364 us
  waiting for transfers between devices: 399 us -> 102 us
  local copies, waits for them, and re-layouts: 115 us -> 26.2 us
  starting transfers between devices: 18.8 us -> 101 us
  matrix products: 76.5 us -> 17.4 us
  Pallas kernels: 0 us -> 51.6 us
  blocking collectives: 76.6 us -> 47.2 us
  other arithmetic: 19.4 us -> 7.34 us
    psum x4 -> x0, waiting for transfers between devices: 280 us -> none  [on_device(): lax.psum(partial_value.astype(jnp.bfloat16), 'tensor').astype(jnp.float32)]
    ppermute x1 -> x36, starting transfers between devices: 0.07 us -> 90.8 us  [the longest x14 57.2 us: ring_shift(): return lax.ppermute(value, 'tensor', pairs)]
    ppermute x1 -> x36, waiting for transfers between devices: 0.01 us -> 86.8 us  [the longest x14 72.6 us: ring_shift(): return lax.ppermute(value, 'tensor', pairs)]
    all_gather x1 -> x0, waiting for transfers between devices: 84.1 us -> none  [on_device(): piece = lax.all_gather(prompt_states[0], 'tensor', axis=0, tiled=True)]
    dot_general x22 -> x16, matrix products: 76.5 us -> 17.4 us  [on_device(): jnp.dot(rows, w_kv, preferred_element_type=jnp.float32)[:half]]
    pallas_call x0 -> x11, Pallas kernels: none -> 51.6 us  [the longest x4 40.1 us: step(): pl.pallas_call(functools.partial(step_kernel, blocks, len(earlier)), out_...]
    all_gather x1 -> x0, blocking collectives: 38.8 us -> none  [on_device(): everyone = lax.all_gather(decode_states[0], 'tensor', axis=0, tiled=True)]
    slice x12 -> x20, local copies, waits for them, and re-layouts: 39.3 us -> 6.84 us  [the longest x8 3.79 us: on_device(): blocks = [rows[half:half + each] for _, rows in seconds]]
  transfers between devices with their start and end apart: 11 -> 38, of which waited for: 10 -> 13; matrix products, arithmetic and copies ran while one was open for 3% -> 11% of each run, Pallas kernels for 0% -> 2%
where the time goes in v1:
time: 365 us; the launch traced here: 364 us
  waiting for transfers between devices  102 us (28%)
  starting transfers between devices  101 us (28%)
  Pallas kernels  51.6 us (14%)
  blocking collectives  47.2 us (13%)
  local copies, waits for them, and re-layouts  26.2 us (7%)
  matrix products  17.4 us (5%)
  between operations  11 us (3%)
  other arithmetic  7.34 us (2%)
    ppermute x14, waiting for transfers between devices, ring_shift(): return lax.ppermute(value, 'tensor', pairs)  72.6 us
    ppermute x14, starting transfers between devices, ring_shift(): return lax.ppermute(value, 'tensor', pairs)  57.2 us
    all_to_all x3, blocking collectives, on_device(): lax.all_to_all(parts, 'tensor', split_axis=0, concat_axis=0, tiled=True)  47.2 us
    pallas_call x4, Pallas kernels, step(): pl.pallas_call(functools.partial(step_kernel, blocks, len(earlier)), out_...  40.1 us
    ppermute x21, starting transfers between devices, swap_xor(): return lax.ppermute(value, 'tensor', [(s, s ^ mask) for s in range(count)])  33.6 us
    dot_general x16, matrix products, on_device(): jnp.dot(rows, w_kv, preferred_element_type=jnp.float32)[:half]  17.4 us
    all_to_all x1, waiting for transfers between devices, on_device(): lax.all_to_all(parts, 'tensor', split_axis=0, concat_axis=0, tiled=True)  15 us
    ppermute x21, waiting for transfers between devices, swap_xor(): return lax.ppermute(value, 'tensor', [(s, s ^ mask) for s in range(count)])  14.2 us
  transfers between devices with their start and end apart: 38, of which 13 were waited for; matrix products, arithmetic and copies ran while one was open for 11% of the time, Pallas kernels for 2%

profile of v1, /device:TPU:0, one launch (start us, length us, event | category | flops | bytes accessed | tf_op | source)
XLA Modules:
  0.0 363.6 jit_solution(8695071481736155589)
XLA Ops:
  4.4 3.1 collective-permute-start
  7.5 2.0 collective-permute-start.7
  10.3 2.2 copy-done.5
  12.5 7.5 %parcels.1 = bf16[8,64,16,256]{3,2,1,0:T(8,128)(2,1)S(1)} custom-call(s32[64]{0:T(128)S(1)} %reshape_squeeze.3.table_ref, bf16[64,16,2048]{2,1,0:T(8,128)(2,1)S(1)} %bitcast.79), custom_call_target="tpu_custom_call" | custom-call | tf_op jit(solution)/shard_map/parcels/pallas_call | solution.py:111
  20.0 2.0 copy-done.4
  22.0 6.4 %all-to-all-start = ((bf16[8,1024,256]{2,1,0:T(8,128)(2,1)}), bf16[8,1024,256]{2,1,0:T(8,128)(2,1)}, u32[]{:S(2)}, u32[]{:S(2)}) async-start(bf16[8,1024,256]{2,1,0:T(8,128)(2,1)} %bitcast.78), calls=%async_computation | async-start | bytes 8388608 | tf_op jit(solution)/shard_map/all_to_all | solution.py:389
  39.6 4.5 %stack.82 = s32[8]{0:T(128)S(1)} concatenate(s32[1]{0:T(128)} %bitcast.3, s32[1]{0:T(128)} %get-tuple-element.84, s32[1]{0:T(128)} %get-tuple-element.83, s32[1]{0:T(128)} %get-tuple-element.82, s32[1]{0:T(128)} %get-tuple-element.81, s32[1]{0:T(128)} %get-tuple-element.80, s32[1]{0:T(128)} %get-tuple-element.79, s32[1]{0:T(128)} %get-tuple-element.85), dimensions={0} | concatenate | bytes 64 | tf_op jit(solution)/shard_map/stack | solution.py:425
  49.1 3.0 convolution_dynamic-update-slice_fusion.15
  53.0 2.1 collective-permute-start.9
  55.2 1.9 convolution_dynamic-update-slice_fusion.14
  57.0 1.9 convolution_dynamic-update-slice_fusion.13
  58.9 2.0 collective-permute-start.2
  60.9 2.4 collective-permute-start.3
  65.0 48.8 %collective-permute-done.9 = bf16[32,8192]{1,0:T(8,128)(2,1)S(1)} collective-permute-done((bf16[32,8192]{1,0:T(8,128)(2,1)}, bf16[32,8192]{1,0:T(8,128)(2,1)S(1)}, u32[]{:S(2)}, u32[]{:S(2)}) %collective-permute-start.9) | collective-permute-done | bytes 524320 | tf_op jit(solution)/shard_map/ppermute | solution.py:30
  113.8 23.6 %collective-permute-start.11 = (bf16[32,8192]{1,0:T(8,128)(2,1)S(1)}, bf16[32,8192]{1,0:T(8,128)(2,1)S(1)}, u32[]{:S(2)}, u32[]{:S(2)}) collective-permute-start(bf16[32,8192]{1,0:T(8,128)(2,1)S(1)} %collective-permute-done.9), channel_id=1, source_target_pairs={{0,4},{4,8},{8,12},{12,14},{14,10},{10,6},{6,2},{2,0},{1,5},{5,9},... | collective-permute-start | bytes 1572872 | tf_op jit(solution)/shard_map/ppermute | solution.py:30
  139.1 12.3 %collective-permute-start.4 = (bf16[40,8192]{1,0:T(8,128)(2,1)S(1)}, bf16[40,8192]{1,0:T(8,128)(2,1)S(1)}, u32[]{:S(2)}, u32[]{:S(2)}) collective-permute-start(bf16[40,8192]{1,0:T(8,128)(2,1)S(1)} %collective-permute-done.2), channel_id=1, source_target_pairs={{0,4},{4,8},{8,12},{12,14},{14,10},{10,6},{6,2},{2,0},{1,5},{5,9},... | collective-permute-start | bytes 1966088 | tf_op jit(solution)/shard_map/ppermute | solution.py:30
  153.1 9.5 %collective-permute-start.13 = (bf16[32,8192]{1,0:T(8,128)(2,1)S(1)}, bf16[32,8192]{1,0:T(8,128)(2,1)S(1)}, u32[]{:S(2)}, u32[]{:S(2)}) collective-permute-start(bf16[32,8192]{1,0:T(8,128)(2,1)S(1)} %collective-permute-done.11), channel_id=1, source_target_pairs={{0,4},{4,8},{8,12},{12,14},{14,10},{10,6},{6,2},{2,0},{1,5},{5,9},... | collective-permute-start | bytes 1572872 | tf_op jit(solution)/shard_map/ppermute | solution.py:30
  164.3 2.0 collective-permute-done.5
  168.0 6.6 %collective-permute-done.13 = bf16[32,8192]{1,0:T(8,128)(2,1)S(1)} collective-permute-done((bf16[32,8192]{1,0:T(8,128)(2,1)S(1)}, bf16[32,8192]{1,0:T(8,128)(2,1)S(1)}, u32[]{:S(2)}, u32[]{:S(2)}) %collective-permute-start.13) | collective-permute-done | bytes 524320 | tf_op jit(solution)/shard_map/ppermute | solution.py:30
  175.4 15.1 %collective-permute-done.6 = bf16[40,8192]{1,0:T(8,128)(2,1)S(1)} collective-permute-done((bf16[40,8192]{1,0:T(8,128)(2,1)S(1)}, bf16[40,8192]{1,0:T(8,128)(2,1)S(1)}, u32[]{:S(2)}, u32[]{:S(2)}) %collective-permute-start.6) | collective-permute-done | bytes 655392 | tf_op jit(solution)/shard_map/ppermute | solution.py:30
  204.3 10.5 %decode_step.4 = (bf16[8,4,8192]{2,1,0:T(4,128)(2,1)}, bf16[32,256]{1,0:T(8,128)(2,1)S(1)}) custom-call(bf16[4,8192]{1,0:T(4,128)(2,1)S(1)} %slice.113.refs_0_, bf16[4,8192]{1,0:T(4,128)(2,1)S(1)} %slice.152.refs_1_, bf16[4,8192]{1,0:T(4,128)(2,1)S(1)} %slice.153.refs_2_, bf16[4,8192]{1,0:T(4,128)(2,1)S(1)} %slice.154.refs_3_, ...), custom_call_target="tpu_custom_call" | custom-call | flops 671088640 | bytes 25165824 | tf_op jit(solution)/shard_map/decode_step/pallas_call | solution.py:298
  214.8 3.9 %all-to-all-start.1 = ((bf16[8,4,8192]{2,1,0:T(4,128)(2,1)}), bf16[8,4,8192]{2,1,0:T(4,128)(2,1)S(1)}, u32[]{:S(2)}, u32[]{:S(2)}) async-start(bf16[8,4,8192]{2,1,0:T(4,128)(2,1)} %get-tuple-element.35), calls=%async_computation.1 | async-start | bytes 1048576 | tf_op jit(solution)/shard_map/all_to_all | solution.py:453
  218.8 15.0 %all-to-all-done.1.parts_ref = bf16[8,4,8192]{2,1,0:T(4,128)(2,1)S(1)} async-done(((bf16[8,4,8192]{2,1,0:T(4,128)(2,1)}), bf16[8,4,8192]{2,1,0:T(4,128)(2,1)S(1)}, u32[]{:S(2)}, u32[]{:S(2)}) %all-to-all-start.1) | async-done | bytes 524320 | tf_op jit(solution)/shard_map/all_to_all | solution.py:453
  234.1 1.5 collective-permute-start.15
  235.6 2.0 collective-permute-start.17
  237.8 3.7 %collective-permute-start.19 = (bf16[4,8192]{1,0:T(4,128)(2,1)S(1)}, bf16[4,8192]{1,0:T(4,128)(2,1)S(1)}, u32[]{:S(2)}, u32[]{:S(2)}) collective-permute-start(bf16[4,8192]{1,0:T(4,128)(2,1)S(1)} %get-tuple-element.37.refs_0_), channel_id=1, source_target_pairs={{0,10},{2,8},{4,14},{6,12},{8,2},{10,0},{12,6},{14,4},{1,11},{3,9}... | collective-permute-start | bytes 196616 | tf_op jit(solution)/shard_map/ppermute | solution.py:35
  242.9 2.4 collective-permute-start.21
  245.4 2.3 collective-permute-done.18.refs_4_
  247.7 2.6 collective-permute-done.19.refs_5_
  250.3 2.2 copy-done.3
  252.5 9.7 %decode_step.5 = (bf16[8,4,8192]{2,1,0:T(4,128)(2,1)S(1)}, bf16[32,256]{1,0:T(8,128)(2,1)S(1)}) custom-call(bf16[4,8192]{1,0:T(4,128)(2,1)S(1)} %get-tuple-element.37.refs_0_, bf16[4,8192]{1,0:T(4,128)(2,1)S(1)} %collective-permute-done.15.refs_1_, bf16[4,8192]{1,0:T(4,128)(2,1)S(1)} %collective-permute-done.16.refs_2_, ...), custom_call_target="tpu_custom_call" | custom-call | flops 671088640 | bytes 25165824 | tf_op jit(solution)/shard_map/decode_step/pallas_call | solution.py:298
  262.2 17.4 %all_to_all.25.parts_ref = bf16[8,4,8192]{2,1,0:T(4,128)(2,1)S(1)} all-to-all(bf16[8,4,8192]{2,1,0:T(4,128)(2,1)S(1)} %get-tuple-element.39), channel_id=1, replica_groups=mesh['groups'=2,'tensor'=8,'section'=2] {'tensor'}, dimensions={0} | all-to-all | bytes 1048576 | tf_op jit(solution)/shard_map/all_to_all | solution.py:453
  279.9 1.6 collective-permute-start.22
  281.5 2.0 collective-permute-start.24
  284.6 2.8 collective-permute-start.26
  288.8 2.4 collective-permute-start.28
  292.7 2.2 collective-permute-done.26.refs_5_
  295.9 9.8 %decode_step.6 = (bf16[8,4,8192]{2,1,0:T(4,128)(2,1)S(1)}, bf16[32,256]{1,0:T(8,128)(2,1)S(1)}) custom-call(bf16[4,8192]{1,0:T(4,128)(2,1)S(1)} %get-tuple-element.41.refs_0_, bf16[4,8192]{1,0:T(4,128)(2,1)S(1)} %collective-permute-done.22.refs_1_, bf16[4,8192]{1,0:T(4,128)(2,1)S(1)} %collective-permute-done.23.refs_2_, ...), custom_call_target="tpu_custom_call" | custom-call | flops 671088640 | bytes 25165824 | tf_op jit(solution)/shard_map/decode_step/pallas_call | solution.py:298
  305.6 15.7 %all_to_all.26.parts_ref = bf16[8,4,8192]{2,1,0:T(4,128)(2,1)S(1)} all-to-all(bf16[8,4,8192]{2,1,0:T(4,128)(2,1)S(1)} %get-tuple-element.43), channel_id=1, replica_groups=mesh['groups'=2,'tensor'=8,'section'=2] {'tensor'}, dimensions={0} | all-to-all | bytes 1048576 | tf_op jit(solution)/shard_map/all_to_all | solution.py:453
  321.6 1.5 collective-permute-start.29
  323.1 2.0 collective-permute-start.31
  326.3 2.7 collective-permute-start.33
  329.0 1.5 collective-permute-start.34
  330.5 2.3 collective-permute-start.35
  333.7 1.9 collective-permute-done.33.refs_5_
  335.6 2.0 collective-permute-done.35.refs_7_
  337.6 10.1 %decode_step.7 = (bf16[8,4,8192]{2,1,0:T(4,128)(2,1)S(1)}, bf16[32,256]{1,0:T(8,128)(2,1)}) custom-call(bf16[4,8192]{1,0:T(4,128)(2,1)S(1)} %get-tuple-element.45.refs_0_, bf16[4,8192]{1,0:T(4,128)(2,1)S(1)} %collective-permute-done.29.refs_1_, bf16[4,8192]{1,0:T(4,128)(2,1)S(1)} %collective-permute-done.30.refs_2_, ...), custom_call_target="tpu_custom_call" | custom-call | flops 671088640 | bytes 25165824 | tf_op jit(solution)/shard_map/decode_step/pallas_call | solution.py:298
  347.7 14.1 %all_to_all.27.parts_ref = bf16[8,4,8192]{2,1,0:T(4,128)(2,1)S(1)} all-to-all(bf16[8,4,8192]{2,1,0:T(4,128)(2,1)S(1)} %get-tuple-element.47), channel_id=1, replica_groups=mesh['groups'=2,'tensor'=8,'section'=2] {'tensor'}, dimensions={0} | all-to-all | bytes 1048576 | tf_op jit(solution)/shard_map/all_to_all | solution.py:453
  (171 shorter events, 46.0 us)
Async XLA Ops:
  0.0 44.3 %copy-start = (s32[2,4,8]{2,1,0:T(4,128)S(1)}, s32[2,4,8]{2,1,0:T(4,128)}, u32[]{:S(2)}) copy-start(s32[2,4,8]{2,1,0:T(4,128)} %param.25) | copy-start | bytes 772
  4.4 54.5 %collective-permute-start = (bf16[40,8192]{1,0:T(8,128)(2,1)S(1)}, bf16[40,8192]{1,0:T(8,128)(2,1)S(1)}, u32[]{:S(2)}, u32[]{:S(2)}) collective-permute-start(bf16[40,8192]{1,0:T(8,128)(2,1)S(1)} %get-tuple-element.33), channel_id=1, source_target_pairs={{0,4},{4,8},{8,12},{12,14},{14,10},{10,6},{6,2},{2,0},{1,5},{5,9},... | collective-permute-start | bytes 1966088 | tf_op jit(solution)/shard_map/ppermute | solution.py:30
  7.5 53.5 %collective-permute-start.1 = (bf16[40,8192]{1,0:T(8,128)(2,1)S(1)}, bf16[40,8192]{1,0:T(8,128)(2,1)S(1)}, u32[]{:S(2)}, u32[]{:S(2)}) collective-permute-start(bf16[40,8192]{1,0:T(8,128)(2,1)S(1)} %get-tuple-element.33), channel_id=1, source_target_pairs={{0,2},{4,0},{8,4},{12,8},{14,12},{10,14},{6,10},{2,6},{1,3},{5,1},... | collective-permute-start | bytes 1966088 | tf_op jit(solution)/shard_map/ppermute | solution.py:30
  7.5 45.5 %collective-permute-start.7 = (bf16[32,8192]{1,0:T(8,128)(2,1)S(1)}, bf16[32,8192]{1,0:T(8,128)(2,1)}, u32[]{:S(2)}, u32[]{:S(2)}) collective-permute-start(bf16[32,8192]{1,0:T(8,128)(2,1)S(1)} %get-tuple-element.34), channel_id=1, source_target_pairs={{0,4},{4,8},{8,12},{12,14},{14,10},{10,6},{6,2},{2,0},{1,5},{5,9},... | collective-permute-start | bytes 1572872 | tf_op jit(solution)/shard_map/ppermute | solution.py:30
  9.5 45.6 %collective-permute-start.8 = (bf16[32,8192]{1,0:T(8,128)(2,1)S(1)}, bf16[32,8192]{1,0:T(8,128)(2,1)}, u32[]{:S(2)}, u32[]{:S(2)}) collective-permute-start(bf16[32,8192]{1,0:T(8,128)(2,1)S(1)} %get-tuple-element.34), channel_id=1, source_target_pairs={{0,2},{4,0},{8,4},{12,8},{14,12},{10,14},{6,10},{2,6},{1,3},{5,1},... | collective-permute-start | bytes 1572872 | tf_op jit(solution)/shard_map/ppermute | solution.py:30
  22.0 22.8 %copy-start.22 = (s32[2,4]{1,0:T(2,128)S(1)}, s32[2,4]{1,0:T(2,128)}, u32[]{:S(2)}) copy-start(s32[2,4]{1,0:T(2,128)} %param.24) | copy-start | bytes 100
  22.0 25.1 %copy-start.21 = (s32[1,32]{1,0:T(1,128)S(1)}, s32[1,32]{1,0:T(1,128)}, u32[]{:S(2)}) copy-start(s32[1,32]{1,0:T(1,128)} %param.23) | copy-start | bytes 388
  22.0 179.9 %all-to-all-start = ((bf16[8,1024,256]{2,1,0:T(8,128)(2,1)}), bf16[8,1024,256]{2,1,0:T(8,128)(2,1)}, u32[]{:S(2)}, u32[]{:S(2)}) async-start(bf16[8,1024,256]{2,1,0:T(8,128)(2,1)} %bitcast.78), calls=%async_computation | async-start | bytes 8388608 | tf_op jit(solution)/shard_map/all_to_all | solution.py:389
  53.0 60.8 %collective-permute-start.9 = (bf16[32,8192]{1,0:T(8,128)(2,1)}, bf16[32,8192]{1,0:T(8,128)(2,1)S(1)}, u32[]{:S(2)}, u32[]{:S(2)}) collective-permute-start(bf16[32,8192]{1,0:T(8,128)(2,1)} %collective-permute-done.7), channel_id=1, source_target_pairs={{0,4},{4,8},{8,12},{12,14},{14,10},{10,6},{6,2},{2,0},{1,5},{5,9},... | collective-permute-start | bytes 1572872 | tf_op jit(solution)/shard_map/ppermute | solution.py:30
  55.1 82.4 %collective-permute-start.10 = (bf16[32,8192]{1,0:T(8,128)(2,1)}, bf16[32,8192]{1,0:T(8,128)(2,1)S(1)}, u32[]{:S(2)}, u32[]{:S(2)}) collective-permute-start(bf16[32,8192]{1,0:T(8,128)(2,1)} %collective-permute-done.8), channel_id=1, source_target_pairs={{0,2},{4,0},{8,4},{12,8},{14,12},{10,14},{6,10},{2,6},{1,3},{5,1},... | collective-permute-start | bytes 1572872 | tf_op jit(solution)/shard_map/ppermute | solution.py:30
  58.9 80.2 %collective-permute-start.2 = (bf16[40,8192]{1,0:T(8,128)(2,1)S(1)}, bf16[40,8192]{1,0:T(8,128)(2,1)S(1)}, u32[]{:S(2)}, u32[]{:S(2)}) collective-permute-start(bf16[40,8192]{1,0:T(8,128)(2,1)S(1)} %collective-permute-done), channel_id=1, source_target_pairs={{0,4},{4,8},{8,12},{12,14},{14,10},{10,6},{6,2},{2,0},{1,5},{5,9},... | collective-permute-start | bytes 1966088 | tf_op jit(solution)/shard_map/ppermute | solution.py:30
  60.9 90.5 %collective-permute-start.3 = (bf16[40,8192]{1,0:T(8,128)(2,1)S(1)}, bf16[40,8192]{1,0:T(8,128)(2,1)S(1)}, u32[]{:S(2)}, u32[]{:S(2)}) collective-permute-start(bf16[40,8192]{1,0:T(8,128)(2,1)S(1)} %collective-permute-done.1), channel_id=1, source_target_pairs={{0,2},{4,0},{8,4},{12,8},{14,12},{10,14},{6,10},{2,6},{1,3},{5,1},... | collective-permute-start | bytes 1966088 | tf_op jit(solution)/shard_map/ppermute | solution.py:30
  113.8 39.3 %collective-permute-start.11 = (bf16[32,8192]{1,0:T(8,128)(2,1)S(1)}, bf16[32,8192]{1,0:T(8,128)(2,1)S(1)}, u32[]{:S(2)}, u32[]{:S(2)}) collective-permute-start(bf16[32,8192]{1,0:T(8,128)(2,1)S(1)} %collective-permute-done.9), channel_id=1, source_target_pairs={{0,4},{4,8},{8,12},{12,14},{14,10},{10,6},{6,2},{2,0},{1,5},{5,9},... | collective-permute-start | bytes 1572872 | tf_op jit(solution)/shard_map/ppermute | solution.py:30
  137.5 26.0 %collective-permute-start.12 = (bf16[32,8192]{1,0:T(8,128)(2,1)S(1)}, bf16[32,8192]{1,0:T(8,128)(2,1)S(1)}, u32[]{:S(2)}, u32[]{:S(2)}) collective-permute-start(bf16[32,8192]{1,0:T(8,128)(2,1)S(1)} %collective-permute-done.10), channel_id=1, source_target_pairs={{0,2},{4,0},{8,4},{12,8},{14,12},{10,14},{6,10},{2,6},{1,3},{5,1},... | collective-permute-start | bytes 1572872 | tf_op jit(solution)/shard_map/ppermute | solution.py:30
  139.1 27.2 %collective-permute-start.4 = (bf16[40,8192]{1,0:T(8,128)(2,1)S(1)}, bf16[40,8192]{1,0:T(8,128)(2,1)S(1)}, u32[]{:S(2)}, u32[]{:S(2)}) collective-permute-start(bf16[40,8192]{1,0:T(8,128)(2,1)S(1)} %collective-permute-done.2), channel_id=1, source_target_pairs={{0,4},{4,8},{8,12},{12,14},{14,10},{10,6},{6,2},{2,0},{1,5},{5,9},... | collective-permute-start | bytes 1966088 | tf_op jit(solution)/shard_map/ppermute | solution.py:30
  151.4 14.9 %collective-permute-start.5 = (bf16[40,8192]{1,0:T(8,128)(2,1)S(1)}, bf16[40,8192]{1,0:T(8,128)(2,1)S(1)}, u32[]{:S(2)}, u32[]{:S(2)}) collective-permute-start(bf16[40,8192]{1,0:T(8,128)(2,1)S(1)} %collective-permute-done.3), channel_id=1, source_target_pairs={{0,2},{4,0},{8,4},{12,8},{14,12},{10,14},{6,10},{2,6},{1,3},{5,1},... | collective-permute-start | bytes 1966088 | tf_op jit(solution)/shard_map/ppermute | solution.py:30
  153.1 21.5 %collective-permute-start.13 = (bf16[32,8192]{1,0:T(8,128)(2,1)S(1)}, bf16[32,8192]{1,0:T(8,128)(2,1)S(1)}, u32[]{:S(2)}, u32[]{:S(2)}) collective-permute-start(bf16[32,8192]{1,0:T(8,128)(2,1)S(1)} %collective-permute-done.11), channel_id=1, source_target_pairs={{0,4},{4,8},{8,12},{12,14},{14,10},{10,6},{6,2},{2,0},{1,5},{5,9},... | collective-permute-start | bytes 1572872 | tf_op jit(solution)/shard_map/ppermute | solution.py:30
  166.3 24.2 %collective-permute-start.6 = (bf16[40,8192]{1,0:T(8,128)(2,1)S(1)}, bf16[40,8192]{1,0:T(8,128)(2,1)S(1)}, u32[]{:S(2)}, u32[]{:S(2)}) collective-permute-start(bf16[40,8192]{1,0:T(8,128)(2,1)S(1)} %collective-permute-done.5), channel_id=1, source_target_pairs={{0,2},{4,0},{8,4},{12,8},{14,12},{10,14},{6,10},{2,6},{1,3},{5,1},... | collective-permute-start | bytes 1966088 | tf_op jit(solution)/shard_map/ppermute | solution.py:30
  175.4 16.5 %copy-start.20 = (s32[4,8]{1,0:T(4,128)S(1)}, s32[4,8]{1,0:T(4,128)}, u32[]{:S(2)}) copy-start(s32[4,8]{1,0:T(4,128)} %dynamic-slice_bitcast_fusion) | copy-start | bytes 388
  191.9 10.1 %collective-permute-start.14 = (bf16[512,256]{1,0:T(8,128)(2,1)S(1)}, bf16[512,256]{1,0:T(8,128)(2,1)S(1)}, u32[]{:S(2)}, u32[]{:S(2)}) collective-permute-start(bf16[512,256]{1,0:T(8,128)(2,1)S(1)} %pad_maximum_fusion), channel_id=1, source_target_pairs={{0,1},{1,0},{2,3},{3,2},{4,5},{5,4},{6,7},{7,6},{8,9},{9,8},{10,11... | collective-permute-start | bytes 786440 | tf_op jit(solution)/shard_map/ppermute | solution.py:422
  204.3 29.5 %copy-start.8 = (bf16[1,4,8192]{2,1,0:T(4,128)(2,1)S(1)}, bf16[1,4,8192]{2,1,0:T(4,128)(2,1)}, u32[]{:S(2)}) copy-start(bf16[1,4,8192]{2,1,0:T(4,128)(2,1)} %param.16) | copy-start | bytes 196612
  204.3 41.0 %copy-start.15 = (f32[32,64]{1,0:T(8,128)S(1)}, f32[32,64]{1,0:T(8,128)}, u32[]{:S(2)}) copy-start(f32[32,64]{1,0:T(8,128)} %get-tuple-element.69) | copy-start | bytes 24580
  204.3 41.0 %copy-start.16 = (f32[32,64]{1,0:T(8,128)S(1)}, f32[32,64]{1,0:T(8,128)}, u32[]{:S(2)}) copy-start(f32[32,64]{1,0:T(8,128)} %get-tuple-element.70) | copy-start | bytes 24580
  204.3 41.0 %copy-start.17 = (f32[32,64]{1,0:T(8,128)S(1)}, f32[32,64]{1,0:T(8,128)}, u32[]{:S(2)}) copy-start(f32[32,64]{1,0:T(8,128)} %get-tuple-element.71) | copy-start | bytes 24580
  214.8 19.0 %all-to-all-start.1 = ((bf16[8,4,8192]{2,1,0:T(4,128)(2,1)}), bf16[8,4,8192]{2,1,0:T(4,128)(2,1)S(1)}, u32[]{:S(2)}, u32[]{:S(2)}) async-start(bf16[8,4,8192]{2,1,0:T(4,128)(2,1)} %get-tuple-element.35), calls=%async_computation.1 | async-start | bytes 1048576 | tf_op jit(solution)/shard_map/all_to_all | solution.py:453
  234.1 7.4 %collective-permute-start.15 = (bf16[4,8192]{1,0:T(4,128)(2,1)S(1)}, bf16[4,8192]{1,0:T(4,128)(2,1)S(1)}, u32[]{:S(2)}, u32[]{:S(2)}) collective-permute-start(bf16[4,8192]{1,0:T(4,128)(2,1)S(1)} %get-tuple-element.37.refs_0_), channel_id=1, source_target_pairs={{0,2},{2,0},{4,6},{6,4},{8,10},{10,8},{12,14},{14,12},{1,3},{3,1},... | collective-permute-start | bytes 196616 | tf_op jit(solution)/shard_map/ppermute | solution.py:35
  235.6 7.3 %collective-permute-start.16 = (bf16[4,8192]{1,0:T(4,128)(2,1)S(1)}, bf16[4,8192]{1,0:T(4,128)(2,1)S(1)}, u32[]{:S(2)}, u32[]{:S(2)}) collective-permute-start(bf16[4,8192]{1,0:T(4,128)(2,1)S(1)} %get-tuple-element.37.refs_0_), channel_id=1, source_target_pairs={{0,4},{2,6},{4,0},{6,2},{8,12},{10,14},{12,8},{14,10},{1,5},{3,7},... | collective-permute-start | bytes 196616 | tf_op jit(solution)/shard_map/ppermute | solution.py:35
  235.6 9.8 %collective-permute-start.17 = (bf16[4,8192]{1,0:T(4,128)(2,1)S(1)}, bf16[4,8192]{1,0:T(4,128)(2,1)S(1)}, u32[]{:S(2)}, u32[]{:S(2)}) collective-permute-start(bf16[4,8192]{1,0:T(4,128)(2,1)S(1)} %get-tuple-element.37.refs_0_), channel_id=1, source_target_pairs={{0,6},{2,4},{4,2},{6,0},{8,14},{10,12},{12,10},{14,8},{1,7},{3,5},... | collective-permute-start | bytes 196616 | tf_op jit(solution)/shard_map/ppermute | solution.py:35
  237.6 10.0 %collective-permute-start.18 = (bf16[4,8192]{1,0:T(4,128)(2,1)S(1)}, bf16[4,8192]{1,0:T(4,128)(2,1)S(1)}, u32[]{:S(2)}, u32[]{:S(2)}) collective-permute-start(bf16[4,8192]{1,0:T(4,128)(2,1)S(1)} %get-tuple-element.37.refs_0_), channel_id=1, source_target_pairs={{0,8},{2,10},{4,12},{6,14},{8,0},{10,2},{12,4},{14,6},{1,9},{3,11}... | collective-permute-start | bytes 196616 | tf_op jit(solution)/shard_map/ppermute | solution.py:35
  237.8 12.5 %collective-permute-start.19 = (bf16[4,8192]{1,0:T(4,128)(2,1)S(1)}, bf16[4,8192]{1,0:T(4,128)(2,1)S(1)}, u32[]{:S(2)}, u32[]{:S(2)}) collective-permute-start(bf16[4,8192]{1,0:T(4,128)(2,1)S(1)} %get-tuple-element.37.refs_0_), channel_id=1, source_target_pairs={{0,10},{2,8},{4,14},{6,12},{8,2},{10,0},{12,6},{14,4},{1,11},{3,9}... | collective-permute-start | bytes 196616 | tf_op jit(solution)/shard_map/ppermute | solution.py:35
  241.5 8.8 %collective-permute-start.20 = (bf16[4,8192]{1,0:T(4,128)(2,1)S(1)}, bf16[4,8192]{1,0:T(4,128)(2,1)S(1)}, u32[]{:S(2)}, u32[]{:S(2)}) collective-permute-start(bf16[4,8192]{1,0:T(4,128)(2,1)S(1)} %get-tuple-element.37.refs_0_), channel_id=1, source_target_pairs={{0,12},{2,14},{4,8},{6,10},{8,4},{10,6},{12,0},{14,2},{1,13},{3,15... | collective-permute-start | bytes 196616 | tf_op jit(solution)/shard_map/ppermute | solution.py:35
  242.9 7.4 %collective-permute-start.21 = (bf16[4,8192]{1,0:T(4,128)(2,1)S(1)}, bf16[4,8192]{1,0:T(4,128)(2,1)S(1)}, u32[]{:S(2)}, u32[]{:S(2)}) collective-permute-start(bf16[4,8192]{1,0:T(4,128)(2,1)S(1)} %get-tuple-element.37.refs_0_), channel_id=1, source_target_pairs={{0,14},{2,12},{4,10},{6,8},{8,6},{10,4},{12,2},{14,0},{1,15},{3,13... | collective-permute-start | bytes 196616 | tf_op jit(solution)/shard_map/ppermute | solution.py:35
  252.5 38.7 %copy-start.13 = (f32[32,64]{1,0:T(8,128)S(1)}, f32[32,64]{1,0:T(8,128)}, u32[]{:S(2)}) copy-start(f32[32,64]{1,0:T(8,128)} %get-tuple-element.67) | copy-start | bytes 24580
  252.5 38.7 %copy-start.14 = (f32[32,64]{1,0:T(8,128)S(1)}, f32[32,64]{1,0:T(8,128)}, u32[]{:S(2)}) copy-start(f32[32,64]{1,0:T(8,128)} %get-tuple-element.68) | copy-start | bytes 24580
  279.9 7.4 %collective-permute-start.22 = (bf16[4,8192]{1,0:T(4,128)(2,1)S(1)}, bf16[4,8192]{1,0:T(4,128)(2,1)S(1)}, u32[]{:S(2)}, u32[]{:S(2)}) collective-permute-start(bf16[4,8192]{1,0:T(4,128)(2,1)S(1)} %get-tuple-element.41.refs_0_), channel_id=1, source_target_pairs={{0,2},{2,0},{4,6},{6,4},{8,10},{10,8},{12,14},{14,12},{1,3},{3,1},... | collective-permute-start | bytes 196616 | tf_op jit(solution)/shard_map/ppermute | solution.py:35
  281.5 7.3 %collective-permute-start.23 = (bf16[4,8192]{1,0:T(4,128)(2,1)S(1)}, bf16[4,8192]{1,0:T(4,128)(2,1)S(1)}, u32[]{:S(2)}, u32[]{:S(2)}) collective-permute-start(bf16[4,8192]{1,0:T(4,128)(2,1)S(1)} %get-tuple-element.41.refs_0_), channel_id=1, source_target_pairs={{0,4},{2,6},{4,0},{6,2},{8,12},{10,14},{12,8},{14,10},{1,5},{3,7},... | collective-permute-start | bytes 196616 | tf_op jit(solution)/shard_map/ppermute | solution.py:35
  281.5 9.7 %collective-permute-start.24 = (bf16[4,8192]{1,0:T(4,128)(2,1)S(1)}, bf16[4,8192]{1,0:T(4,128)(2,1)S(1)}, u32[]{:S(2)}, u32[]{:S(2)}) collective-permute-start(bf16[4,8192]{1,0:T(4,128)(2,1)S(1)} %get-tuple-element.41.refs_0_), channel_id=1, source_target_pairs={{0,6},{2,4},{4,2},{6,0},{8,14},{10,12},{12,10},{14,8},{1,7},{3,5},... | collective-permute-start | bytes 196616 | tf_op jit(solution)/shard_map/ppermute | solution.py:35
  283.5 9.2 %collective-permute-start.25 = (bf16[4,8192]{1,0:T(4,128)(2,1)S(1)}, bf16[4,8192]{1,0:T(4,128)(2,1)S(1)}, u32[]{:S(2)}, u32[]{:S(2)}) collective-permute-start(bf16[4,8192]{1,0:T(4,128)(2,1)S(1)} %get-tuple-element.41.refs_0_), channel_id=1, source_target_pairs={{0,8},{2,10},{4,12},{6,14},{8,0},{10,2},{12,4},{14,6},{1,9},{3,11}... | collective-permute-start | bytes 196616 | tf_op jit(solution)/shard_map/ppermute | solution.py:35
  284.6 10.3 %collective-permute-start.26 = (bf16[4,8192]{1,0:T(4,128)(2,1)S(1)}, bf16[4,8192]{1,0:T(4,128)(2,1)S(1)}, u32[]{:S(2)}, u32[]{:S(2)}) collective-permute-start(bf16[4,8192]{1,0:T(4,128)(2,1)S(1)} %get-tuple-element.41.refs_0_), channel_id=1, source_target_pairs={{0,10},{2,8},{4,14},{6,12},{8,2},{10,0},{12,6},{14,4},{1,11},{3,9}... | collective-permute-start | bytes 196616 | tf_op jit(solution)/shard_map/ppermute | solution.py:35
  287.4 7.5 %collective-permute-start.27 = (bf16[4,8192]{1,0:T(4,128)(2,1)S(1)}, bf16[4,8192]{1,0:T(4,128)(2,1)S(1)}, u32[]{:S(2)}, u32[]{:S(2)}) collective-permute-start(bf16[4,8192]{1,0:T(4,128)(2,1)S(1)} %get-tuple-element.41.refs_0_), channel_id=1, source_target_pairs={{0,12},{2,14},{4,8},{6,10},{8,4},{10,6},{12,0},{14,2},{1,13},{3,15... | collective-permute-start | bytes 196616 | tf_op jit(solution)/shard_map/ppermute | solution.py:35
  288.8 7.1 %collective-permute-start.28 = (bf16[4,8192]{1,0:T(4,128)(2,1)S(1)}, bf16[4,8192]{1,0:T(4,128)(2,1)S(1)}, u32[]{:S(2)}, u32[]{:S(2)}) collective-permute-start(bf16[4,8192]{1,0:T(4,128)(2,1)S(1)} %get-tuple-element.41.refs_0_), channel_id=1, source_target_pairs={{0,14},{2,12},{4,10},{6,8},{8,6},{10,4},{12,2},{14,0},{1,15},{3,13... | collective-permute-start | bytes 196616 | tf_op jit(solution)/shard_map/ppermute | solution.py:35
  321.6 7.4 %collective-permute-start.29 = (bf16[4,8192]{1,0:T(4,128)(2,1)S(1)}, bf16[4,8192]{1,0:T(4,128)(2,1)S(1)}, u32[]{:S(2)}, u32[]{:S(2)}) collective-permute-start(bf16[4,8192]{1,0:T(4,128)(2,1)S(1)} %get-tuple-element.45.refs_0_), channel_id=1, source_target_pairs={{0,2},{2,0},{4,6},{6,4},{8,10},{10,8},{12,14},{14,12},{1,3},{3,1},... | collective-permute-start | bytes 196616 | tf_op jit(solution)/shard_map/ppermute | solution.py:35
  323.1 7.4 %collective-permute-start.30 = (bf16[4,8192]{1,0:T(4,128)(2,1)S(1)}, bf16[4,8192]{1,0:T(4,128)(2,1)S(1)}, u32[]{:S(2)}, u32[]{:S(2)}) collective-permute-start(bf16[4,8192]{1,0:T(4,128)(2,1)S(1)} %get-tuple-element.45.refs_0_), channel_id=1, source_target_pairs={{0,4},{2,6},{4,0},{6,2},{8,12},{10,14},{12,8},{14,10},{1,5},{3,7},... | collective-permute-start | bytes 196616 | tf_op jit(solution)/shard_map/ppermute | solution.py:35
  323.1 9.8 %collective-permute-start.31 = (bf16[4,8192]{1,0:T(4,128)(2,1)S(1)}, bf16[4,8192]{1,0:T(4,128)(2,1)S(1)}, u32[]{:S(2)}, u32[]{:S(2)}) collective-permute-start(bf16[4,8192]{1,0:T(4,128)(2,1)S(1)} %get-tuple-element.45.refs_0_), channel_id=1, source_target_pairs={{0,6},{2,4},{4,2},{6,0},{8,14},{10,12},{12,10},{14,8},{1,7},{3,5},... | collective-permute-start | bytes 196616 | tf_op jit(solution)/shard_map/ppermute | solution.py:35
  325.2 8.5 %collective-permute-start.32 = (bf16[4,8192]{1,0:T(4,128)(2,1)S(1)}, bf16[4,8192]{1,0:T(4,128)(2,1)S(1)}, u32[]{:S(2)}, u32[]{:S(2)}) collective-permute-start(bf16[4,8192]{1,0:T(4,128)(2,1)S(1)} %get-tuple-element.45.refs_0_), channel_id=1, source_target_pairs={{0,8},{2,10},{4,12},{6,14},{8,0},{10,2},{12,4},{14,6},{1,9},{3,11}... | collective-permute-start | bytes 196616 | tf_op jit(solution)/shard_map/ppermute | solution.py:35
  326.3 9.3 %collective-permute-start.33 = (bf16[4,8192]{1,0:T(4,128)(2,1)S(1)}, bf16[4,8192]{1,0:T(4,128)(2,1)S(1)}, u32[]{:S(2)}, u32[]{:S(2)}) collective-permute-start(bf16[4,8192]{1,0:T(4,128)(2,1)S(1)} %get-tuple-element.45.refs_0_), channel_id=1, source_target_pairs={{0,10},{2,8},{4,14},{6,12},{8,2},{10,0},{12,6},{14,4},{1,11},{3,9}... | collective-permute-start | bytes 196616 | tf_op jit(solution)/shard_map/ppermute | solution.py:35
  329.0 6.6 %collective-permute-start.34 = (bf16[4,8192]{1,0:T(4,128)(2,1)S(1)}, bf16[4,8192]{1,0:T(4,128)(2,1)S(1)}, u32[]{:S(2)}, u32[]{:S(2)}) collective-permute-start(bf16[4,8192]{1,0:T(4,128)(2,1)S(1)} %get-tuple-element.45.refs_0_), channel_id=1, source_target_pairs={{0,12},{2,14},{4,8},{6,10},{8,4},{10,6},{12,0},{14,2},{1,13},{3,15... | collective-permute-start | bytes 196616 | tf_op jit(solution)/shard_map/ppermute | solution.py:35
  330.5 7.1 %collective-permute-start.35 = (bf16[4,8192]{1,0:T(4,128)(2,1)S(1)}, bf16[4,8192]{1,0:T(4,128)(2,1)S(1)}, u32[]{:S(2)}, u32[]{:S(2)}) collective-permute-start(bf16[4,8192]{1,0:T(4,128)(2,1)S(1)} %get-tuple-element.45.refs_0_), channel_id=1, source_target_pairs={{0,14},{2,12},{4,10},{6,8},{8,6},{10,4},{12,2},{14,0},{1,15},{3,13... | collective-permute-start | bytes 196616 | tf_op jit(solution)/shard_map/ppermute | solution.py:35
  (14 other events, 44.1 us)

commit v2 on v1

v2 whole, which is shorter than its diff:
```python
import functools

import jax
import jax.numpy as jnp
from jax import lax
from jax.experimental import pallas as pl
from jax.experimental.pallas import tpu as pltpu
from jax.sharding import PartitionSpec as P

HD = 128
PLEN = 128
STEPS = 4
EPS = 1e-05
ROPE_BASE = 500000.0
LANES = 8
CHUNKS = 8
VMEM_LIMIT = 16 * 1024 * 1024


def ring_order(count):
    if count == 8:
        return [0, 2, 4, 6, 7, 5, 3, 1]
    return list(range(count))


def ring_shift(value, steps):
    count = lax.axis_size("tensor")
    order = ring_order(count)
    pairs = [(order[i], order[(i + steps) % count]) for i in range(count)]
    return lax.ppermute(value, "tensor", pairs)


def swap_xor(value, mask):
    count = lax.axis_size("tensor")
    return lax.ppermute(value, "tensor", [(s, s ^ mask) for s in range(count)])


def rope_tables(positions):
    half_dim = HD // 2
    freqs = ROPE_BASE ** (-(jnp.arange(half_dim, dtype=jnp.float32) * 2.0 / HD))
    angles = positions.astype(jnp.float32)[:, None] * freqs[None, :]
    cosine = jnp.cos(angles)
    sine = jnp.sin(angles)
    return (
        jnp.concatenate([cosine, cosine], axis=1),
        jnp.concatenate([-sine, sine], axis=1),
    )


def whole():
    return pl.BlockSpec(memory_space=pltpu.VMEM)


def normed_rows(values, gain):
    square = jnp.mean(values * values, axis=-1, keepdims=True)
    return values * lax.rsqrt(square + EPS) * gain


def normalize_kernel(rows_ref, gain_ref, out_ref):
    gain = gain_ref[...].astype(jnp.float32)
    out_ref[...] = normed_rows(rows_ref[...].astype(jnp.float32), gain).astype(jnp.bfloat16)


def normalize(rows, gain):
    return pl.pallas_call(
        normalize_kernel,
        out_shape=jax.ShapeDtypeStruct(rows.shape, jnp.bfloat16),
        in_specs=[whole()] * 2,
        out_specs=whole(),
        compiler_params=pltpu.CompilerParams(vmem_limit_bytes=VMEM_LIMIT),
        name="normalize",
    )(rows, gain)


def fetch_kernel(*refs):
    count = len(refs) // 2
    sems = refs[-1]
    copies = [pltpu.make_async_copy(refs[i], refs[count + i], sems.at[i]) for i in range(count)]
    for copy in copies:
        copy.start()
    for copy in copies:
        copy.wait()


def fetch(*arrays):
    return pl.pallas_call(
        fetch_kernel,
        out_shape=tuple(pltpu.VMEM(a.shape, a.dtype) for a in arrays),
        in_specs=[pl.BlockSpec(memory_space=pl.ANY)] * len(arrays),
        out_specs=tuple(whole() for _ in arrays),
        scratch_shapes=[pltpu.SemaphoreType.DMA((len(arrays),))],
        compiler_params=pltpu.CompilerParams(vmem_limit_bytes=VMEM_LIMIT),
        name="fetch",
    )(*arrays)


def parcels_kernel(heads, table_ref, pool_ref, out_ref, held, load_sem, store_sem):
    pages = held.shape[0]
    width = out_ref.shape[-1]

    def load(index):
        return pltpu.make_async_copy(pool_ref.at[table_ref[index]], held.at[index], load_sem.at[index])

    for index in range(pages):
        load(index).start()
    for index in range(pages):
        load(index).wait()
    stores = []
    for target, head in enumerate(heads):
        copy = pltpu.make_async_copy(
            held.at[:, :, pl.ds(head * width, width)], out_ref.at[target], store_sem.at[target]
        )
        copy.start()
        stores.append(copy)
    for copy in stores:
        copy.wait()


def make_parcels(table, pool, heads, width):
    pages, rows, _ = pool.shape
    return pl.pallas_call(
        functools.partial(parcels_kernel, heads),
        out_shape=jax.ShapeDtypeStruct((len(heads), pages, rows, width), jnp.bfloat16),
        in_specs=[pl.BlockSpec(memory_space=pltpu.SMEM), pl.BlockSpec(memory_space=pl.ANY)],
        out_specs=pl.BlockSpec(memory_space=pl.ANY),
        scratch_shapes=[
            pltpu.VMEM(pool.shape, jnp.bfloat16),
            pltpu.SemaphoreType.DMA((pages,)),
            pltpu.SemaphoreType.DMA((len(heads),)),
        ],
        compiler_params=pltpu.CompilerParams(vmem_limit_bytes=VMEM_LIMIT),
        name="parcels",
    )(table, pool)


def assemble_kernel(rows, request_ref, offset_ref, arrived_ref, cache_ref, out_ref, sems):
    fetched = pltpu.make_async_copy(cache_ref, out_ref, sems.at[0])
    fetched.start()
    fetched.wait()
    copies = []
    for piece in range(arrived_ref.shape[0] // rows):
        offset = pl.multiple_of(offset_ref[piece], rows)
        copy = pltpu.make_async_copy(
            arrived_ref.at[pl.ds(piece * rows, rows), :],
            out_ref.at[request_ref[piece], pl.ds(offset, rows), :],
            sems.at[piece + 1],
        )
        copy.start()
        copies.append(copy)
    for copy in copies:
        copy.wait()


def assemble(requests, offsets, arrived, cache, rows):
    smem = pl.BlockSpec(memory_space=pltpu.SMEM)
    anywhere = pl.BlockSpec(memory_space=pl.ANY)
    return pl.pallas_call(
        functools.partial(assemble_kernel, rows),
        out_shape=pltpu.VMEM(cache.shape, cache.dtype),
        in_specs=[smem, smem, anywhere, anywhere],
        out_specs=whole(),
        scratch_shapes=[pltpu.SemaphoreType.DMA((arrived.shape[0] // rows + 1,))],
        compiler_params=pltpu.CompilerParams(vmem_limit_bytes=VMEM_LIMIT),
        name="assemble",
    )(requests, offsets, arrived, cache)


def turn(values, cosine, sine):
    return values * cosine + pltpu.roll(values, HD // 2, 1) * sine


def step_kernel(blocks, iteration, *refs):
    x_refs = refs[:blocks]
    order_ref, lens_ref, wq, wkv, wo, cache, cos_ref, sin_ref = refs[blocks : blocks + 8]
    new_refs = refs[blocks + 8 : blocks + 8 + iteration]
    out_ref, fresh_ref, x_rows, q_s, score_s, mix_s, new_s = refs[blocks + 8 + iteration :]
    width, q_cols = wq.shape
    count, span = cache.shape[:2]
    each = count // out_ref.shape[0]
    heads = q_cols // HD
    depth = width // CHUNKS

    if blocks > 1:
        for k in range(blocks):
            x_rows[k * each : (k + 1) * each, :] = x_refs[k][...].astype(jnp.float32)
        order = order_ref[...]

    query = jnp.zeros((count, q_cols), jnp.float32)
    keyvalue = jnp.zeros((count, 2 * HD), jnp.float32)
    for c in range(CHUNKS):
        part = slice(c * depth, (c + 1) * depth)
        if blocks > 1:
            x = jnp.dot(
                order, x_rows[:, part].astype(jnp.bfloat16), preferred_element_type=jnp.float32
            ).astype(jnp.bfloat16)
        else:
            x = x_refs[0][:, part]
        query += jnp.dot(x, wq[part, :], preferred_element_type=jnp.float32)
        keyvalue += jnp.dot(x, wkv[part, :], preferred_element_type=jnp.float32)

    cosine = cos_ref[iteration]
    sine = sin_ref[iteration]
    key = turn(keyvalue[:, :HD], cosine, sine).astype(jnp.bfloat16)
    value = keyvalue[:, HD:].astype(jnp.bfloat16)
    fresh_ref[:, :HD] = key
    fresh_ref[:, HD:] = value
    news = [(ref[:, :HD], ref[:, HD:]) for ref in new_refs] + [(key, value)]
    for j in range(LANES):
        lane = pl.ds(j, count, LANES)
        if j < heads:
            turned = turn(query[:, j * HD : (j + 1) * HD], cosine, sine).astype(jnp.bfloat16)
            q_s[lane, :] = turned.astype(jnp.float32)
        else:
            q_s[lane, :] = jnp.zeros((count, HD), jnp.float32)
        for t, pair in enumerate(news):
            for half in range(2):
                new_s[t, half, lane, :] = pair[half].astype(jnp.float32)

    scale = HD**-0.5
    column = lax.broadcasted_iota(jnp.int32, (LANES, span), 1)
    for r in range(count):
        rows = slice(r * LANES, (r + 1) * LANES)
        found = lax.dot_general(
            q_s[rows, :].astype(jnp.bfloat16),
            cache[r, :, :HD],
            (((1,), (1,)), ((), ())),
            preferred_element_type=jnp.float32,
        )
        score_s[rows, :] = jnp.where(column < lens_ref[r], found * scale, -1e30)

    scores = score_s[...]
    queries = q_s[...]
    fresh_scores = [
        jnp.sum(queries * new_s[t, 0], axis=-1, keepdims=True) * scale for t in range(iteration + 1)
    ]
    top = jnp.max(scores, axis=-1, keepdims=True)
    for s in fresh_scores:
        top = jnp.maximum(top, s)
    weights = jnp.exp(scores - top)
    fresh_weights = [jnp.exp(s - top) for s in fresh_scores]
    total = jnp.sum(weights, axis=-1, keepdims=True)
    for w in fresh_weights:
        total = total + w
    score_s[...] = weights / total
    row = lax.broadcasted_iota(jnp.int32, (span, HD), 0)
    for r in range(count):
        rows = slice(r * LANES, (r + 1) * LANES)
        mix_s[rows, :] = jnp.dot(
            score_s[rows, :].astype(jnp.bfloat16),
            jnp.where(row < lens_ref[r], cache[r, :, HD:], jnp.zeros((), jnp.bfloat16)),
            preferred_element_type=jnp.float32,
        )
    mixed = mix_s[...]
    for t in range(iteration + 1):
        weight = (fresh_weights[t] / total).astype(jnp.bfloat16).astype(jnp.float32)
        mixed = mixed + weight * new_s[t, 1]
    mix_s[...] = mixed
    columns = jnp.concatenate(
        [mix_s[pl.ds(j, count, LANES), :].astype(jnp.bfloat16) for j in range(heads)], axis=1
    )
    for c in range(CHUNKS):
        part = slice(c * depth, (c + 1) * depth)
        product = jnp.dot(columns, wo[:, part], preferred_element_type=jnp.float32)
        for d in range(count // each):
            out_ref[d, :, part] = product[d * each : (d + 1) * each, :].astype(jnp.bfloat16)


def step(x_blocks, order, lengths, wq, wkv, wo, cache, cosine, sine, earlier, owners):
    width, q_cols = wq.shape
    count, span = cache.shape[:2]
    each = count // owners
    iteration = len(earlier)
    blocks = len(x_blocks)
    smem = pl.BlockSpec(memory_space=pltpu.SMEM)
    return pl.pallas_call(
        functools.partial(step_kernel, blocks, iteration),
        out_shape=(
            jax.ShapeDtypeStruct((owners, each, width), jnp.bfloat16),
            jax.ShapeDtypeStruct((count, 2 * HD), jnp.bfloat16),
        ),
        in_specs=[whole()] * (blocks + 1) + [smem] + [whole()] * (6 + iteration),
        out_specs=(whole(), whole()),
        scratch_shapes=[
            pltpu.VMEM((count, width), jnp.float32),
            pltpu.VMEM((count * LANES, HD), jnp.float32),
            pltpu.VMEM((count * LANES, span), jnp.float32),
            pltpu.VMEM((count * LANES, HD), jnp.float32),
            pltpu.VMEM((iteration + 1, 2, count * LANES, HD), jnp.float32),
        ],
        compiler_params=pltpu.CompilerParams(vmem_limit_bytes=VMEM_LIMIT),
        cost_estimate=pl.CostEstimate(
            flops=2 * count * width * (2 * q_cols + 2 * HD),
            bytes_accessed=2 * (2 * wq.size + wkv.size + cache.size),
            transcendentals=count * LANES * span,
        ),
        name="decode_step",
    )(*x_blocks, order, lengths, wq, wkv, wo, cache, cosine, sine, *earlier)


def settle_kernel(parts_ref, state_ref, gain_ref, next_ref, normed_ref):
    total = parts_ref[0].astype(jnp.float32)
    for d in range(1, parts_ref.shape[0]):
        total = total + parts_ref[d].astype(jnp.float32)
    state = (state_ref[...].astype(jnp.float32) + total).astype(jnp.bfloat16)
    next_ref[...] = state
    gain = gain_ref[...].astype(jnp.float32)
    normed_ref[...] = normed_rows(state.astype(jnp.float32), gain).astype(jnp.bfloat16)


def settle(parts, state, gain):
    shape = jax.ShapeDtypeStruct(state.shape, jnp.bfloat16)
    return pl.pallas_call(
        settle_kernel,
        out_shape=(shape, shape),
        in_specs=[whole()] * 3,
        out_specs=(whole(), whole()),
        compiler_params=pltpu.CompilerParams(vmem_limit_bytes=VMEM_LIMIT),
        name="settle",
    )(parts, state, gain)


def on_device(
    prompt_states,
    decode_states,
    norm_gain,
    w_query,
    w_keyvalue,
    w_output,
    cache_pages,
    page_table,
    cache_len,
    dest_rank,
    dest_page,
):
    rank = lax.axis_index("tensor")
    section = lax.axis_index("section")
    count = lax.axis_size("tensor")
    pool = cache_pages[0]
    page_size, kv_width = pool.shape[1:]
    own_table = page_table[0]
    lengths = cache_len[0]
    each, width = decode_states.shape[1:]
    tokens = prompt_states.shape[1]
    q_cols = w_query.shape[1]
    kv_heads = kv_width // (2 * HD)
    shared = count // kv_heads if count > kv_heads else 1
    gain = norm_gain[None, :]

    if w_keyvalue.shape[1] < 2 * HD:
        other = swap_xor(w_keyvalue, 1)
        is_key = rank % 2 == 0
        w_kv = jnp.concatenate(
            [jnp.where(is_key, w_keyvalue, other), jnp.where(is_key, other, w_keyvalue)], axis=1
        )
    else:
        w_kv = w_keyvalue

    w_q, w_kv, w_o = fetch(w_query, w_kv, w_output)
    first_pages = lax.all_gather(own_table[:, 0], "tensor", axis=0)
    states = lax.all_gather(normalize(decode_states[0], gain), "tensor", axis=0, tiled=True)

    heads = tuple(target // shared for target in range(count))
    parcels = make_parcels(own_table.reshape(-1), pool, heads, 2 * HD)
    span = own_table.shape[1] * page_size
    cache = lax.all_to_all(
        parcels.reshape(count, each * span, 2 * HD), "tensor", split_axis=0, concat_axis=0, tiled=True
    ).reshape(count * each, span, 2 * HD)

    half = tokens // 2
    ready = normalize(prompt_states[0], gain)
    pieces = [ready[:half], ready[half:]]
    order = ring_order(count)
    place = jnp.array([order.index(r) for r in range(count)], jnp.int32)[rank]
    ring = jnp.array(order, jnp.int32)
    arrivals = [(0, 0, pieces[0]), (0, 1, pieces[1])]
    going = [[piece, piece] for piece in pieces]
    for hop in range(1, count // 2 + 1):
        for piece in range(2):
            for way in range(2):
                if hop == count // 2 and piece != way:
                    continue
                sign = 1 if way == 0 else -1
                going[piece][way] = ring_shift(going[piece][way], sign)
                arrivals.append((-sign * hop, piece, going[piece][way]))
    products = [
        jnp.dot(rows, w_kv, preferred_element_type=jnp.float32) for _, _, rows in arrivals
    ]
    behind = jnp.array([steps for steps, _, _ in arrivals], jnp.int32)
    halves = jnp.array([piece for _, piece, _ in arrivals], jnp.int32)
    starts = ring[(place + behind) % count] * tokens + halves * half
    row_index = (starts[:, None] + jnp.arange(half, dtype=jnp.int32)[None, :]).reshape(-1)
    cosine, sine = rope_tables(row_index % PLEN)
    values = jnp.concatenate(products, axis=0)
    keys = values[:, :HD]
    keys = keys * cosine + jnp.roll(keys, HD // 2, axis=1) * sine
    prompt_kv = jnp.concatenate([keys, values[:, HD:]], axis=1).astype(jnp.bfloat16)
    sections = lax.axis_size("section")
    arrived = lax.ppermute(prompt_kv, "section", [(s, (s + 1) % sections) for s in range(sections)])

    anchor = (section + 1) % sections
    targets = lax.dynamic_index_in_dim(dest_rank, anchor, 0, keepdims=False)
    landing = lax.dynamic_index_in_dim(dest_page, anchor, 0, keepdims=False)[:, 0]
    numbers = jnp.arange(count * each, dtype=jnp.int32)
    here = (numbers[None, :] // each == targets[:, None]) & (
        first_pages.reshape(1, -1) == landing[:, None]
    )
    receivers = jnp.sum(jnp.where(here, numbers[None, :], 0), axis=1)
    cache = assemble(receivers[starts // PLEN], starts % PLEN, arrived, cache, half)

    times = lengths[None, :] + jnp.arange(STEPS, dtype=jnp.int32)[:, None]
    cosine, sine = rope_tables(times.reshape(-1))
    cosine = cosine.reshape(STEPS, count * each, HD)
    sine = sine.reshape(STEPS, count * each, HD)
    rows_of = ((rank ^ (numbers // each)) * each + numbers % each)[None, :]
    chosen = (numbers[:, None] == rows_of).astype(jnp.bfloat16)
    state = decode_states[0]
    blocks = [states]
    outputs = []
    earlier = []
    for iteration in range(STEPS):
        parts, fresh = step(
            blocks, chosen, lengths, w_q, w_kv, w_o, cache, cosine, sine, earlier, count
        )
        earlier.append(fresh)
        parts = lax.all_to_all(parts, "tensor", split_axis=0, concat_axis=0, tiled=True)
        state, normed = settle(parts, state, gain)
        outputs.append(state)
        if iteration + 1 < STEPS:
            blocks = [normed] + [swap_xor(normed, bits) for bits in range(1, count)]
    return jnp.stack(outputs)[:, None]


def solution(mesh):
    in_specs = (
        P(("groups", "section"), "tensor", None),
        P(("groups", "section"), "tensor", None),
        P(),
        P(None, "tensor"),
        P(None, "tensor"),
        P("tensor", None),
        P(("groups", "section"), "tensor", None, None),
        P(("groups", "section"), "tensor", None),
        P(("groups", "section"), None),
        P("groups", None),
        P("groups", None, None),
    )
    out_specs = P(None, ("groups", "section"), "tensor", None)
    return jax.shard_map(
        on_device, mesh=mesh, in_specs=in_specs, out_specs=out_specs, check_vma=False
    )
```

time: 365 us -> 385 us (1.055)
  blocking collectives: 47.2 us -> 187 us
  waiting for transfers between devices: 102 us -> 47.9 us
  starting transfers between devices: 101 us -> 55.3 us
  between operations: 11 us -> 1.11 us
  Pallas kernels: 51.6 us -> 42.8 us
  local copies, waits for them, and re-layouts: 26.2 us -> 33 us
    unnamed x0 -> x1, blocking collectives: none -> 91.8 us
    ppermute x14, starting transfers between devices: 57.2 us -> 15.2 us  [ring_shift(): return lax.ppermute(value, 'tensor', pairs)]
    ppermute x14, waiting for transfers between devices: 72.6 us -> 33.2 us  [ring_shift(): return lax.ppermute(value, 'tensor', pairs)]
    all_gather x0 -> x1, blocking collectives: none -> 31.8 us  [on_device(): lax.all_gather(normalize(decode_states[0], gain), 'tensor', axis=0, tiled...]
    unnamed x48 -> x53, local copies, waits for them, and re-layouts: 9.4 us -> 28.7 us
    all_to_all x3 -> x4, blocking collectives: 47.2 us -> 62.9 us  [on_device(): lax.all_to_all(parts, 'tensor', split_axis=0, concat_axis=0, tiled=True)]
    all_to_all x1 -> x0, waiting for transfers between devices: 15 us -> none  [on_device(): lax.all_to_all(parts, 'tensor', split_axis=0, concat_axis=0, tiled=True)]
    pallas_call x6 -> x8, Pallas kernels: 42.2 us -> 33.5 us  [the longest x4 24.8 us: step(): pl.pallas_call(functools.partial(step_kernel, blocks, iteration), out_sha...]
  transfers between devices with their start and end apart: 38 -> 37, of which waited for: 13 -> 16; matrix products, arithmetic and copies ran while one was open for 11% -> 5% of each run, Pallas kernels for 2% -> 3%
where the time goes in v2:
time: 385 us; the launch traced here: 384 us
  blocking collectives  187 us (49%)
  starting transfers between devices  55.3 us (14%)
  waiting for transfers between devices  47.9 us (12%)
  Pallas kernels  42.8 us (11%)
  local copies, waits for them, and re-layouts  33 us (9%)
  matrix products  14.2 us (4%)
    unnamed x1, blocking collectives  91.8 us
    all_to_all x4, blocking collectives, on_device(): lax.all_to_all(parts, 'tensor', split_axis=0, concat_axis=0, tiled=True)  62.9 us
    ppermute x21, starting transfers between devices, swap_xor(): return lax.ppermute(value, 'tensor', [(s, s ^ mask) for s in range(count)])  33.6 us
    ppermute x14, waiting for transfers between devices, ring_shift(): return lax.ppermute(value, 'tensor', pairs)  33.2 us
    all_gather x1, blocking collectives, on_device(): lax.all_gather(normalize(decode_states[0], gain), 'tensor', axis=0, tiled...  31.8 us
    unnamed x53, local copies, waits for them, and re-layouts  28.7 us
    pallas_call x4, Pallas kernels, step(): pl.pallas_call(functools.partial(step_kernel, blocks, iteration), out_sha...  24.8 us
    ppermute x14, starting transfers between devices, ring_shift(): return lax.ppermute(value, 'tensor', pairs)  15.2 us
  transfers between devices with their start and end apart: 37, of which 16 were waited for; matrix products, arithmetic and copies ran while one was open for 5% of the time, Pallas kernels for 3%

profile of v2, /device:TPU:0, one launch (start us, length us, event | category | flops | bytes accessed | tf_op | source)
XLA Modules:
  0.0 384.4 jit_solution(16802779446094133642)
XLA Ops:
  3.7 3.0 collective-permute-start
  6.7 2.0 collective-permute-start.2
  8.8 2.2 copy-done.12
  11.0 7.5 %parcels.1 = bf16[8,64,16,256]{3,2,1,0:T(8,128)(2,1)S(1)} custom-call(s32[64]{0:T(128)S(1)} %reshape_squeeze.3.table_ref, bf16[64,16,2048]{2,1,0:T(8,128)(2,1)S(1)} %bitcast.55), custom_call_target="tpu_custom_call" | custom-call | tf_op jit(solution)/shard_map/parcels/pallas_call | solution.py:121
  18.6 2.0 copy-done.9
  20.6 6.4 %all-to-all-start = ((bf16[8,1024,256]{2,1,0:T(8,128)(2,1)}), bf16[8,1024,256]{2,1,0:T(8,128)(2,1)}, u32[]{:S(2)}, u32[]{:S(2)}) async-start(bf16[8,1024,256]{2,1,0:T(8,128)(2,1)} %bitcast.54), calls=%async_computation | async-start | bytes 8388608 | tf_op jit(solution)/shard_map/all_to_all | solution.py:365
  31.0 91.8 %all-reduce = s32[32]{0:T(128)S(1)} all-reduce(s32[32]{0:T(128)S(1)} %dynamic-update-slice), channel_id=2, replica_groups=mesh['groups'=2,'tensor'=8,'section'=2] {'tensor'}, use_global_device_ids=true, to_apply=%add | all-reduce | flops 32 | bytes 256
  123.3 3.4 copy-done.10
  126.6 2.2 copy-done.11
  128.8 4.2 %fetch.1 = (bf16[8192,512]{1,0:T(8,128)(2,1)S(1)}, bf16[8192,256]{1,0:T(8,128)(2,1)S(1)}, bf16[512,8192]{1,0:T(8,128)(2,1)S(1)}) custom-call(bf16[8192,512]{1,0:T(8,128)(2,1)S(1)} %copy-done.10, bf16[8192,256]{1,0:T(8,128)(2,1)S(1)} %copy-done.11, bf16[512,8192]{1,0:T(8,128)(2,1)} %refs_2_.1), custom_call_target="tpu_custom_call" | custom-call | tf_op jit(solution)/shard_map/fetch/pallas_call | solution.py:86
  133.1 3.3 copy-done.4
  136.4 3.3 copy-done.7
  141.8 31.8 %all-gather.1 = bf16[8,4,8192]{2,1,0:T(4,128)(2,1)S(1)} all-gather(bf16[1,4,8192]{2,1,0:T(4,128)(2,1)S(1)} %bitcast.59), channel_id=1, replica_groups=mesh['groups'=2,'tensor'=8,'section'=2] {'tensor'}, dimensions={0}, use_global_device_ids=true | all-gather | bytes 589824 | tf_op jit(solution)/shard_map/all_gather | solution.py:360
  174.5 2.0 collective-permute-start.5
  176.6 2.0 collective-permute-start.7
  178.6 1.9 convolution_dynamic-update-slice_fusion.13
  182.9 6.7 %collective-permute-done.4 = bf16[32,8192]{1,0:T(8,128)(2,1)S(1)} collective-permute-done((bf16[32,8192]{1,0:T(8,128)(2,1)}, bf16[32,8192]{1,0:T(8,128)(2,1)S(1)}, u32[]{:S(2)}, u32[]{:S(2)}) %collective-permute-start.4) | collective-permute-done | bytes 524320 | tf_op jit(solution)/shard_map/ppermute | solution.py:30
  189.6 2.0 collective-permute-start.9
  191.6 9.2 %collective-permute-done.6 = bf16[32,8192]{1,0:T(8,128)(2,1)S(1)} collective-permute-done((bf16[32,8192]{1,0:T(8,128)(2,1)S(1)}, bf16[32,8192]{1,0:T(8,128)(2,1)S(1)}, u32[]{:S(2)}, u32[]{:S(2)}) %collective-permute-start.6) | collective-permute-done | bytes 524320 | tf_op jit(solution)/shard_map/ppermute | solution.py:30
  200.8 2.0 collective-permute-start.11
  206.1 5.9 %collective-permute-done.8 = bf16[32,8192]{1,0:T(8,128)(2,1)S(1)} collective-permute-done((bf16[32,8192]{1,0:T(8,128)(2,1)S(1)}, bf16[32,8192]{1,0:T(8,128)(2,1)S(1)}, u32[]{:S(2)}, u32[]{:S(2)}) %collective-permute-start.8) | collective-permute-done | bytes 524320 | tf_op jit(solution)/shard_map/ppermute | solution.py:30
  212.0 8.3 %collective-permute-done.11 = bf16[32,8192]{1,0:T(8,128)(2,1)S(1)} collective-permute-done((bf16[32,8192]{1,0:T(8,128)(2,1)S(1)}, bf16[32,8192]{1,0:T(8,128)(2,1)S(1)}, u32[]{:S(2)}, u32[]{:S(2)}) %collective-permute-start.11) | collective-permute-done | bytes 524320 | tf_op jit(solution)/shard_map/ppermute | solution.py:30
  220.4 2.0 collective-permute-start.13
  227.7 1.8 collective-permute-done.13
  232.5 3.6 assemble.1.refs_6_.refs_13_
  236.1 3.4 copy-done.5
  239.4 3.4 copy-done.8
  242.8 6.2 %decode_step.4 = (bf16[8,4,8192]{2,1,0:T(4,128)(2,1)S(1)}, bf16[32,256]{1,0:T(8,128)(2,1)S(1)}) custom-call(bf16[32,8192]{1,0:T(8,128)(2,1)S(1)} %reshape.174.refs_0_, bf16[32,32]{1,0:T(8,128)(2,1)S(1)} %fusion.4.refs_1_.refs_8_, s32[32]{0:T(128)S(1)} %bitcast.65, bf16[8192,512]{1,0:T(8,128)(2,1)S(1)} %copy-done.5, bf16[8192,256]{1,0:T(8,128)(2,1)S(1)} %copy-done.3, ...), custom_call_target="tpu_custom_call" | custom-call | flops 671088640 | bytes 25165824 | tf_op jit(solution)/shard_map/decode_step/pallas_call | solution.py:275
  249.0 18.5 %all_to_all.25.parts_ref = bf16[8,4,8192]{2,1,0:T(4,128)(2,1)S(1)} all-to-all(bf16[8,4,8192]{2,1,0:T(4,128)(2,1)S(1)} %get-tuple-element.25), channel_id=1, replica_groups=mesh['groups'=2,'tensor'=8,'section'=2] {'tensor'}, dimensions={0} | all-to-all | bytes 1048576 | tf_op jit(solution)/shard_map/all_to_all | solution.py:425
  269.3 2.0 collective-permute-start.17
  272.4 2.7 collective-permute-start.19
  276.6 2.4 collective-permute-start.21
  280.6 3.1 collective-permute-done.19.refs_5_
  283.7 3.4 copy-done.6
  287.1 6.2 %decode_step.5 = (bf16[8,4,8192]{2,1,0:T(4,128)(2,1)S(1)}, bf16[32,256]{1,0:T(8,128)(2,1)S(1)}) custom-call(bf16[4,8192]{1,0:T(4,128)(2,1)S(1)} %get-tuple-element.27.refs_0_, bf16[4,8192]{1,0:T(4,128)(2,1)S(1)} %collective-permute-done.15.refs_1_, bf16[4,8192]{1,0:T(4,128)(2,1)S(1)} %collective-permute-done.16.refs_2_, ...), custom_call_target="tpu_custom_call" | custom-call | flops 671088640 | bytes 25165824 | tf_op jit(solution)/shard_map/decode_step/pallas_call | solution.py:275
  293.3 15.9 %all_to_all.26.parts_ref = bf16[8,4,8192]{2,1,0:T(4,128)(2,1)S(1)} all-to-all(bf16[8,4,8192]{2,1,0:T(4,128)(2,1)S(1)} %get-tuple-element.29), channel_id=1, replica_groups=mesh['groups'=2,'tensor'=8,'section'=2] {'tensor'}, dimensions={0} | all-to-all | bytes 1048576 | tf_op jit(solution)/shard_map/all_to_all | solution.py:425
  311.0 2.0 collective-permute-start.24
  314.1 2.7 collective-permute-start.26
  318.3 2.4 collective-permute-start.28
  321.7 2.2 collective-permute-done.26.refs_5_
  325.4 6.2 %decode_step.6 = (bf16[8,4,8192]{2,1,0:T(4,128)(2,1)S(1)}, bf16[32,256]{1,0:T(8,128)(2,1)S(1)}) custom-call(bf16[4,8192]{1,0:T(4,128)(2,1)S(1)} %get-tuple-element.31.refs_0_, bf16[4,8192]{1,0:T(4,128)(2,1)S(1)} %collective-permute-done.22.refs_1_, bf16[4,8192]{1,0:T(4,128)(2,1)S(1)} %collective-permute-done.23.refs_2_, ...), custom_call_target="tpu_custom_call" | custom-call | flops 671088640 | bytes 25165824 | tf_op jit(solution)/shard_map/decode_step/pallas_call | solution.py:275
  331.6 14.8 %all_to_all.27.parts_ref = bf16[8,4,8192]{2,1,0:T(4,128)(2,1)S(1)} all-to-all(bf16[8,4,8192]{2,1,0:T(4,128)(2,1)S(1)} %get-tuple-element.33), channel_id=1, replica_groups=mesh['groups'=2,'tensor'=8,'section'=2] {'tensor'}, dimensions={0} | all-to-all | bytes 1048576 | tf_op jit(solution)/shard_map/all_to_all | solution.py:425
  348.2 2.1 collective-permute-start.31
  351.3 2.7 collective-permute-start.33
  355.5 2.4 collective-permute-start.35
  360.2 2.3 collective-permute-done.35.refs_7_
  362.5 6.3 %decode_step.7 = (bf16[8,4,8192]{2,1,0:T(4,128)(2,1)S(1)}, bf16[32,256]{1,0:T(8,128)(2,1)}) custom-call(bf16[4,8192]{1,0:T(4,128)(2,1)S(1)} %get-tuple-element.35.refs_0_, bf16[4,8192]{1,0:T(4,128)(2,1)S(1)} %collective-permute-done.29.refs_1_, bf16[4,8192]{1,0:T(4,128)(2,1)S(1)} %collective-permute-done.30.refs_2_, ...), custom_call_target="tpu_custom_call" | custom-call | flops 671088640 | bytes 25165824 | tf_op jit(solution)/shard_map/decode_step/pallas_call | solution.py:275
  368.8 13.8 %all_to_all.28.parts_ref = bf16[8,4,8192]{2,1,0:T(4,128)(2,1)S(1)} all-to-all(bf16[8,4,8192]{2,1,0:T(4,128)(2,1)S(1)} %get-tuple-element.37), channel_id=1, replica_groups=mesh['groups'=2,'tensor'=8,'section'=2] {'tensor'}, dimensions={0} | all-to-all | bytes 1048576 | tf_op jit(solution)/shard_map/all_to_all | solution.py:425
  (147 shorter events, 46.0 us)
Async XLA Ops:
  0.0 29.2 %copy-start = (s32[2,4,8]{2,1,0:T(4,128)S(1)}, s32[2,4,8]{2,1,0:T(4,128)}, u32[]{:S(2)}) copy-start(s32[2,4,8]{2,1,0:T(4,128)} %param.25) | copy-start | bytes 772
  0.0 8.7 %copy-start.17 = (s32[1,4,16]{2,1,0:T(4,128)S(1)}, s32[1,4,16]{2,1,0:T(4,128)}, u32[]{:S(2)}) copy-start(s32[1,4,16]{2,1,0:T(4,128)} %param.22) | copy-start | bytes 772
  3.7 170.8 %collective-permute-start = (bf16[32,8192]{1,0:T(8,128)(2,1)}, bf16[32,8192]{1,0:T(8,128)(2,1)}, u32[]{:S(2)}, u32[]{:S(2)}) collective-permute-start(bf16[32,8192]{1,0:T(8,128)(2,1)} %get-tuple-element.40), channel_id=1, source_target_pairs={{0,4},{4,8},{8,12},{12,14},{14,10},{10,6},{6,2},{2,0},{1,5},{5,9},... | collective-permute-start | bytes 1572872 | tf_op jit(solution)/shard_map/ppermute | solution.py:30
  6.7 167.8 %collective-permute-start.1 = (bf16[32,8192]{1,0:T(8,128)(2,1)}, bf16[32,8192]{1,0:T(8,128)(2,1)S(1)}, u32[]{:S(2)}, u32[]{:S(2)}) collective-permute-start(bf16[32,8192]{1,0:T(8,128)(2,1)} %get-tuple-element.40), channel_id=1, source_target_pairs={{0,2},{4,0},{8,4},{12,8},{14,12},{10,14},{6,10},{2,6},{1,3},{5,1},... | collective-permute-start | bytes 1572872 | tf_op jit(solution)/shard_map/ppermute | solution.py:30
  6.7 169.8 %collective-permute-start.2 = (bf16[32,8192]{1,0:T(8,128)(2,1)}, bf16[32,8192]{1,0:T(8,128)(2,1)S(1)}, u32[]{:S(2)}, u32[]{:S(2)}) collective-permute-start(bf16[32,8192]{1,0:T(8,128)(2,1)} %get-tuple-element.39), channel_id=1, source_target_pairs={{0,4},{4,8},{8,12},{12,14},{14,10},{10,6},{6,2},{2,0},{1,5},{5,9},... | collective-permute-start | bytes 1572872 | tf_op jit(solution)/shard_map/ppermute | solution.py:30
  8.7 167.9 %collective-permute-start.3 = (bf16[32,8192]{1,0:T(8,128)(2,1)}, bf16[32,8192]{1,0:T(8,128)(2,1)S(1)}, u32[]{:S(2)}, u32[]{:S(2)}) collective-permute-start(bf16[32,8192]{1,0:T(8,128)(2,1)} %get-tuple-element.39), channel_id=1, source_target_pairs={{0,2},{4,0},{8,4},{12,8},{14,12},{10,14},{6,10},{2,6},{1,3},{5,1},... | collective-permute-start | bytes 1572872 | tf_op jit(solution)/shard_map/ppermute | solution.py:30
  20.6 8.5 %copy-start.18 = (s32[16]{0:T(128)S(1)}, s32[16]{0:T(128)}, u32[]{:S(2)}) copy-start(s32[16]{0:T(128)} %constant.145) | copy-start | bytes 196
  20.6 8.8 %copy-start.19 = (s32[2,4]{1,0:T(2,128)S(1)}, s32[2,4]{1,0:T(2,128)}, u32[]{:S(2)}) copy-start(s32[2,4]{1,0:T(2,128)} %param.24) | copy-start | bytes 100
  20.6 8.9 %copy-start.20 = (u32[32]{0:T(128)S(1)}, u32[32]{0:T(128)}, u32[]{:S(2)}) copy-start(u32[32]{0:T(128)} %constant.148) | copy-start | bytes 388
  20.6 102.2 %copy-start.15 = (s32[1,32]{1,0:T(1,128)S(1)}, s32[1,32]{1,0:T(1,128)}, u32[]{:S(2)}) copy-start(s32[1,32]{1,0:T(1,128)} %param.23) | copy-start | bytes 388
  20.6 102.1 %copy-start.14 = (bf16[1,4,8192]{2,1,0:T(4,128)(2,1)S(1)}, bf16[1,4,8192]{2,1,0:T(4,128)(2,1)}, u32[]{:S(2)}) copy-start(bf16[1,4,8192]{2,1,0:T(4,128)(2,1)} %param.16) | copy-start | bytes 196612
  20.6 211.9 %all-to-all-start = ((bf16[8,1024,256]{2,1,0:T(8,128)(2,1)}), bf16[8,1024,256]{2,1,0:T(8,128)(2,1)}, u32[]{:S(2)}, u32[]{:S(2)}) async-start(bf16[8,1024,256]{2,1,0:T(8,128)(2,1)} %bitcast.54), calls=%async_computation | async-start | bytes 8388608 | tf_op jit(solution)/shard_map/all_to_all | solution.py:365
  139.7 89.9 %copy-start.2 = (bf16[8192,256]{1,0:T(8,128)(2,1)}, bf16[8192,256]{1,0:T(8,128)(2,1)S(1)}, u32[]{:S(2)}) copy-start(bf16[8192,256]{1,0:T(8,128)(2,1)S(1)} %get-tuple-element.23.refs_4_.refs_11_) | copy-start | bytes 12582916
  174.4 15.1 %collective-permute-start.4 = (bf16[32,8192]{1,0:T(8,128)(2,1)}, bf16[32,8192]{1,0:T(8,128)(2,1)S(1)}, u32[]{:S(2)}, u32[]{:S(2)}) collective-permute-start(bf16[32,8192]{1,0:T(8,128)(2,1)} %collective-permute-done), channel_id=1, source_target_pairs={{0,4},{4,8},{8,12},{12,14},{14,10},{10,6},{6,2},{2,0},{1,5},{5,9},... | collective-permute-start | bytes 1572872 | tf_op jit(solution)/shard_map/ppermute | solution.py:30
  174.5 15.1 %collective-permute-start.5 = (bf16[32,8192]{1,0:T(8,128)(2,1)S(1)}, bf16[32,8192]{1,0:T(8,128)(2,1)S(1)}, u32[]{:S(2)}, u32[]{:S(2)}) collective-permute-start(bf16[32,8192]{1,0:T(8,128)(2,1)S(1)} %collective-permute-done.1), channel_id=1, source_target_pairs={{0,2},{4,0},{8,4},{12,8},{14,12},{10,14},{6,10},{2,6},{1,3},{5,1},... | collective-permute-start | bytes 1572872 | tf_op jit(solution)/shard_map/ppermute | solution.py:30
  176.5 24.3 %collective-permute-start.6 = (bf16[32,8192]{1,0:T(8,128)(2,1)S(1)}, bf16[32,8192]{1,0:T(8,128)(2,1)S(1)}, u32[]{:S(2)}, u32[]{:S(2)}) collective-permute-start(bf16[32,8192]{1,0:T(8,128)(2,1)S(1)} %collective-permute-done.2), channel_id=1, source_target_pairs={{0,4},{4,8},{8,12},{12,14},{14,10},{10,6},{6,2},{2,0},{1,5},{5,9},... | collective-permute-start | bytes 1572872 | tf_op jit(solution)/shard_map/ppermute | solution.py:30
  176.6 24.2 %collective-permute-start.7 = (bf16[32,8192]{1,0:T(8,128)(2,1)S(1)}, bf16[32,8192]{1,0:T(8,128)(2,1)S(1)}, u32[]{:S(2)}, u32[]{:S(2)}) collective-permute-start(bf16[32,8192]{1,0:T(8,128)(2,1)S(1)} %collective-permute-done.3), channel_id=1, source_target_pairs={{0,2},{4,0},{8,4},{12,8},{14,12},{10,14},{6,10},{2,6},{1,3},{5,1},... | collective-permute-start | bytes 1572872 | tf_op jit(solution)/shard_map/ppermute | solution.py:30
  189.6 22.5 %collective-permute-start.8 = (bf16[32,8192]{1,0:T(8,128)(2,1)S(1)}, bf16[32,8192]{1,0:T(8,128)(2,1)S(1)}, u32[]{:S(2)}, u32[]{:S(2)}) collective-permute-start(bf16[32,8192]{1,0:T(8,128)(2,1)S(1)} %collective-permute-done.4), channel_id=1, source_target_pairs={{0,4},{4,8},{8,12},{12,14},{14,10},{10,6},{6,2},{2,0},{1,5},{5,9},... | collective-permute-start | bytes 1572872 | tf_op jit(solution)/shard_map/ppermute | solution.py:30
  189.6 33.6 %collective-permute-start.9 = (bf16[32,8192]{1,0:T(8,128)(2,1)S(1)}, bf16[32,8192]{1,0:T(8,128)(2,1)S(1)}, u32[]{:S(2)}, u32[]{:S(2)}) collective-permute-start(bf16[32,8192]{1,0:T(8,128)(2,1)S(1)} %collective-permute-done.5), channel_id=1, source_target_pairs={{0,2},{4,0},{8,4},{12,8},{14,12},{10,14},{6,10},{2,6},{1,3},{5,1},... | collective-permute-start | bytes 1572872 | tf_op jit(solution)/shard_map/ppermute | solution.py:30
  200.8 23.2 %collective-permute-start.10 = (bf16[32,8192]{1,0:T(8,128)(2,1)S(1)}, bf16[32,8192]{1,0:T(8,128)(2,1)S(1)}, u32[]{:S(2)}, u32[]{:S(2)}) collective-permute-start(bf16[32,8192]{1,0:T(8,128)(2,1)S(1)} %collective-permute-done.6), channel_id=1, source_target_pairs={{0,4},{4,8},{8,12},{12,14},{14,10},{10,6},{6,2},{2,0},{1,5},{5,9},... | collective-permute-start | bytes 1572872 | tf_op jit(solution)/shard_map/ppermute | solution.py:30
  200.8 19.6 %collective-permute-start.11 = (bf16[32,8192]{1,0:T(8,128)(2,1)S(1)}, bf16[32,8192]{1,0:T(8,128)(2,1)S(1)}, u32[]{:S(2)}, u32[]{:S(2)}) collective-permute-start(bf16[32,8192]{1,0:T(8,128)(2,1)S(1)} %collective-permute-done.7), channel_id=1, source_target_pairs={{0,2},{4,0},{8,4},{12,8},{14,12},{10,14},{6,10},{2,6},{1,3},{5,1},... | collective-permute-start | bytes 1572872 | tf_op jit(solution)/shard_map/ppermute | solution.py:30
  212.0 14.8 %collective-permute-start.12 = (bf16[32,8192]{1,0:T(8,128)(2,1)S(1)}, bf16[32,8192]{1,0:T(8,128)(2,1)S(1)}, u32[]{:S(2)}, u32[]{:S(2)}) collective-permute-start(bf16[32,8192]{1,0:T(8,128)(2,1)S(1)} %collective-permute-done.8), channel_id=1, source_target_pairs={{0,4},{4,8},{8,12},{12,14},{14,10},{10,6},{6,2},{2,0},{1,5},{5,9},... | collective-permute-start | bytes 1572872 | tf_op jit(solution)/shard_map/ppermute | solution.py:30
  220.4 9.2 %collective-permute-start.13 = (bf16[32,8192]{1,0:T(8,128)(2,1)S(1)}, bf16[32,8192]{1,0:T(8,128)(2,1)S(1)}, u32[]{:S(2)}, u32[]{:S(2)}) collective-permute-start(bf16[32,8192]{1,0:T(8,128)(2,1)S(1)} %collective-permute-done.11), channel_id=1, source_target_pairs={{0,2},{4,0},{8,4},{12,8},{14,12},{10,14},{6,10},{2,6},{1,3},{5,1},... | collective-permute-start | bytes 1572872 | tf_op jit(solution)/shard_map/ppermute | solution.py:30
  230.9 1.6 collective-permute-start.14
  242.8 82.6 %slice-start = ((s8[8388608]{0:T(1024)(128)(4,1)}), s8[4194304]{0:T(1024)(128)(4,1)S(1)}, s32[]{:S(2)}) async-start(s8[8388608]{0:T(1024)(128)(4,1)} %bitcast.52), calls=%async_computation.5 | async-start | bytes 8388608
  267.8 7.4 %collective-permute-start.15 = (bf16[4,8192]{1,0:T(4,128)(2,1)S(1)}, bf16[4,8192]{1,0:T(4,128)(2,1)S(1)}, u32[]{:S(2)}, u32[]{:S(2)}) collective-permute-start(bf16[4,8192]{1,0:T(4,128)(2,1)S(1)} %get-tuple-element.27.refs_0_), channel_id=1, source_target_pairs={{0,2},{2,0},{4,6},{6,4},{8,10},{10,8},{12,14},{14,12},{1,3},{3,1},... | collective-permute-start | bytes 196616 | tf_op jit(solution)/shard_map/ppermute | solution.py:35
  269.3 7.3 %collective-permute-start.16 = (bf16[4,8192]{1,0:T(4,128)(2,1)S(1)}, bf16[4,8192]{1,0:T(4,128)(2,1)S(1)}, u32[]{:S(2)}, u32[]{:S(2)}) collective-permute-start(bf16[4,8192]{1,0:T(4,128)(2,1)S(1)} %get-tuple-element.27.refs_0_), channel_id=1, source_target_pairs={{0,4},{2,6},{4,0},{6,2},{8,12},{10,14},{12,8},{14,10},{1,5},{3,7},... | collective-permute-start | bytes 196616 | tf_op jit(solution)/shard_map/ppermute | solution.py:35
  269.3 9.7 %collective-permute-start.17 = (bf16[4,8192]{1,0:T(4,128)(2,1)S(1)}, bf16[4,8192]{1,0:T(4,128)(2,1)S(1)}, u32[]{:S(2)}, u32[]{:S(2)}) collective-permute-start(bf16[4,8192]{1,0:T(4,128)(2,1)S(1)} %get-tuple-element.27.refs_0_), channel_id=1, source_target_pairs={{0,6},{2,4},{4,2},{6,0},{8,14},{10,12},{12,10},{14,8},{1,7},{3,5},... | collective-permute-start | bytes 196616 | tf_op jit(solution)/shard_map/ppermute | solution.py:35
  271.3 9.3 %collective-permute-start.18 = (bf16[4,8192]{1,0:T(4,128)(2,1)S(1)}, bf16[4,8192]{1,0:T(4,128)(2,1)S(1)}, u32[]{:S(2)}, u32[]{:S(2)}) collective-permute-start(bf16[4,8192]{1,0:T(4,128)(2,1)S(1)} %get-tuple-element.27.refs_0_), channel_id=1, source_target_pairs={{0,8},{2,10},{4,12},{6,14},{8,0},{10,2},{12,4},{14,6},{1,9},{3,11}... | collective-permute-start | bytes 196616 | tf_op jit(solution)/shard_map/ppermute | solution.py:35
  272.4 11.3 %collective-permute-start.19 = (bf16[4,8192]{1,0:T(4,128)(2,1)S(1)}, bf16[4,8192]{1,0:T(4,128)(2,1)S(1)}, u32[]{:S(2)}, u32[]{:S(2)}) collective-permute-start(bf16[4,8192]{1,0:T(4,128)(2,1)S(1)} %get-tuple-element.27.refs_0_), channel_id=1, source_target_pairs={{0,10},{2,8},{4,14},{6,12},{8,2},{10,0},{12,6},{14,4},{1,11},{3,9}... | collective-permute-start | bytes 196616 | tf_op jit(solution)/shard_map/ppermute | solution.py:35
  275.1 8.6 %collective-permute-start.20 = (bf16[4,8192]{1,0:T(4,128)(2,1)S(1)}, bf16[4,8192]{1,0:T(4,128)(2,1)S(1)}, u32[]{:S(2)}, u32[]{:S(2)}) collective-permute-start(bf16[4,8192]{1,0:T(4,128)(2,1)S(1)} %get-tuple-element.27.refs_0_), channel_id=1, source_target_pairs={{0,12},{2,14},{4,8},{6,10},{8,4},{10,6},{12,0},{14,2},{1,13},{3,15... | collective-permute-start | bytes 196616 | tf_op jit(solution)/shard_map/ppermute | solution.py:35
  276.6 7.1 %collective-permute-start.21 = (bf16[4,8192]{1,0:T(4,128)(2,1)S(1)}, bf16[4,8192]{1,0:T(4,128)(2,1)S(1)}, u32[]{:S(2)}, u32[]{:S(2)}) collective-permute-start(bf16[4,8192]{1,0:T(4,128)(2,1)S(1)} %get-tuple-element.27.refs_0_), channel_id=1, source_target_pairs={{0,14},{2,12},{4,10},{6,8},{8,6},{10,4},{12,2},{14,0},{1,15},{3,13... | collective-permute-start | bytes 196616 | tf_op jit(solution)/shard_map/ppermute | solution.py:35
  287.1 38.3 %slice-start.1 = ((s8[8388608]{0:T(1024)(128)(4,1)}), s8[4194304]{0:T(1024)(128)(4,1)S(1)}, s32[]{:S(2)}) async-start(s8[8388608]{0:T(1024)(128)(4,1)} %bitcast.52), calls=%async_computation.6 | async-start | bytes 8388608
  309.4 7.4 %collective-permute-start.22 = (bf16[4,8192]{1,0:T(4,128)(2,1)S(1)}, bf16[4,8192]{1,0:T(4,128)(2,1)S(1)}, u32[]{:S(2)}, u32[]{:S(2)}) collective-permute-start(bf16[4,8192]{1,0:T(4,128)(2,1)S(1)} %get-tuple-element.31.refs_0_), channel_id=1, source_target_pairs={{0,2},{2,0},{4,6},{6,4},{8,10},{10,8},{12,14},{14,12},{1,3},{3,1},... | collective-permute-start | bytes 196616 | tf_op jit(solution)/shard_map/ppermute | solution.py:35
  311.0 7.3 %collective-permute-start.23 = (bf16[4,8192]{1,0:T(4,128)(2,1)S(1)}, bf16[4,8192]{1,0:T(4,128)(2,1)S(1)}, u32[]{:S(2)}, u32[]{:S(2)}) collective-permute-start(bf16[4,8192]{1,0:T(4,128)(2,1)S(1)} %get-tuple-element.31.refs_0_), channel_id=1, source_target_pairs={{0,4},{2,6},{4,0},{6,2},{8,12},{10,14},{12,8},{14,10},{1,5},{3,7},... | collective-permute-start | bytes 196616 | tf_op jit(solution)/shard_map/ppermute | solution.py:35
  311.0 9.7 %collective-permute-start.24 = (bf16[4,8192]{1,0:T(4,128)(2,1)S(1)}, bf16[4,8192]{1,0:T(4,128)(2,1)S(1)}, u32[]{:S(2)}, u32[]{:S(2)}) collective-permute-start(bf16[4,8192]{1,0:T(4,128)(2,1)S(1)} %get-tuple-element.31.refs_0_), channel_id=1, source_target_pairs={{0,6},{2,4},{4,2},{6,0},{8,14},{10,12},{12,10},{14,8},{1,7},{3,5},... | collective-permute-start | bytes 196616 | tf_op jit(solution)/shard_map/ppermute | solution.py:35
  313.0 8.7 %collective-permute-start.25 = (bf16[4,8192]{1,0:T(4,128)(2,1)S(1)}, bf16[4,8192]{1,0:T(4,128)(2,1)S(1)}, u32[]{:S(2)}, u32[]{:S(2)}) collective-permute-start(bf16[4,8192]{1,0:T(4,128)(2,1)S(1)} %get-tuple-element.31.refs_0_), channel_id=1, source_target_pairs={{0,8},{2,10},{4,12},{6,14},{8,0},{10,2},{12,4},{14,6},{1,9},{3,11}... | collective-permute-start | bytes 196616 | tf_op jit(solution)/shard_map/ppermute | solution.py:35
  314.1 9.8 %collective-permute-start.26 = (bf16[4,8192]{1,0:T(4,128)(2,1)S(1)}, bf16[4,8192]{1,0:T(4,128)(2,1)S(1)}, u32[]{:S(2)}, u32[]{:S(2)}) collective-permute-start(bf16[4,8192]{1,0:T(4,128)(2,1)S(1)} %get-tuple-element.31.refs_0_), channel_id=1, source_target_pairs={{0,10},{2,8},{4,14},{6,12},{8,2},{10,0},{12,6},{14,4},{1,11},{3,9}... | collective-permute-start | bytes 196616 | tf_op jit(solution)/shard_map/ppermute | solution.py:35
  316.8 7.1 %collective-permute-start.27 = (bf16[4,8192]{1,0:T(4,128)(2,1)S(1)}, bf16[4,8192]{1,0:T(4,128)(2,1)S(1)}, u32[]{:S(2)}, u32[]{:S(2)}) collective-permute-start(bf16[4,8192]{1,0:T(4,128)(2,1)S(1)} %get-tuple-element.31.refs_0_), channel_id=1, source_target_pairs={{0,12},{2,14},{4,8},{6,10},{8,4},{10,6},{12,0},{14,2},{1,13},{3,15... | collective-permute-start | bytes 196616 | tf_op jit(solution)/shard_map/ppermute | solution.py:35
  318.3 7.1 %collective-permute-start.28 = (bf16[4,8192]{1,0:T(4,128)(2,1)S(1)}, bf16[4,8192]{1,0:T(4,128)(2,1)S(1)}, u32[]{:S(2)}, u32[]{:S(2)}) collective-permute-start(bf16[4,8192]{1,0:T(4,128)(2,1)S(1)} %get-tuple-element.31.refs_0_), channel_id=1, source_target_pairs={{0,14},{2,12},{4,10},{6,8},{8,6},{10,4},{12,2},{14,0},{1,15},{3,13... | collective-permute-start | bytes 196616 | tf_op jit(solution)/shard_map/ppermute | solution.py:35
  346.7 7.3 %collective-permute-start.29 = (bf16[4,8192]{1,0:T(4,128)(2,1)S(1)}, bf16[4,8192]{1,0:T(4,128)(2,1)S(1)}, u32[]{:S(2)}, u32[]{:S(2)}) collective-permute-start(bf16[4,8192]{1,0:T(4,128)(2,1)S(1)} %get-tuple-element.35.refs_0_), channel_id=1, source_target_pairs={{0,2},{2,0},{4,6},{6,4},{8,10},{10,8},{12,14},{14,12},{1,3},{3,1},... | collective-permute-start | bytes 196616 | tf_op jit(solution)/shard_map/ppermute | solution.py:35
  348.2 7.3 %collective-permute-start.30 = (bf16[4,8192]{1,0:T(4,128)(2,1)S(1)}, bf16[4,8192]{1,0:T(4,128)(2,1)S(1)}, u32[]{:S(2)}, u32[]{:S(2)}) collective-permute-start(bf16[4,8192]{1,0:T(4,128)(2,1)S(1)} %get-tuple-element.35.refs_0_), channel_id=1, source_target_pairs={{0,4},{2,6},{4,0},{6,2},{8,12},{10,14},{12,8},{14,10},{1,5},{3,7},... | collective-permute-start | bytes 196616 | tf_op jit(solution)/shard_map/ppermute | solution.py:35
  348.2 9.7 %collective-permute-start.31 = (bf16[4,8192]{1,0:T(4,128)(2,1)S(1)}, bf16[4,8192]{1,0:T(4,128)(2,1)S(1)}, u32[]{:S(2)}, u32[]{:S(2)}) collective-permute-start(bf16[4,8192]{1,0:T(4,128)(2,1)S(1)} %get-tuple-element.35.refs_0_), channel_id=1, source_target_pairs={{0,6},{2,4},{4,2},{6,0},{8,14},{10,12},{12,10},{14,8},{1,7},{3,5},... | collective-permute-start | bytes 196616 | tf_op jit(solution)/shard_map/ppermute | solution.py:35
  350.3 7.9 %collective-permute-start.32 = (bf16[4,8192]{1,0:T(4,128)(2,1)S(1)}, bf16[4,8192]{1,0:T(4,128)(2,1)S(1)}, u32[]{:S(2)}, u32[]{:S(2)}) collective-permute-start(bf16[4,8192]{1,0:T(4,128)(2,1)S(1)} %get-tuple-element.35.refs_0_), channel_id=1, source_target_pairs={{0,8},{2,10},{4,12},{6,14},{8,0},{10,2},{12,4},{14,6},{1,9},{3,11}... | collective-permute-start | bytes 196616 | tf_op jit(solution)/shard_map/ppermute | solution.py:35
  351.3 7.8 %collective-permute-start.33 = (bf16[4,8192]{1,0:T(4,128)(2,1)S(1)}, bf16[4,8192]{1,0:T(4,128)(2,1)S(1)}, u32[]{:S(2)}, u32[]{:S(2)}) collective-permute-start(bf16[4,8192]{1,0:T(4,128)(2,1)S(1)} %get-tuple-element.35.refs_0_), channel_id=1, source_target_pairs={{0,10},{2,8},{4,14},{6,12},{8,2},{10,0},{12,6},{14,4},{1,11},{3,9}... | collective-permute-start | bytes 196616 | tf_op jit(solution)/shard_map/ppermute | solution.py:35
  354.1 6.2 %collective-permute-start.34 = (bf16[4,8192]{1,0:T(4,128)(2,1)S(1)}, bf16[4,8192]{1,0:T(4,128)(2,1)S(1)}, u32[]{:S(2)}, u32[]{:S(2)}) collective-permute-start(bf16[4,8192]{1,0:T(4,128)(2,1)S(1)} %get-tuple-element.35.refs_0_), channel_id=1, source_target_pairs={{0,12},{2,14},{4,8},{6,10},{8,4},{10,6},{12,0},{14,2},{1,13},{3,15... | collective-permute-start | bytes 196616 | tf_op jit(solution)/shard_map/ppermute | solution.py:35
  355.5 7.0 %collective-permute-start.35 = (bf16[4,8192]{1,0:T(4,128)(2,1)S(1)}, bf16[4,8192]{1,0:T(4,128)(2,1)S(1)}, u32[]{:S(2)}, u32[]{:S(2)}) collective-permute-start(bf16[4,8192]{1,0:T(4,128)(2,1)S(1)} %get-tuple-element.35.refs_0_), channel_id=1, source_target_pairs={{0,14},{2,12},{4,10},{6,8},{8,6},{10,4},{12,2},{14,0},{1,15},{3,13... | collective-permute-start | bytes 196616 | tf_op jit(solution)/shard_map/ppermute | solution.py:35
  362.5 21.9 %copy-start.1 = (s32[2,4,8]{2,1,0:T(4,128)S(1)}, s32[2,4,8]{2,1,0:T(4,128)}, u32[]{:S(2)}) copy-start(s32[2,4,8]{2,1,0:T(4,128)} %param.25) | copy-start | bytes 772
  (14 other events, 52.8 us)

commit v3 on v2

--- a/solution.py
+++ b/solution.py
@@ -14,6 +14,7 @@
 ROPE_BASE = 500000.0
 LANES = 8
 CHUNKS = 8
+KEPT = (16, 24, 32, 36, 40, 44, 48, 52, 56)
 VMEM_LIMIT = 16 * 1024 * 1024
 
 
@@ -72,6 +73,25 @@
     )(rows, gain)
 
 
+def opening_kernel(rows_ref, gain_ref, pages_ref, out_ref):
+    width = rows_ref.shape[1]
+    gain = gain_ref[...].astype(jnp.float32)
+    out_ref[:, :width] = normed_rows(rows_ref[...].astype(jnp.float32), gain).astype(jnp.bfloat16)
+    out_ref[:, width:] = pages_ref[...]
+
+
+def opening(rows, gain, pages):
+    shape = (rows.shape[0], rows.shape[1] + pages.shape[1])
+    return pl.pallas_call(
+        opening_kernel,
+        out_shape=jax.ShapeDtypeStruct(shape, jnp.bfloat16),
+        in_specs=[whole()] * 3,
+        out_specs=whole(),
+        compiler_params=pltpu.CompilerParams(vmem_limit_bytes=VMEM_LIMIT),
+        name="opening",
+    )(rows, gain, pages)
+
+
 def fetch_kernel(*refs):
     count = len(refs) // 2
     sems = refs[-1]
@@ -94,21 +114,33 @@
     )(*arrays)
 
 
-def parcels_kernel(heads, table_ref, pool_ref, out_ref, held, load_sem, store_sem):
-    pages = held.shape[0]
+def parcels_kernel(heads, kept, table_ref, used_ref, pool_ref, out_ref, held, load_sem, store_sem):
     width = out_ref.shape[-1]
-
-    def load(index):
-        return pltpu.make_async_copy(pool_ref.at[table_ref[index]], held.at[index], load_sem.at[index])
-
-    for index in range(pages):
-        load(index).start()
-    for index in range(pages):
-        load(index).wait()
+    each, per_request = table_ref.shape
+    total = used_ref[0]
+    for r in range(1, each):
+        total = total + used_ref[r]
+    loads = []
+    front, back = 0, total
+    for r in range(each):
+        used = used_ref[r]
+        for p in range(per_request):
+            spot = jnp.where(p < used, front + p, back + p - used)
+            copy = pltpu.make_async_copy(
+                pool_ref.at[table_ref[r, p]], held.at[spot], load_sem.at[r * per_request + p]
+            )
+            copy.start()
+            loads.append(copy)
+        front = front + used
+        back = back + per_request - used
+    for copy in loads:
+        copy.wait()
     stores = []
     for target, head in enumerate(heads):
         copy = pltpu.make_async_copy(
-            held.at[:, :, pl.ds(head * width, width)], out_ref.at[target], store_sem.at[target]
+            held.at[pl.ds(0, kept), :, pl.ds(head * width, width)],
+            out_ref.at[target],
+            store_sem.at[target],
         )
         copy.start()
         stores.append(copy)
@@ -116,13 +148,15 @@
         copy.wait()
 
 
-def make_parcels(table, pool, heads, width):
+def make_parcels(table, used, pool, heads, width, kept):
     pages, rows, _ = pool.shape
-    return pl.pallas_call(
-        functools.partial(parcels_kernel, heads),
-        out_shape=jax.ShapeDtypeStruct((len(heads), pages, rows, width), jnp.bfloat16),
-        in_specs=[pl.BlockSpec(memory_space=pltpu.SMEM), pl.BlockSpec(memory_space=pl.ANY)],
-        out_specs=pl.BlockSpec(memory_space=pl.ANY),
+    smem = pl.BlockSpec(memory_space=pltpu.SMEM)
+    anywhere = pl.BlockSpec(memory_space=pl.ANY)
+    return pl.pallas_call(
+        functools.partial(parcels_kernel, heads, kept),
+        out_shape=jax.ShapeDtypeStruct((len(heads), kept, rows, width), jnp.bfloat16),
+        in_specs=[smem, smem, anywhere],
+        out_specs=anywhere,
         scratch_shapes=[
             pltpu.VMEM(pool.shape, jnp.bfloat16),
             pltpu.SemaphoreType.DMA((pages,)),
@@ -130,20 +164,63 @@
         ],
         compiler_params=pltpu.CompilerParams(vmem_limit_bytes=VMEM_LIMIT),
         name="parcels",
-    )(table, pool)
-
-
-def assemble_kernel(rows, request_ref, offset_ref, arrived_ref, cache_ref, out_ref, sems):
-    fetched = pltpu.make_async_copy(cache_ref, out_ref, sems.at[0])
-    fetched.start()
-    fetched.wait()
+    )(table, used, pool)
+
+
+def unpack_kernel(used_ref, first_ref, packed_ref, out_ref, sems):
+    count, per_request = out_ref.shape[:2]
+    each = count // packed_ref.shape[0]
+    sizes = []
+    size = per_request
+    while size:
+        sizes.append(size)
+        size //= 2
+
+    def copies(r, action):
+        used = used_ref[r]
+        done = jnp.int32(0)
+        for index, size in enumerate(sizes):
+            present = (used // size) % 2 == 1
+
+            @pl.when(present)
+            def _():
+                copy = pltpu.make_async_copy(
+                    packed_ref.at[r // each, pl.ds(first_ref[r] + done, size)],
+                    out_ref.at[r, pl.ds(done, size)],
+                    sems.at[r, index],
+                )
+                action(copy)
+
+            done = done + jnp.where(present, size, 0)
+
+    for r in range(count):
+        copies(r, lambda copy: copy.start())
+    for r in range(count):
+        copies(r, lambda copy: copy.wait())
+
+
+def unpack(used, first, packed, count, per_request):
+    smem = pl.BlockSpec(memory_space=pltpu.SMEM)
+    anywhere = pl.BlockSpec(memory_space=pl.ANY)
+    return pl.pallas_call(
+        unpack_kernel,
+        out_shape=jax.ShapeDtypeStruct((count, per_request) + packed.shape[2:], packed.dtype),
+        in_specs=[smem, smem, anywhere],
+        out_specs=anywhere,
+        scratch_shapes=[pltpu.SemaphoreType.DMA((count, per_request.bit_length()))],
+        compiler_params=pltpu.CompilerParams(vmem_limit_bytes=VMEM_LIMIT),
+        name="unpack",
+    )(used, first, packed)
+
+
+def patch_kernel(rows, request_ref, offset_ref, arrived_ref, _cache_in, out_ref, sems):
     copies = []
     for piece in range(arrived_ref.shape[0] // rows):
         offset = pl.multiple_of(offset_ref[piece], rows)
         copy = pltpu.make_async_copy(
             arrived_ref.at[pl.ds(piece * rows, rows), :],
             out_ref.at[request_ref[piece], pl.ds(offset, rows), :],
-            sems.at[piece + 1],
+            sems.at[piece],
         )
         copy.start()
         copies.append(copy)
@@ -151,17 +228,17 @@
         copy.wait()
 
 
-def assemble(requests, offsets, arrived, cache, rows):
+def patch(requests, offsets, arrived, cache, rows):
     smem = pl.BlockSpec(memory_space=pltpu.SMEM)
-    anywhere = pl.BlockSpec(memory_space=pl.ANY)
-    return pl.pallas_call(
-        functools.partial(assemble_kernel, rows),
+    return pl.pallas_call(
+        functools.partial(patch_kernel, rows),
         out_shape=pltpu.VMEM(cache.shape, cache.dtype),
-        in_specs=[smem, smem, anywhere, anywhere],
+        in_specs=[smem, smem, pl.BlockSpec(memory_space=pl.ANY), whole()],
         out_specs=whole(),
-        scratch_shapes=[pltpu.SemaphoreType.DMA((arrived.shape[0] // rows + 1,))],
-        compiler_params=pltpu.CompilerParams(vmem_limit_bytes=VMEM_LIMIT),
-        name="assemble",
+        scratch_shapes=[pltpu.SemaphoreType.DMA((arrived.shape[0] // rows,))],
+        input_output_aliases={3: 0},
+        compiler_params=pltpu.CompilerParams(vmem_limit_bytes=VMEM_LIMIT),
+        name="patch",
     )(requests, offsets, arrived, cache)
 
 
@@ -180,21 +257,17 @@
     heads = q_cols // HD
     depth = width // CHUNKS
 
-    if blocks > 1:
-        for k in range(blocks):
-            x_rows[k * each : (k + 1) * each, :] = x_refs[k][...].astype(jnp.float32)
-        order = order_ref[...]
+    for k in range(blocks):
+        x_rows[k * each : (k + 1) * each, :] = x_refs[k][:, :width].astype(jnp.float32)
+    order = order_ref[...]
 
     query = jnp.zeros((count, q_cols), jnp.float32)
     keyvalue = jnp.zeros((count, 2 * HD), jnp.float32)
     for c in range(CHUNKS):
         part = slice(c * depth, (c + 1) * depth)
-        if blocks > 1:
-            x = jnp.dot(
-                order, x_rows[:, part].astype(jnp.bfloat16), preferred_element_type=jnp.float32
-            ).astype(jnp.bfloat16)
-        else:
-            x = x_refs[0][:, part]
+        x = jnp.dot(
+            order, x_rows[:, part].astype(jnp.bfloat16), preferred_element_type=jnp.float32
+        ).astype(jnp.bfloat16)
         query += jnp.dot(x, wq[part, :], preferred_element_type=jnp.float32)
         keyvalue += jnp.dot(x, wkv[part, :], preferred_element_type=jnp.float32)
 
@@ -349,22 +422,43 @@
     if w_keyvalue.shape[1] < 2 * HD:
         other = swap_xor(w_keyvalue, 1)
         is_key = rank % 2 == 0
-        w_kv = jnp.concatenate(
+        w_pair = jnp.concatenate(
             [jnp.where(is_key, w_keyvalue, other), jnp.where(is_key, other, w_keyvalue)], axis=1
         )
     else:
-        w_kv = w_keyvalue
-
-    w_q, w_kv, w_o = fetch(w_query, w_kv, w_output)
-    first_pages = lax.all_gather(own_table[:, 0], "tensor", axis=0)
-    states = lax.all_gather(normalize(decode_states[0], gain), "tensor", axis=0, tiled=True)
+        w_pair = w_keyvalue
+
+    numbers = jnp.arange(count * each, dtype=jnp.int32)
+    pages = jnp.broadcast_to(own_table[:, :1], (each, HD)).astype(jnp.bfloat16)
+    opened = opening(decode_states[0], gain, pages)
+    blocks = [opened] + [swap_xor(opened, bits) for bits in range(1, count)]
+    first_pages = jnp.concatenate([block[:, width:] for block in blocks])[:, 0].astype(jnp.int32)
 
     heads = tuple(target // shared for target in range(count))
-    parcels = make_parcels(own_table.reshape(-1), pool, heads, 2 * HD)
-    span = own_table.shape[1] * page_size
-    cache = lax.all_to_all(
-        parcels.reshape(count, each * span, 2 * HD), "tensor", split_axis=0, concat_axis=0, tiled=True
-    ).reshape(count * each, span, 2 * HD)
+    per_request = own_table.shape[1]
+    used = (lengths + page_size - 1) // page_size
+    by_owner = used.reshape(count, each)
+    most = jnp.max(jnp.sum(by_owner, axis=1, keepdims=True), keepdims=True)
+    for axis in ("section", "groups"):
+        for bit in range(lax.axis_size(axis).bit_length() - 1):
+            pairs = [(s, s ^ (1 << bit)) for s in range(lax.axis_size(axis))]
+            most = jnp.maximum(most, lax.ppermute(most, axis, pairs))
+    first = (jnp.cumsum(by_owner, axis=1) - by_owner).reshape(-1)
+    own_used = lax.dynamic_slice_in_dim(used, rank * each, each)
+    limits = [limit for limit in KEPT if limit < pool.shape[0]] + [pool.shape[0]]
+
+    def exchange(kept):
+        def branch(table, own, used, first, pool):
+            parcels = make_parcels(table, own, pool, heads, 2 * HD, kept)
+            packed = lax.all_to_all(parcels, "tensor", split_axis=0, concat_axis=0, tiled=True)
+            return unpack(used, first, packed, count * each, per_request)
+
+        return branch
+
+    choice = jnp.sum((most[0, 0] > jnp.array(limits[:-1], jnp.int32)).astype(jnp.int32))
+    cache = lax.switch(
+        choice, [exchange(limit) for limit in limits], own_table, own_used, used, first, pool
+    ).reshape(count * each, per_request * page_size, 2 * HD)
 
     half = tokens // 2
     ready = normalize(prompt_states[0], gain)
@@ -383,7 +477,7 @@
                 going[piece][way] = ring_shift(going[piece][way], sign)
                 arrivals.append((-sign * hop, piece, going[piece][way]))
     products = [
-        jnp.dot(rows, w_kv, preferred_element_type=jnp.float32) for _, _, rows in arrivals
+        jnp.dot(rows, w_pair, preferred_element_type=jnp.float32) for _, _, rows in arrivals
     ]
     behind = jnp.array([steps for steps, _, _ in arrivals], jnp.int32)
     halves = jnp.array([piece for _, piece, _ in arrivals], jnp.int32)
@@ -400,21 +494,18 @@
     anchor = (section + 1) % sections
     targets = lax.dynamic_index_in_dim(dest_rank, anchor, 0, keepdims=False)
     landing = lax.dynamic_index_in_dim(dest_page, anchor, 0, keepdims=False)[:, 0]
-    numbers = jnp.arange(count * each, dtype=jnp.int32)
-    here = (numbers[None, :] // each == targets[:, None]) & (
-        first_pages.reshape(1, -1) == landing[:, None]
-    )
-    receivers = jnp.sum(jnp.where(here, numbers[None, :], 0), axis=1)
-    cache = assemble(receivers[starts // PLEN], starts % PLEN, arrived, cache, half)
+    rows_of = (rank ^ (numbers // each)) * each + numbers % each
+    here = (rows_of[None, :] // each == targets[:, None]) & (first_pages[None, :] == landing[:, None])
+    receivers = jnp.sum(jnp.where(here, rows_of[None, :], 0), axis=1)
+    w_q, w_kv, w_o, cache = fetch(w_query, w_pair, w_output, cache)
+    cache = patch(receivers[starts // PLEN], starts % PLEN, arrived, cache, half)
 
     times = lengths[None, :] + jnp.arange(STEPS, dtype=jnp.int32)[:, None]
     cosine, sine = rope_tables(times.reshape(-1))
     cosine = cosine.reshape(STEPS, count * each, HD)
     sine = sine.reshape(STEPS, count * each, HD)
-    rows_of = ((rank ^ (numbers // each)) * each + numbers % each)[None, :]
-    chosen = (numbers[:, None] == rows_of).astype(jnp.bfloat16)
+    chosen = (numbers[:, None] == rows_of[None, :]).astype(jnp.bfloat16)
     state = decode_states[0]
-    blocks = [states]
     outputs = []
     earlier = []
     for iteration in range(STEPS):

time: 385 us -> 391 us (1.016)
  blocking collectives: 187 us -> 62.9 us
  waiting for transfers between devices: 47.9 us -> 119 us
  loops' own time: 0 us -> 16.1 us
  starting transfers between devices: 55.3 us -> 70.5 us
  local copies, waits for them, and re-layouts: 33 us -> 42.3 us
  matrix products: 14.2 us -> 20.6 us
  other arithmetic: 3.62 us -> 7.76 us
    unnamed x1 -> x0, blocking collectives: 91.8 us -> none
    all_to_all x1, waiting for transfers between devices: 0.01 us -> 65.7 us  [branch(): lax.all_to_all(parcels, 'tensor', split_axis=0, concat_axis=0, tiled=True)]
    all_gather x1 -> x0, blocking collectives: 31.8 us -> none  [on_device(): lax.all_gather(normalize(decode_states[0], gain), 'tensor', axis=0, tiled...]
    another operation x0 -> x1, loops' own time: none -> 16.1 us  [on_device(): lax.switch(choice, [exchange(limit) for limit in limits], own_table, own_...]
    ppermute x21 -> x28, starting transfers between devices: 33.6 us -> 47.2 us  [swap_xor(): return lax.ppermute(value, 'tensor', [(s, s ^ mask) for s in range(count)])]
    dot_general x16, matrix products: 14.2 us -> 20.6 us  [on_device(): jnp.dot(rows, w_pair, preferred_element_type=jnp.float32)]
    slice x1 -> x9, local copies, waits for them, and re-layouts: 0.11 us -> 5.86 us  [the longest x8 5.74 us: on_device(): block[:, width:]]
    ppermute x14, waiting for transfers between devices: 33.2 us -> 38.6 us  [ring_shift(): return lax.ppermute(value, 'tensor', pairs)]
  transfers between devices with their start and end apart: 37 -> 46, of which waited for: 16 -> 21; matrix products, arithmetic and copies ran while one was open for 5% -> 10% of each run, Pallas kernels for 3% -> 4%
where the time goes in v3:
time: 391 us; the launch traced here: 388 us
  waiting for transfers between devices  119 us (30%)
  starting transfers between devices  70.5 us (18%)
  blocking collectives  62.9 us (16%)
  Pallas kernels  45.7 us (12%)
  local copies, waits for them, and re-layouts  42.3 us (11%)
  matrix products  20.6 us (5%)
  loops' own time  16.1 us (4%)
  other arithmetic  7.76 us (2%)
    all_to_all x1, waiting for transfers between devices, branch(): lax.all_to_all(parcels, 'tensor', split_axis=0, concat_axis=0, tiled=True)  65.7 us
    all_to_all x4, blocking collectives, on_device(): lax.all_to_all(parts, 'tensor', split_axis=0, concat_axis=0, tiled=True)  62.9 us
    ppermute x28, starting transfers between devices, swap_xor(): return lax.ppermute(value, 'tensor', [(s, s ^ mask) for s in range(count)])  47.2 us
    ppermute x14, waiting for transfers between devices, ring_shift(): return lax.ppermute(value, 'tensor', pairs)  38.6 us
    unnamed x72, local copies, waits for them, and re-layouts  30.7 us
    pallas_call x4, Pallas kernels, step(): pl.pallas_call(functools.partial(step_kernel, blocks, iteration), out_sha...  25.5 us
    dot_general x16, matrix products, on_device(): jnp.dot(rows, w_pair, preferred_element_type=jnp.float32)  20.6 us
    another operation x1, loops' own time, on_device(): lax.switch(choice, [exchange(limit) for limit in limits], own_table, own_...  16.1 us
  transfers between devices with their start and end apart: 46, of which 21 were waited for; matrix products, arithmetic and copies ran while one was open for 10% of the time, Pallas kernels for 4%

profile of v3, /device:TPU:0, one launch (start us, length us, event | category | flops | bytes accessed | tf_op | source)
XLA Modules:
  0.0 388.1 jit_solution(5401392285196801650)
XLA Ops:
  3.8 3.0 collective-permute-start.9
  6.8 2.0 collective-permute-start.11
  10.3 3.0 convolution_dynamic-update-slice_fusion.15
  21.6 3.0 convolution_dynamic-update-slice_fusion.14
  26.0 3.3 collective-permute-start.8
  43.7 7.2 %collective-permute-done.13 = bf16[32,8192]{1,0:T(8,128)(2,1)S(1)} collective-permute-done((bf16[32,8192]{1,0:T(8,128)(2,1)}, bf16[32,8192]{1,0:T(8,128)(2,1)S(1)}, u32[]{:S(2)}, u32[]{:S(2)}) %collective-permute-start.13) | collective-permute-done | bytes 524320 | tf_op jit(solution)/shard_map/ppermute | solution.py:31
  56.8 5.3 %collective-permute-done.15 = bf16[32,8192]{1,0:T(8,128)(2,1)S(1)} collective-permute-done((bf16[32,8192]{1,0:T(8,128)(2,1)}, bf16[32,8192]{1,0:T(8,128)(2,1)S(1)}, u32[]{:S(2)}, u32[]{:S(2)}) %collective-permute-start.15) | collective-permute-done | bytes 524320 | tf_op jit(solution)/shard_map/ppermute | solution.py:31
  63.5 2.0 collective-permute-done.16
  68.1 5.3 %collective-permute-done.17 = bf16[32,8192]{1,0:T(8,128)(2,1)S(1)} collective-permute-done((bf16[32,8192]{1,0:T(8,128)(2,1)S(1)}, bf16[32,8192]{1,0:T(8,128)(2,1)S(1)}, u32[]{:S(2)}, u32[]{:S(2)}) %collective-permute-start.17) | collective-permute-done | bytes 524320 | tf_op jit(solution)/shard_map/ppermute | solution.py:31
  74.7 2.0 collective-permute-done.18
  78.2 5.2 %collective-permute-done.19 = bf16[32,8192]{1,0:T(8,128)(2,1)S(1)} collective-permute-done((bf16[32,8192]{1,0:T(8,128)(2,1)S(1)}, bf16[32,8192]{1,0:T(8,128)(2,1)S(1)}, u32[]{:S(2)}, u32[]{:S(2)}) %collective-permute-start.19) | collective-permute-done | bytes 524320 | tf_op jit(solution)/shard_map/ppermute | solution.py:31
  84.1 2.4 collective-permute-done.20
  89.1 6.3 %collective-permute-done.21 = bf16[32,8192]{1,0:T(8,128)(2,1)S(1)} collective-permute-done((bf16[32,8192]{1,0:T(8,128)(2,1)S(1)}, bf16[32,8192]{1,0:T(8,128)(2,1)S(1)}, u32[]{:S(2)}, u32[]{:S(2)}) %collective-permute-start.21) | collective-permute-done | bytes 524320 | tf_op jit(solution)/shard_map/ppermute | solution.py:31
  104.1 4.5 %collective-permute-start.6 = (bf16[4,8320]{1,0:T(4,128)(2,1)}, bf16[4,8320]{1,0:T(4,128)(2,1)}, u32[]{:S(2)}, u32[]{:S(2)}) collective-permute-start(bf16[4,8320]{1,0:T(4,128)(2,1)} %opening.1.refs_0_), channel_id=1, source_target_pairs={{0,14},{2,12},{4,10},{6,8},{8,6},{10,4},{12,2},{14,0},{1,15},{3,13... | collective-permute-start | bytes 199688 | tf_op jit(solution)/shard_map/ppermute | solution.py:36
  109.9 96.3 %conditional.1 = (bf16[32,256,256]{2,1,0:T(8,128)(2,1)}) conditional(s32[]{:T(128)} %clamp.3, (s32[8,4]{1,0:T(8,128)S(1)}, s32[32]{0:T(128)S(1)}, s32[]{:T(128)}, bf16[1,64,16,2048]{3,2,1,0:T(8,128)(2,1)}, s32[4,16]{1,0:T(4,128)S(1)}) %tuple.67, (s32[8,4]{1,0:T(8,128)S(1)}, s32[32]{0:T(128)S(1)}, s32[]{:T(128)}, ...), branch_computations={%region_4.5_spmd, %region_5.6_spmd, %region_6.7_spmd, %region_7.8_... | conditional | flops 35 | bytes 29360906 | solution.py:459
  118.8 5.0 %parcels.15 = bf16[8,44,16,256]{3,2,1,0:T(8,128)(2,1)} custom-call(s32[4,16]{1,0:T(4,128)S(1)} %get-tuple-element.274.table_ref, s32[4]{0:T(128)S(1)} %dynamic_slice.34.used_ref, bf16[64,16,2048]{2,1,0:T(8,128)(2,1)} %bitcast.88), custom_call_target="tpu_custom_call" | custom-call | tf_op jit(solution)/shard_map/cond/branch_5_fun/parcels/pallas_call | solution.py:155
  123.8 4.8 %all-to-all-start.5 = ((bf16[8,44,16,256]{3,2,1,0:T(8,128)(2,1)}), bf16[8,44,16,256]{3,2,1,0:T(8,128)(2,1)S(1)}, u32[]{:S(2)}, u32[]{:S(2)}) async-start(bf16[8,44,16,256]{3,2,1,0:T(8,128)(2,1)} %parcels.15), calls=%async_computation.5 | async-start | bytes 5767168 | tf_op jit(solution)/shard_map/cond/branch_5_fun/all_to_all | solution.py:453
  128.7 65.7 %all-to-all-done.5.packed_ref = bf16[8,44,16,256]{3,2,1,0:T(8,128)(2,1)S(1)} async-done(((bf16[8,44,16,256]{3,2,1,0:T(8,128)(2,1)}), bf16[8,44,16,256]{3,2,1,0:T(8,128)(2,1)S(1)}, u32[]{:S(2)}, u32[]{:S(2)}) %all-to-all-start.5) | async-done | bytes 2883616 | tf_op jit(solution)/shard_map/cond/branch_5_fun/all_to_all | solution.py:453
  194.3 4.6 %unpack.15 = bf16[32,16,16,256]{3,2,1,0:T(8,128)(2,1)} custom-call(s32[32]{0:T(128)S(1)} %get-tuple-element.272.used_ref, s32[32]{0:T(128)S(1)} %sub.52.first_ref, bf16[8,44,16,256]{3,2,1,0:T(8,128)(2,1)S(1)} %all-to-all-done.5.packed_ref), custom_call_target="tpu_custom_call" | custom-call | tf_op jit(solution)/shard_map/cond/branch_5_fun/unpack/pallas_call | solution.py:205
  206.3 2.2 copy-done.3
  208.4 3.4 copy-done.18
  211.8 5.4 %fetch.1 = (bf16[8192,512]{1,0:T(8,128)(2,1)S(1)}, bf16[8192,256]{1,0:T(8,128)(2,1)S(1)}, bf16[512,8192]{1,0:T(8,128)(2,1)S(1)}, bf16[32,256,256]{2,1,0:T(8,128)(2,1)S(1)}) custom-call(bf16[8192,512]{1,0:T(8,128)(2,1)S(1)} %copy-done.18, bf16[8192,256]{1,0:T(8,128)(2,1)S(1)} %copy-done.3, bf16[512,8192]{1,0:T(8,128)(2,1)} %refs_2_.1, ...), custom_call_target="tpu_custom_call" | custom-call | tf_op jit(solution)/shard_map/fetch/pallas_call | solution.py:106
  217.3 3.3 copy-done.4
  220.6 3.3 copy-done.6
  233.7 2.2 copy-done.10
  237.7 2.1 copy-done.11
  240.9 3.4 copy-done.7
  244.3 2.2 copy-done.12
  246.5 2.2 copy-done.14
  248.7 6.9 %decode_step.4 = (bf16[8,4,8192]{2,1,0:T(4,128)(2,1)S(1)}, bf16[32,256]{1,0:T(8,128)(2,1)S(1)}) custom-call(bf16[4,8320]{1,0:T(4,128)(2,1)} %opening.1.refs_0_, bf16[4,8320]{1,0:T(4,128)(2,1)} %collective-permute-done.refs_1_, bf16[4,8320]{1,0:T(4,128)(2,1)} %collective-permute-done.1.refs_2_, bf16[4,8320]{1,0:T(4,128)(2,1)} %collective-permute-done.2.refs_3_, ...), custom_call_target="tpu_custom_call" | custom-call | flops 671088640 | bytes 25165824 | tf_op jit(solution)/shard_map/decode_step/pallas_call | solution.py:348
  255.6 18.1 %all_to_all.60.parts_ref = bf16[8,4,8192]{2,1,0:T(4,128)(2,1)S(1)} all-to-all(bf16[8,4,8192]{2,1,0:T(4,128)(2,1)S(1)} %get-tuple-element.319), channel_id=1, replica_groups=mesh['groups'=2,'tensor'=8,'section'=2] {'tensor'}, dimensions={0} | all-to-all | bytes 1048576 | tf_op jit(solution)/shard_map/all_to_all | solution.py:516
  275.6 2.0 collective-permute-start.26
  278.7 2.7 collective-permute-start.28
  282.9 2.4 collective-permute-start.30
  286.9 3.1 collective-permute-done.28.refs_5_
  290.0 6.2 %decode_step.5 = (bf16[8,4,8192]{2,1,0:T(4,128)(2,1)S(1)}, bf16[32,256]{1,0:T(8,128)(2,1)S(1)}) custom-call(bf16[4,8192]{1,0:T(4,128)(2,1)S(1)} %get-tuple-element.321.refs_0_, bf16[4,8192]{1,0:T(4,128)(2,1)S(1)} %collective-permute-done.24.refs_1_, bf16[4,8192]{1,0:T(4,128)(2,1)S(1)} %collective-permute-done.25.refs_2_, ...), custom_call_target="tpu_custom_call" | custom-call | flops 671088640 | bytes 25165824 | tf_op jit(solution)/shard_map/decode_step/pallas_call | solution.py:348
  296.2 16.1 %all_to_all.61.parts_ref = bf16[8,4,8192]{2,1,0:T(4,128)(2,1)S(1)} all-to-all(bf16[8,4,8192]{2,1,0:T(4,128)(2,1)S(1)} %get-tuple-element.323), channel_id=1, replica_groups=mesh['groups'=2,'tensor'=8,'section'=2] {'tensor'}, dimensions={0} | all-to-all | bytes 1048576 | tf_op jit(solution)/shard_map/all_to_all | solution.py:516
  317.3 2.7 collective-permute-start.35
  321.5 2.4 collective-permute-start.37
  324.8 2.2 collective-permute-done.35.refs_5_
  328.5 6.2 %decode_step.6 = (bf16[8,4,8192]{2,1,0:T(4,128)(2,1)S(1)}, bf16[32,256]{1,0:T(8,128)(2,1)S(1)}) custom-call(bf16[4,8192]{1,0:T(4,128)(2,1)S(1)} %get-tuple-element.325.refs_0_, bf16[4,8192]{1,0:T(4,128)(2,1)S(1)} %collective-permute-done.31.refs_1_, bf16[4,8192]{1,0:T(4,128)(2,1)S(1)} %collective-permute-done.32.refs_2_, ...), custom_call_target="tpu_custom_call" | custom-call | flops 671088640 | bytes 25165824 | tf_op jit(solution)/shard_map/decode_step/pallas_call | solution.py:348
  334.8 14.8 %all_to_all.62.parts_ref = bf16[8,4,8192]{2,1,0:T(4,128)(2,1)S(1)} all-to-all(bf16[8,4,8192]{2,1,0:T(4,128)(2,1)S(1)} %get-tuple-element.327), channel_id=1, replica_groups=mesh['groups'=2,'tensor'=8,'section'=2] {'tensor'}, dimensions={0} | all-to-all | bytes 1048576 | tf_op jit(solution)/shard_map/all_to_all | solution.py:516
  351.4 2.1 collective-permute-start.40
  354.5 2.7 collective-permute-start.42
  358.7 2.4 collective-permute-start.44
  363.4 2.3 collective-permute-done.44.refs_7_
  365.7 6.3 %decode_step.7 = (bf16[8,4,8192]{2,1,0:T(4,128)(2,1)S(1)}, bf16[32,256]{1,0:T(8,128)(2,1)}) custom-call(bf16[4,8192]{1,0:T(4,128)(2,1)S(1)} %get-tuple-element.329.refs_0_, bf16[4,8192]{1,0:T(4,128)(2,1)S(1)} %collective-permute-done.38.refs_1_, bf16[4,8192]{1,0:T(4,128)(2,1)S(1)} %collective-permute-done.39.refs_2_, ...), custom_call_target="tpu_custom_call" | custom-call | flops 671088640 | bytes 25165824 | tf_op jit(solution)/shard_map/decode_step/pallas_call | solution.py:348
  371.9 13.8 %all_to_all.63.parts_ref = bf16[8,4,8192]{2,1,0:T(4,128)(2,1)S(1)} all-to-all(bf16[8,4,8192]{2,1,0:T(4,128)(2,1)S(1)} %get-tuple-element.331), channel_id=1, replica_groups=mesh['groups'=2,'tensor'=8,'section'=2] {'tensor'}, dimensions={0} | all-to-all | bytes 1048576 | tf_op jit(solution)/shard_map/all_to_all | solution.py:516
  (202 shorter events, 88.7 us)
Async XLA Ops:
  3.8 28.5 %collective-permute-start.9 = (bf16[32,8192]{1,0:T(8,128)(2,1)}, bf16[32,8192]{1,0:T(8,128)(2,1)}, u32[]{:S(2)}, u32[]{:S(2)}) collective-permute-start(bf16[32,8192]{1,0:T(8,128)(2,1)} %get-tuple-element.336), channel_id=1, source_target_pairs={{0,4},{4,8},{8,12},{12,14},{14,10},{10,6},{6,2},{2,0},{1,5},{5,9},... | collective-permute-start | bytes 1572872 | tf_op jit(solution)/shard_map/ppermute | solution.py:31
  6.8 29.0 %collective-permute-start.10 = (bf16[32,8192]{1,0:T(8,128)(2,1)}, bf16[32,8192]{1,0:T(8,128)(2,1)}, u32[]{:S(2)}, u32[]{:S(2)}) collective-permute-start(bf16[32,8192]{1,0:T(8,128)(2,1)} %get-tuple-element.336), channel_id=1, source_target_pairs={{0,2},{4,0},{8,4},{12,8},{14,12},{10,14},{6,10},{2,6},{1,3},{5,1},... | collective-permute-start | bytes 1572872 | tf_op jit(solution)/shard_map/ppermute | solution.py:31
  6.8 31.4 %collective-permute-start.11 = (bf16[32,8192]{1,0:T(8,128)(2,1)}, bf16[32,8192]{1,0:T(8,128)(2,1)}, u32[]{:S(2)}, u32[]{:S(2)}) collective-permute-start(bf16[32,8192]{1,0:T(8,128)(2,1)} %get-tuple-element.335), channel_id=1, source_target_pairs={{0,4},{4,8},{8,12},{12,14},{14,10},{10,6},{6,2},{2,0},{1,5},{5,9},... | collective-permute-start | bytes 1572872 | tf_op jit(solution)/shard_map/ppermute | solution.py:31
  8.8 32.9 %collective-permute-start.12 = (bf16[32,8192]{1,0:T(8,128)(2,1)}, bf16[32,8192]{1,0:T(8,128)(2,1)S(1)}, u32[]{:S(2)}, u32[]{:S(2)}) collective-permute-start(bf16[32,8192]{1,0:T(8,128)(2,1)} %get-tuple-element.335), channel_id=1, source_target_pairs={{0,2},{4,0},{8,4},{12,8},{14,12},{10,14},{6,10},{2,6},{1,3},{5,1},... | collective-permute-start | bytes 1572872 | tf_op jit(solution)/shard_map/ppermute | solution.py:31
  9.7 15.0 %collective-permute-start.7 = (s32[1,1]{1,0:T(1,128)}, s32[1,1]{1,0:T(1,128)}, u32[]{:S(2)}, u32[]{:S(2)}) collective-permute-start(s32[1,1]{1,0:T(1,128)} %bitcast.23), channel_id=1, source_target_pairs={{0,1},{1,0},{2,3},{3,2},{4,5},{5,4},{6,7},{7,6},{8,9},{9,8},{10,11... | collective-permute-start | bytes 20 | tf_op jit(solution)/shard_map/ppermute | solution.py:445
  26.0 3.7 collective-permute-start.8
  29.7 72.6 %collective-permute-start = (bf16[4,8320]{1,0:T(4,128)(2,1)}, bf16[4,8320]{1,0:T(4,128)(2,1)}, u32[]{:S(2)}, u32[]{:S(2)}) collective-permute-start(bf16[4,8320]{1,0:T(4,128)(2,1)} %opening.1.refs_0_), channel_id=1, source_target_pairs={{0,2},{2,0},{4,6},{6,4},{8,10},{10,8},{12,14},{14,12},{1,3},{3,1},... | collective-permute-start | bytes 199688 | tf_op jit(solution)/shard_map/ppermute | solution.py:36
  32.3 71.8 %collective-permute-start.1 = (bf16[4,8320]{1,0:T(4,128)(2,1)}, bf16[4,8320]{1,0:T(4,128)(2,1)}, u32[]{:S(2)}, u32[]{:S(2)}) collective-permute-start(bf16[4,8320]{1,0:T(4,128)(2,1)} %opening.1.refs_0_), channel_id=1, source_target_pairs={{0,4},{2,6},{4,0},{6,2},{8,12},{10,14},{12,8},{14,10},{1,5},{3,7},... | collective-permute-start | bytes 199688 | tf_op jit(solution)/shard_map/ppermute | solution.py:36
  35.8 15.1 %collective-permute-start.13 = (bf16[32,8192]{1,0:T(8,128)(2,1)}, bf16[32,8192]{1,0:T(8,128)(2,1)S(1)}, u32[]{:S(2)}, u32[]{:S(2)}) collective-permute-start(bf16[32,8192]{1,0:T(8,128)(2,1)} %collective-permute-done.9), channel_id=1, source_target_pairs={{0,4},{4,8},{8,12},{12,14},{14,10},{10,6},{6,2},{2,0},{1,5},{5,9},... | collective-permute-start | bytes 1572872 | tf_op jit(solution)/shard_map/ppermute | solution.py:31
  38.2 15.8 %collective-permute-start.14 = (bf16[32,8192]{1,0:T(8,128)(2,1)}, bf16[32,8192]{1,0:T(8,128)(2,1)S(1)}, u32[]{:S(2)}, u32[]{:S(2)}) collective-permute-start(bf16[32,8192]{1,0:T(8,128)(2,1)} %collective-permute-done.10), channel_id=1, source_target_pairs={{0,2},{4,0},{8,4},{12,8},{14,12},{10,14},{6,10},{2,6},{1,3},{5,1},... | collective-permute-start | bytes 1572872 | tf_op jit(solution)/shard_map/ppermute | solution.py:31
  41.7 20.5 %collective-permute-start.15 = (bf16[32,8192]{1,0:T(8,128)(2,1)}, bf16[32,8192]{1,0:T(8,128)(2,1)S(1)}, u32[]{:S(2)}, u32[]{:S(2)}) collective-permute-start(bf16[32,8192]{1,0:T(8,128)(2,1)} %collective-permute-done.11), channel_id=1, source_target_pairs={{0,4},{4,8},{8,12},{12,14},{14,10},{10,6},{6,2},{2,0},{1,5},{5,9},... | collective-permute-start | bytes 1572872 | tf_op jit(solution)/shard_map/ppermute | solution.py:31
  50.9 14.6 %collective-permute-start.16 = (bf16[32,8192]{1,0:T(8,128)(2,1)S(1)}, bf16[32,8192]{1,0:T(8,128)(2,1)S(1)}, u32[]{:S(2)}, u32[]{:S(2)}) collective-permute-start(bf16[32,8192]{1,0:T(8,128)(2,1)S(1)} %collective-permute-done.12), channel_id=1, source_target_pairs={{0,2},{4,0},{8,4},{12,8},{14,12},{10,14},{6,10},{2,6},{1,3},{5,1},... | collective-permute-start | bytes 1572872 | tf_op jit(solution)/shard_map/ppermute | solution.py:31
  54.0 19.4 %collective-permute-start.17 = (bf16[32,8192]{1,0:T(8,128)(2,1)S(1)}, bf16[32,8192]{1,0:T(8,128)(2,1)S(1)}, u32[]{:S(2)}, u32[]{:S(2)}) collective-permute-start(bf16[32,8192]{1,0:T(8,128)(2,1)S(1)} %collective-permute-done.13), channel_id=1, source_target_pairs={{0,4},{4,8},{8,12},{12,14},{14,10},{10,6},{6,2},{2,0},{1,5},{5,9},... | collective-permute-start | bytes 1572872 | tf_op jit(solution)/shard_map/ppermute | solution.py:31
  62.2 14.6 %collective-permute-start.18 = (bf16[32,8192]{1,0:T(8,128)(2,1)S(1)}, bf16[32,8192]{1,0:T(8,128)(2,1)S(1)}, u32[]{:S(2)}, u32[]{:S(2)}) collective-permute-start(bf16[32,8192]{1,0:T(8,128)(2,1)S(1)} %collective-permute-done.14), channel_id=1, source_target_pairs={{0,2},{4,0},{8,4},{12,8},{14,12},{10,14},{6,10},{2,6},{1,3},{5,1},... | collective-permute-start | bytes 1572872 | tf_op jit(solution)/shard_map/ppermute | solution.py:31
  65.5 17.9 %collective-permute-start.19 = (bf16[32,8192]{1,0:T(8,128)(2,1)S(1)}, bf16[32,8192]{1,0:T(8,128)(2,1)S(1)}, u32[]{:S(2)}, u32[]{:S(2)}) collective-permute-start(bf16[32,8192]{1,0:T(8,128)(2,1)S(1)} %collective-permute-done.15), channel_id=1, source_target_pairs={{0,4},{4,8},{8,12},{12,14},{14,10},{10,6},{6,2},{2,0},{1,5},{5,9},... | collective-permute-start | bytes 1572872 | tf_op jit(solution)/shard_map/ppermute | solution.py:31
  73.4 13.1 %collective-permute-start.20 = (bf16[32,8192]{1,0:T(8,128)(2,1)S(1)}, bf16[32,8192]{1,0:T(8,128)(2,1)S(1)}, u32[]{:S(2)}, u32[]{:S(2)}) collective-permute-start(bf16[32,8192]{1,0:T(8,128)(2,1)S(1)} %collective-permute-done.16), channel_id=1, source_target_pairs={{0,2},{4,0},{8,4},{12,8},{14,12},{10,14},{6,10},{2,6},{1,3},{5,1},... | collective-permute-start | bytes 1572872 | tf_op jit(solution)/shard_map/ppermute | solution.py:31
  76.8 31.8 %collective-permute-start.2 = (bf16[4,8320]{1,0:T(4,128)(2,1)}, bf16[4,8320]{1,0:T(4,128)(2,1)}, u32[]{:S(2)}, u32[]{:S(2)}) collective-permute-start(bf16[4,8320]{1,0:T(4,128)(2,1)} %opening.1.refs_0_), channel_id=1, source_target_pairs={{0,6},{2,4},{4,2},{6,0},{8,14},{10,12},{12,10},{14,8},{1,7},{3,5},... | collective-permute-start | bytes 199688 | tf_op jit(solution)/shard_map/ppermute | solution.py:36
  83.4 11.9 %collective-permute-start.21 = (bf16[32,8192]{1,0:T(8,128)(2,1)S(1)}, bf16[32,8192]{1,0:T(8,128)(2,1)S(1)}, u32[]{:S(2)}, u32[]{:S(2)}) collective-permute-start(bf16[32,8192]{1,0:T(8,128)(2,1)S(1)} %collective-permute-done.17), channel_id=1, source_target_pairs={{0,4},{4,8},{8,12},{12,14},{14,10},{10,6},{6,2},{2,0},{1,5},{5,9},... | collective-permute-start | bytes 1572872 | tf_op jit(solution)/shard_map/ppermute | solution.py:31
  86.5 12.7 %collective-permute-start.22 = (bf16[32,8192]{1,0:T(8,128)(2,1)S(1)}, bf16[32,8192]{1,0:T(8,128)(2,1)S(1)}, u32[]{:S(2)}, u32[]{:S(2)}) collective-permute-start(bf16[32,8192]{1,0:T(8,128)(2,1)S(1)} %collective-permute-done.20), channel_id=1, source_target_pairs={{0,2},{4,0},{8,4},{12,8},{14,12},{10,14},{6,10},{2,6},{1,3},{5,1},... | collective-permute-start | bytes 1572872 | tf_op jit(solution)/shard_map/ppermute | solution.py:31
  95.3 134.5 %collective-permute-start.3 = (bf16[4,8320]{1,0:T(4,128)(2,1)}, bf16[4,8320]{1,0:T(4,128)(2,1)}, u32[]{:S(2)}, u32[]{:S(2)}) collective-permute-start(bf16[4,8320]{1,0:T(4,128)(2,1)} %opening.1.refs_0_), channel_id=1, source_target_pairs={{0,8},{2,10},{4,12},{6,14},{8,0},{10,2},{12,4},{14,6},{1,9},{3,11}... | collective-permute-start | bytes 199688 | tf_op jit(solution)/shard_map/ppermute | solution.py:36
  99.1 131.4 %collective-permute-start.4 = (bf16[4,8320]{1,0:T(4,128)(2,1)}, bf16[4,8320]{1,0:T(4,128)(2,1)}, u32[]{:S(2)}, u32[]{:S(2)}) collective-permute-start(bf16[4,8320]{1,0:T(4,128)(2,1)} %opening.1.refs_0_), channel_id=1, source_target_pairs={{0,10},{2,8},{4,14},{6,12},{8,2},{10,0},{12,6},{14,4},{1,11},{3,9}... | collective-permute-start | bytes 199688 | tf_op jit(solution)/shard_map/ppermute | solution.py:36
  102.3 128.9 %collective-permute-start.5 = (bf16[4,8320]{1,0:T(4,128)(2,1)}, bf16[4,8320]{1,0:T(4,128)(2,1)}, u32[]{:S(2)}, u32[]{:S(2)}) collective-permute-start(bf16[4,8320]{1,0:T(4,128)(2,1)} %opening.1.refs_0_), channel_id=1, source_target_pairs={{0,12},{2,14},{4,8},{6,10},{8,4},{10,6},{12,0},{14,2},{1,13},{3,15... | collective-permute-start | bytes 199688 | tf_op jit(solution)/shard_map/ppermute | solution.py:36
  104.1 127.7 %collective-permute-start.6 = (bf16[4,8320]{1,0:T(4,128)(2,1)}, bf16[4,8320]{1,0:T(4,128)(2,1)}, u32[]{:S(2)}, u32[]{:S(2)}) collective-permute-start(bf16[4,8320]{1,0:T(4,128)(2,1)} %opening.1.refs_0_), channel_id=1, source_target_pairs={{0,14},{2,12},{4,10},{6,8},{8,6},{10,4},{12,2},{14,0},{1,15},{3,13... | collective-permute-start | bytes 199688 | tf_op jit(solution)/shard_map/ppermute | solution.py:36
  108.6 125.1 %collective-permute-start.23 = (bf16[512,256]{1,0:T(8,128)(2,1)}, bf16[512,256]{1,0:T(8,128)(2,1)}, u32[]{:S(2)}, u32[]{:S(2)}) collective-permute-start(bf16[512,256]{1,0:T(8,128)(2,1)} %pad_maximum_fusion), channel_id=1, source_target_pairs={{0,1},{1,0},{2,3},{3,2},{4,5},{5,4},{6,7},{7,6},{8,9},{9,8},{10,11... | collective-permute-start | bytes 786440 | tf_op jit(solution)/shard_map/ppermute | solution.py:492
  123.8 70.5 %all-to-all-start.5 = ((bf16[8,44,16,256]{3,2,1,0:T(8,128)(2,1)}), bf16[8,44,16,256]{3,2,1,0:T(8,128)(2,1)S(1)}, u32[]{:S(2)}, u32[]{:S(2)}) async-start(bf16[8,44,16,256]{3,2,1,0:T(8,128)(2,1)} %parcels.15), calls=%async_computation.5 | async-start | bytes 5767168 | tf_op jit(solution)/shard_map/cond/branch_5_fun/all_to_all | solution.py:453
  248.7 25.0 %copy-start.24 = (bf16[1,4,8192]{2,1,0:T(4,128)(2,1)S(1)}, bf16[1,4,8192]{2,1,0:T(4,128)(2,1)}, u32[]{:S(2)}) copy-start(bf16[1,4,8192]{2,1,0:T(4,128)(2,1)} %param.27) | copy-start | bytes 196612
  248.7 41.3 %copy-start.8 = (bf16[512,8192]{1,0:T(8,128)(2,1)S(1)}, bf16[512,8192]{1,0:T(8,128)(2,1)}, u32[]{:S(2)}) copy-start(bf16[512,8192]{1,0:T(8,128)(2,1)} %copy-done.6) | copy-start | bytes 25165828
  274.0 7.4 %collective-permute-start.24 = (bf16[4,8192]{1,0:T(4,128)(2,1)S(1)}, bf16[4,8192]{1,0:T(4,128)(2,1)S(1)}, u32[]{:S(2)}, u32[]{:S(2)}) collective-permute-start(bf16[4,8192]{1,0:T(4,128)(2,1)S(1)} %get-tuple-element.321.refs_0_), channel_id=1, source_target_pairs={{0,2},{2,0},{4,6},{6,4},{8,10},{10,8},{12,14},{14,12},{1,3},{3,1},... | collective-permute-start | bytes 196616 | tf_op jit(solution)/shard_map/ppermute | solution.py:36
  275.6 7.3 %collective-permute-start.25 = (bf16[4,8192]{1,0:T(4,128)(2,1)S(1)}, bf16[4,8192]{1,0:T(4,128)(2,1)S(1)}, u32[]{:S(2)}, u32[]{:S(2)}) collective-permute-start(bf16[4,8192]{1,0:T(4,128)(2,1)S(1)} %get-tuple-element.321.refs_0_), channel_id=1, source_target_pairs={{0,4},{2,6},{4,0},{6,2},{8,12},{10,14},{12,8},{14,10},{1,5},{3,7},... | collective-permute-start | bytes 196616 | tf_op jit(solution)/shard_map/ppermute | solution.py:36
  275.6 9.7 %collective-permute-start.26 = (bf16[4,8192]{1,0:T(4,128)(2,1)S(1)}, bf16[4,8192]{1,0:T(4,128)(2,1)S(1)}, u32[]{:S(2)}, u32[]{:S(2)}) collective-permute-start(bf16[4,8192]{1,0:T(4,128)(2,1)S(1)} %get-tuple-element.321.refs_0_), channel_id=1, source_target_pairs={{0,6},{2,4},{4,2},{6,0},{8,14},{10,12},{12,10},{14,8},{1,7},{3,5},... | collective-permute-start | bytes 196616 | tf_op jit(solution)/shard_map/ppermute | solution.py:36
  277.6 9.3 %collective-permute-start.27 = (bf16[4,8192]{1,0:T(4,128)(2,1)S(1)}, bf16[4,8192]{1,0:T(4,128)(2,1)S(1)}, u32[]{:S(2)}, u32[]{:S(2)}) collective-permute-start(bf16[4,8192]{1,0:T(4,128)(2,1)S(1)} %get-tuple-element.321.refs_0_), channel_id=1, source_target_pairs={{0,8},{2,10},{4,12},{6,14},{8,0},{10,2},{12,4},{14,6},{1,9},{3,11}... | collective-permute-start | bytes 196616 | tf_op jit(solution)/shard_map/ppermute | solution.py:36
  278.7 11.3 %collective-permute-start.28 = (bf16[4,8192]{1,0:T(4,128)(2,1)S(1)}, bf16[4,8192]{1,0:T(4,128)(2,1)S(1)}, u32[]{:S(2)}, u32[]{:S(2)}) collective-permute-start(bf16[4,8192]{1,0:T(4,128)(2,1)S(1)} %get-tuple-element.321.refs_0_), channel_id=1, source_target_pairs={{0,10},{2,8},{4,14},{6,12},{8,2},{10,0},{12,6},{14,4},{1,11},{3,9}... | collective-permute-start | bytes 196616 | tf_op jit(solution)/shard_map/ppermute | solution.py:36
  281.4 8.5 %collective-permute-start.29 = (bf16[4,8192]{1,0:T(4,128)(2,1)S(1)}, bf16[4,8192]{1,0:T(4,128)(2,1)S(1)}, u32[]{:S(2)}, u32[]{:S(2)}) collective-permute-start(bf16[4,8192]{1,0:T(4,128)(2,1)S(1)} %get-tuple-element.321.refs_0_), channel_id=1, source_target_pairs={{0,12},{2,14},{4,8},{6,10},{8,4},{10,6},{12,0},{14,2},{1,13},{3,15... | collective-permute-start | bytes 196616 | tf_op jit(solution)/shard_map/ppermute | solution.py:36
  282.9 7.1 %collective-permute-start.30 = (bf16[4,8192]{1,0:T(4,128)(2,1)S(1)}, bf16[4,8192]{1,0:T(4,128)(2,1)S(1)}, u32[]{:S(2)}, u32[]{:S(2)}) collective-permute-start(bf16[4,8192]{1,0:T(4,128)(2,1)S(1)} %get-tuple-element.321.refs_0_), channel_id=1, source_target_pairs={{0,14},{2,12},{4,10},{6,8},{8,6},{10,4},{12,2},{14,0},{1,15},{3,13... | collective-permute-start | bytes 196616 | tf_op jit(solution)/shard_map/ppermute | solution.py:36
  312.6 7.4 %collective-permute-start.31 = (bf16[4,8192]{1,0:T(4,128)(2,1)S(1)}, bf16[4,8192]{1,0:T(4,128)(2,1)S(1)}, u32[]{:S(2)}, u32[]{:S(2)}) collective-permute-start(bf16[4,8192]{1,0:T(4,128)(2,1)S(1)} %get-tuple-element.325.refs_0_), channel_id=1, source_target_pairs={{0,2},{2,0},{4,6},{6,4},{8,10},{10,8},{12,14},{14,12},{1,3},{3,1},... | collective-permute-start | bytes 196616 | tf_op jit(solution)/shard_map/ppermute | solution.py:36
  314.1 7.3 %collective-permute-start.32 = (bf16[4,8192]{1,0:T(4,128)(2,1)S(1)}, bf16[4,8192]{1,0:T(4,128)(2,1)S(1)}, u32[]{:S(2)}, u32[]{:S(2)}) collective-permute-start(bf16[4,8192]{1,0:T(4,128)(2,1)S(1)} %get-tuple-element.325.refs_0_), channel_id=1, source_target_pairs={{0,4},{2,6},{4,0},{6,2},{8,12},{10,14},{12,8},{14,10},{1,5},{3,7},... | collective-permute-start | bytes 196616 | tf_op jit(solution)/shard_map/ppermute | solution.py:36
  314.1 9.7 %collective-permute-start.33 = (bf16[4,8192]{1,0:T(4,128)(2,1)S(1)}, bf16[4,8192]{1,0:T(4,128)(2,1)S(1)}, u32[]{:S(2)}, u32[]{:S(2)}) collective-permute-start(bf16[4,8192]{1,0:T(4,128)(2,1)S(1)} %get-tuple-element.325.refs_0_), channel_id=1, source_target_pairs={{0,6},{2,4},{4,2},{6,0},{8,14},{10,12},{12,10},{14,8},{1,7},{3,5},... | collective-permute-start | bytes 196616 | tf_op jit(solution)/shard_map/ppermute | solution.py:36
  316.2 8.7 %collective-permute-start.34 = (bf16[4,8192]{1,0:T(4,128)(2,1)S(1)}, bf16[4,8192]{1,0:T(4,128)(2,1)S(1)}, u32[]{:S(2)}, u32[]{:S(2)}) collective-permute-start(bf16[4,8192]{1,0:T(4,128)(2,1)S(1)} %get-tuple-element.325.refs_0_), channel_id=1, source_target_pairs={{0,8},{2,10},{4,12},{6,14},{8,0},{10,2},{12,4},{14,6},{1,9},{3,11}... | collective-permute-start | bytes 196616 | tf_op jit(solution)/shard_map/ppermute | solution.py:36
  317.3 9.8 %collective-permute-start.35 = (bf16[4,8192]{1,0:T(4,128)(2,1)S(1)}, bf16[4,8192]{1,0:T(4,128)(2,1)S(1)}, u32[]{:S(2)}, u32[]{:S(2)}) collective-permute-start(bf16[4,8192]{1,0:T(4,128)(2,1)S(1)} %get-tuple-element.325.refs_0_), channel_id=1, source_target_pairs={{0,10},{2,8},{4,14},{6,12},{8,2},{10,0},{12,6},{14,4},{1,11},{3,9}... | collective-permute-start | bytes 196616 | tf_op jit(solution)/shard_map/ppermute | solution.py:36
  320.0 7.1 %collective-permute-start.36 = (bf16[4,8192]{1,0:T(4,128)(2,1)S(1)}, bf16[4,8192]{1,0:T(4,128)(2,1)S(1)}, u32[]{:S(2)}, u32[]{:S(2)}) collective-permute-start(bf16[4,8192]{1,0:T(4,128)(2,1)S(1)} %get-tuple-element.325.refs_0_), channel_id=1, source_target_pairs={{0,12},{2,14},{4,8},{6,10},{8,4},{10,6},{12,0},{14,2},{1,13},{3,15... | collective-permute-start | bytes 196616 | tf_op jit(solution)/shard_map/ppermute | solution.py:36
  321.5 7.1 %collective-permute-start.37 = (bf16[4,8192]{1,0:T(4,128)(2,1)S(1)}, bf16[4,8192]{1,0:T(4,128)(2,1)S(1)}, u32[]{:S(2)}, u32[]{:S(2)}) collective-permute-start(bf16[4,8192]{1,0:T(4,128)(2,1)S(1)} %get-tuple-element.325.refs_0_), channel_id=1, source_target_pairs={{0,14},{2,12},{4,10},{6,8},{8,6},{10,4},{12,2},{14,0},{1,15},{3,13... | collective-permute-start | bytes 196616 | tf_op jit(solution)/shard_map/ppermute | solution.py:36
  349.9 7.3 %collective-permute-start.38 = (bf16[4,8192]{1,0:T(4,128)(2,1)S(1)}, bf16[4,8192]{1,0:T(4,128)(2,1)S(1)}, u32[]{:S(2)}, u32[]{:S(2)}) collective-permute-start(bf16[4,8192]{1,0:T(4,128)(2,1)S(1)} %get-tuple-element.329.refs_0_), channel_id=1, source_target_pairs={{0,2},{2,0},{4,6},{6,4},{8,10},{10,8},{12,14},{14,12},{1,3},{3,1},... | collective-permute-start | bytes 196616 | tf_op jit(solution)/shard_map/ppermute | solution.py:36
  351.4 7.3 %collective-permute-start.39 = (bf16[4,8192]{1,0:T(4,128)(2,1)S(1)}, bf16[4,8192]{1,0:T(4,128)(2,1)S(1)}, u32[]{:S(2)}, u32[]{:S(2)}) collective-permute-start(bf16[4,8192]{1,0:T(4,128)(2,1)S(1)} %get-tuple-element.329.refs_0_), channel_id=1, source_target_pairs={{0,4},{2,6},{4,0},{6,2},{8,12},{10,14},{12,8},{14,10},{1,5},{3,7},... | collective-permute-start | bytes 196616 | tf_op jit(solution)/shard_map/ppermute | solution.py:36
  351.4 9.7 %collective-permute-start.40 = (bf16[4,8192]{1,0:T(4,128)(2,1)S(1)}, bf16[4,8192]{1,0:T(4,128)(2,1)S(1)}, u32[]{:S(2)}, u32[]{:S(2)}) collective-permute-start(bf16[4,8192]{1,0:T(4,128)(2,1)S(1)} %get-tuple-element.329.refs_0_), channel_id=1, source_target_pairs={{0,6},{2,4},{4,2},{6,0},{8,14},{10,12},{12,10},{14,8},{1,7},{3,5},... | collective-permute-start | bytes 196616 | tf_op jit(solution)/shard_map/ppermute | solution.py:36
  353.4 7.9 %collective-permute-start.41 = (bf16[4,8192]{1,0:T(4,128)(2,1)S(1)}, bf16[4,8192]{1,0:T(4,128)(2,1)S(1)}, u32[]{:S(2)}, u32[]{:S(2)}) collective-permute-start(bf16[4,8192]{1,0:T(4,128)(2,1)S(1)} %get-tuple-element.329.refs_0_), channel_id=1, source_target_pairs={{0,8},{2,10},{4,12},{6,14},{8,0},{10,2},{12,4},{14,6},{1,9},{3,11}... | collective-permute-start | bytes 196616 | tf_op jit(solution)/shard_map/ppermute | solution.py:36
  354.5 7.8 %collective-permute-start.42 = (bf16[4,8192]{1,0:T(4,128)(2,1)S(1)}, bf16[4,8192]{1,0:T(4,128)(2,1)S(1)}, u32[]{:S(2)}, u32[]{:S(2)}) collective-permute-start(bf16[4,8192]{1,0:T(4,128)(2,1)S(1)} %get-tuple-element.329.refs_0_), channel_id=1, source_target_pairs={{0,10},{2,8},{4,14},{6,12},{8,2},{10,0},{12,6},{14,4},{1,11},{3,9}... | collective-permute-start | bytes 196616 | tf_op jit(solution)/shard_map/ppermute | solution.py:36
  357.2 6.2 %collective-permute-start.43 = (bf16[4,8192]{1,0:T(4,128)(2,1)S(1)}, bf16[4,8192]{1,0:T(4,128)(2,1)S(1)}, u32[]{:S(2)}, u32[]{:S(2)}) collective-permute-start(bf16[4,8192]{1,0:T(4,128)(2,1)S(1)} %get-tuple-element.329.refs_0_), channel_id=1, source_target_pairs={{0,12},{2,14},{4,8},{6,10},{8,4},{10,6},{12,0},{14,2},{1,13},{3,15... | collective-permute-start | bytes 196616 | tf_op jit(solution)/shard_map/ppermute | solution.py:36
  358.7 7.0 %collective-permute-start.44 = (bf16[4,8192]{1,0:T(4,128)(2,1)S(1)}, bf16[4,8192]{1,0:T(4,128)(2,1)S(1)}, u32[]{:S(2)}, u32[]{:S(2)}) collective-permute-start(bf16[4,8192]{1,0:T(4,128)(2,1)S(1)} %get-tuple-element.329.refs_0_), channel_id=1, source_target_pairs={{0,14},{2,12},{4,10},{6,8},{8,6},{10,4},{12,2},{14,0},{1,15},{3,13... | collective-permute-start | bytes 196616 | tf_op jit(solution)/shard_map/ppermute | solution.py:36
  (34 other events, 379.0 us)

commit v4 on v2

v4 whole, which is shorter than its diff:
```python
import functools

import jax
import jax.numpy as jnp
from jax import lax
from jax.experimental import pallas as pl
from jax.experimental.pallas import tpu as pltpu
from jax.sharding import PartitionSpec as P

HD = 128
PLEN = 128
STEPS = 4
EPS = 1e-05
ROPE_BASE = 500000.0
LANES = 8
CHUNKS = 8
VMEM_LIMIT = 16 * 1024 * 1024


def ring_shift(value, steps):
    count = lax.axis_size("tensor")
    return lax.ppermute(value, "tensor", [(s, (s + steps) % count) for s in range(count)])


def swap_xor(value, mask):
    count = lax.axis_size("tensor")
    return lax.ppermute(value, "tensor", [(s, s ^ mask) for s in range(count)])


def along_ring(pieces, opened, gate):
    count = lax.axis_size("tensor")
    rank = lax.axis_index("tensor")
    arrivals = [(rank, piece, rows) for piece, rows in enumerate(pieces)]
    going = [[rows, rows] for rows in pieces]
    middle = None
    for hop in range(1, count // 2 + 1):
        for piece in range(2):
            for way in range(2):
                if hop == count // 2 and piece != way:
                    continue
                sign = 1 if way == 0 else -1
                going[piece][way] = ring_shift(going[piece][way], sign)
                arrivals.append(((rank - sign * hop) % count, piece, going[piece][way]))
        if hop == 1:
            going, opened, gate = lax.optimization_barrier((going, opened, gate))
        if hop == count // 4:
            middle = going[1][1]
    return arrivals, opened, gate, middle


def along_grid(pieces, opened, gate):
    rank = lax.axis_index("tensor")
    z, y = rank // 2, rank % 2

    def shift(rows, steps, starts):
        pairs = [(2 * s + c, 2 * (s + steps) + c) for s in starts for c in range(2)]
        return lax.ppermute(rows, "tensor", pairs)

    def cross(rows):
        return lax.ppermute(rows, "tensor", [(r, r ^ 1) for r in range(8)])

    def pick(*rows):
        return jnp.where(z == 0, rows[0], jnp.where(z == 1, rows[1], jnp.where(z == 2, rows[2], rows[3])))

    origin = [z, z ^ 1, jnp.where(z < 2, 2, 1), jnp.where(z < 2, 3, 0)]
    state = []
    for rows in pieces:
        state.append((rows, shift(rows, 1, (0, 1, 2)), shift(rows, -1, (1, 2, 3)), cross(rows)))
    state, opened, gate = lax.optimization_barrier((state, opened, gate))
    arrivals = []
    middle = None
    for piece, (rows, up, down, crossed) in enumerate(state):
        second = pick(down, up, down, up)
        up2, down2, crossed2 = lax.optimization_barrier(
            (shift(up, 1, (1, 2)), shift(down, -1, (1, 2)), cross(second))
        )
        middle = up2
        third = pick(down2, down, up, up2)
        up3, down3, crossed3 = lax.optimization_barrier(
            (shift(up2, 1, (2,)), shift(down2, -1, (1,)), cross(third))
        )
        fourth = pick(down3, down2, up2, up3)
        crossed4 = cross(fourth)
        straight = (rows, second, third, fourth)
        for source, block in zip(origin, straight):
            arrivals.append((2 * source + y, piece, block))
        for source, block in zip(origin, (crossed, crossed2, crossed3, crossed4)):
            arrivals.append((2 * source + 1 - y, piece, block))
    return arrivals, opened, gate, middle


def rope_tables(positions):
    half_dim = HD // 2
    freqs = ROPE_BASE ** (-(jnp.arange(half_dim, dtype=jnp.float32) * 2.0 / HD))
    angles = positions.astype(jnp.float32)[:, None] * freqs[None, :]
    cosine = jnp.cos(angles)
    sine = jnp.sin(angles)
    return (
        jnp.concatenate([cosine, cosine], axis=1),
        jnp.concatenate([-sine, sine], axis=1),
    )


def whole():
    return pl.BlockSpec(memory_space=pltpu.VMEM)


def normed_rows(values, gain):
    square = jnp.mean(values * values, axis=-1, keepdims=True)
    return values * lax.rsqrt(square + EPS) * gain


def normalize_kernel(rows_ref, gain_ref, out_ref):
    gain = gain_ref[...].astype(jnp.float32)
    out_ref[...] = normed_rows(rows_ref[...].astype(jnp.float32), gain).astype(jnp.bfloat16)


def normalize(rows, gain):
    return pl.pallas_call(
        normalize_kernel,
        out_shape=jax.ShapeDtypeStruct(rows.shape, jnp.bfloat16),
        in_specs=[whole()] * 2,
        out_specs=whole(),
        compiler_params=pltpu.CompilerParams(vmem_limit_bytes=VMEM_LIMIT),
        name="normalize",
    )(rows, gain)


def opening_kernel(rows_ref, gain_ref, pages_ref, out_ref):
    width = rows_ref.shape[1]
    gain = gain_ref[...].astype(jnp.float32)
    out_ref[:, :width] = normed_rows(rows_ref[...].astype(jnp.float32), gain).astype(jnp.bfloat16)
    out_ref[:, width:] = pages_ref[...]


def opening(rows, gain, pages):
    shape = (rows.shape[0], rows.shape[1] + pages.shape[1])
    return pl.pallas_call(
        opening_kernel,
        out_shape=jax.ShapeDtypeStruct(shape, jnp.bfloat16),
        in_specs=[whole()] * 3,
        out_specs=whole(),
        compiler_params=pltpu.CompilerParams(vmem_limit_bytes=VMEM_LIMIT),
        name="opening",
    )(rows, gain, pages)


def parcels_kernel(heads, table_ref, pool_ref, out_ref, held, load_sem, store_sem):
    width = out_ref.shape[-1]
    each, per_request = table_ref.shape
    loads = []
    for r in range(each):
        for p in range(per_request):
            index = r * per_request + p
            copy = pltpu.make_async_copy(
                pool_ref.at[table_ref[r, p]], held.at[index], load_sem.at[index]
            )
            copy.start()
            loads.append(copy)
    for copy in loads:
        copy.wait()
    stores = []
    for target, head in enumerate(heads):
        copy = pltpu.make_async_copy(
            held.at[:, :, pl.ds(head * width, width)], out_ref.at[target], store_sem.at[target]
        )
        copy.start()
        stores.append(copy)
    for copy in stores:
        copy.wait()


def make_parcels(table, pool, heads, width):
    pages, rows, _ = pool.shape
    hbm = pl.BlockSpec(memory_space=pltpu.HBM)
    return pl.pallas_call(
        functools.partial(parcels_kernel, heads),
        out_shape=pltpu.HBM((len(heads), pages, rows, width), jnp.bfloat16),
        in_specs=[pl.BlockSpec(memory_space=pltpu.SMEM), hbm],
        out_specs=hbm,
        scratch_shapes=[
            pltpu.VMEM(pool.shape, jnp.bfloat16),
            pltpu.SemaphoreType.DMA((pages,)),
            pltpu.SemaphoreType.DMA((len(heads),)),
        ],
        compiler_params=pltpu.CompilerParams(vmem_limit_bytes=VMEM_LIMIT),
        name="parcels",
    )(table, pool)


def turn(values, cosine, sine):
    return values * cosine + pltpu.roll(values, HD // 2, 1) * sine


def step_kernel(blocks, iteration, *refs):
    x_refs = refs[:blocks]
    order_ref, lens_ref, cos_ref, sin_ref = refs[blocks : blocks + 4]
    new_refs = refs[blocks + 4 : blocks + 4 + iteration]
    refs = refs[blocks + 4 + iteration :]
    if iteration == 0:
        request_ref, offset_ref, arrived_ref, wq_in, wkv_in, wo_in, cache_in = refs[:7]
        out_ref, fresh_ref, wq, wkv, wo, cache = refs[7:13]
        x_rows, q_s, score_s, mix_s, new_s, sems = refs[13:]
    else:
        wq, wkv, wo, cache = refs[:4]
        out_ref, fresh_ref, x_rows, q_s, score_s, mix_s, new_s = refs[4:]
    width, q_cols = wq.shape
    count, span = cache.shape[:2]
    each = count // out_ref.shape[0]
    heads = q_cols // HD
    depth = width // CHUNKS

    waits = {}
    if iteration == 0:
        for c in range(CHUNKS):
            part = pl.ds(c * depth, depth)
            waits[c] = [
                pltpu.make_async_copy(wq_in.at[part, :], wq.at[part, :], sems.at[0, c]),
                pltpu.make_async_copy(wkv_in.at[part, :], wkv.at[part, :], sems.at[1, c]),
            ]
            waits["out", c] = [pltpu.make_async_copy(wo_in.at[:, part], wo.at[:, part], sems.at[2, c])]
        waits["cache"] = [pltpu.make_async_copy(cache_in, cache, sems.at[3, 0])]
        for name in [0, 1, 2, 3, "cache", 4, 5, 6, 7] + [("out", c) for c in range(CHUNKS)]:
            for copy in waits[name]:
                copy.start()

    def wait(name):
        for copy in waits.get(name, ()):
            copy.wait()

    def patch(action):
        pieces = offset_ref.shape[0]
        rows = arrived_ref.shape[0] // pieces
        for piece in range(pieces):
            offset = pl.multiple_of(offset_ref[piece], rows)
            copy = pltpu.make_async_copy(
                arrived_ref.at[pl.ds(piece * rows, rows), :],
                cache.at[request_ref[piece], pl.ds(offset, rows), :],
                sems.at[4 + piece // CHUNKS, piece % CHUNKS],
            )
            action(copy)

    for k in range(blocks):
        x_rows[k * each : (k + 1) * each, :] = x_refs[k][:, :width].astype(jnp.float32)
    order = order_ref[...]

    query = jnp.zeros((count, q_cols), jnp.float32)
    keyvalue = jnp.zeros((count, 2 * HD), jnp.float32)
    for c in range(CHUNKS):
        part = slice(c * depth, (c + 1) * depth)
        x = jnp.dot(
            order, x_rows[:, part].astype(jnp.bfloat16), preferred_element_type=jnp.float32
        ).astype(jnp.bfloat16)
        wait(c)
        query += jnp.dot(x, wq[part, :], preferred_element_type=jnp.float32)
        keyvalue += jnp.dot(x, wkv[part, :], preferred_element_type=jnp.float32)
        if iteration == 0 and c == CHUNKS - 2:
            wait("cache")
            patch(lambda copy: copy.start())

    cosine = cos_ref[iteration]
    sine = sin_ref[iteration]
    key = turn(keyvalue[:, :HD], cosine, sine).astype(jnp.bfloat16)
    value = keyvalue[:, HD:].astype(jnp.bfloat16)
    fresh_ref[:, :HD] = key
    fresh_ref[:, HD:] = value
    news = [(ref[:, :HD], ref[:, HD:]) for ref in new_refs] + [(key, value)]
    for j in range(LANES):
        lane = pl.ds(j, count, LANES)
        if j < heads:
            turned = turn(query[:, j * HD : (j + 1) * HD], cosine, sine).astype(jnp.bfloat16)
            q_s[lane, :] = turned.astype(jnp.float32)
        else:
            q_s[lane, :] = jnp.zeros((count, HD), jnp.float32)
        for t, pair in enumerate(news):
            for half in range(2):
                new_s[t, half, lane, :] = pair[half].astype(jnp.float32)

    if iteration == 0:
        patch(lambda copy: copy.wait())
    scale = HD**-0.5
    column = lax.broadcasted_iota(jnp.int32, (LANES, span), 1)
    for r in range(count):
        rows = slice(r * LANES, (r + 1) * LANES)
        found = lax.dot_general(
            q_s[rows, :].astype(jnp.bfloat16),
            cache[r, :, :HD],
            (((1,), (1,)), ((), ())),
            preferred_element_type=jnp.float32,
        )
        score_s[rows, :] = jnp.where(column < lens_ref[r], found * scale, -1e30)

    scores = score_s[...]
    queries = q_s[...]
    fresh_scores = [
        jnp.sum(queries * new_s[t, 0], axis=-1, keepdims=True) * scale for t in range(iteration + 1)
    ]
    top = jnp.max(scores, axis=-1, keepdims=True)
    for s in fresh_scores:
        top = jnp.maximum(top, s)
    weights = jnp.exp(scores - top)
    fresh_weights = [jnp.exp(s - top) for s in fresh_scores]
    total = jnp.sum(weights, axis=-1, keepdims=True)
    for w in fresh_weights:
        total = total + w
    score_s[...] = weights / total
    row = lax.broadcasted_iota(jnp.int32, (span, HD), 0)
    for r in range(count):
        rows = slice(r * LANES, (r + 1) * LANES)
        mix_s[rows, :] = jnp.dot(
            score_s[rows, :].astype(jnp.bfloat16),
            jnp.where(row < lens_ref[r], cache[r, :, HD:], jnp.zeros((), jnp.bfloat16)),
            preferred_element_type=jnp.float32,
        )
    mixed = mix_s[...]
    for t in range(iteration + 1):
        weight = (fresh_weights[t] / total).astype(jnp.bfloat16).astype(jnp.float32)
        mixed = mixed + weight * new_s[t, 1]
    mix_s[...] = mixed
    columns = jnp.concatenate(
        [mix_s[pl.ds(j, count, LANES), :].astype(jnp.bfloat16) for j in range(heads)], axis=1
    )
    for c in range(CHUNKS):
        part = slice(c * depth, (c + 1) * depth)
        wait(("out", c))
        product = jnp.dot(columns, wo[:, part], preferred_element_type=jnp.float32)
        for d in range(count // each):
            out_ref[d, :, part] = product[d * each : (d + 1) * each, :].astype(jnp.bfloat16)


def step(x_blocks, order, lengths, cosine, sine, earlier, held, owners, prompts=()):
    width, q_cols = held[0].shape
    count, span = held[3].shape[:2]
    each = count // owners
    iteration = len(earlier)
    blocks = len(x_blocks)
    smem = pl.BlockSpec(memory_space=pltpu.SMEM)
    hbm = pl.BlockSpec(memory_space=pltpu.HBM)
    out_shape = [
        jax.ShapeDtypeStruct((owners, each, width), jnp.bfloat16),
        jax.ShapeDtypeStruct((count, 2 * HD), jnp.bfloat16),
    ]
    in_specs = [whole()] * (blocks + 1) + [smem] + [whole()] * (2 + iteration)
    scratch = [
        pltpu.VMEM((count, width), jnp.float32),
        pltpu.VMEM((count * LANES, HD), jnp.float32),
        pltpu.VMEM((count * LANES, span), jnp.float32),
        pltpu.VMEM((count * LANES, HD), jnp.float32),
        pltpu.VMEM((iteration + 1, 2, count * LANES, HD), jnp.float32),
    ]
    if iteration == 0:
        in_specs += [smem, smem, whole()] + [hbm] * 4
        out_shape += [pltpu.VMEM(a.shape, a.dtype) for a in held]
        banks = -(-prompts[1].shape[0] // CHUNKS)
        scratch.append(pltpu.SemaphoreType.DMA((4 + banks, CHUNKS)))
    else:
        in_specs += [whole()] * 4
    return pl.pallas_call(
        functools.partial(step_kernel, blocks, iteration),
        out_shape=tuple(out_shape),
        in_specs=in_specs,
        out_specs=tuple(whole() for _ in out_shape),
        scratch_shapes=scratch,
        compiler_params=pltpu.CompilerParams(vmem_limit_bytes=VMEM_LIMIT),
        cost_estimate=pl.CostEstimate(
            flops=2 * count * width * (2 * q_cols + 2 * HD),
            bytes_accessed=2 * sum(a.size for a in held),
            transcendentals=count * LANES * span,
        ),
        name="decode_step",
    )(*x_blocks, order, lengths, cosine, sine, *earlier, *prompts, *held)


def settle_kernel(parts_ref, state_ref, gain_ref, next_ref, normed_ref):
    total = parts_ref[0].astype(jnp.float32)
    for d in range(1, parts_ref.shape[0]):
        total = total + parts_ref[d].astype(jnp.float32)
    state = (state_ref[...].astype(jnp.float32) + total).astype(jnp.bfloat16)
    next_ref[...] = state
    gain = gain_ref[...].astype(jnp.float32)
    normed_ref[...] = normed_rows(state.astype(jnp.float32), gain).astype(jnp.bfloat16)


def settle(parts, state, gain):
    shape = jax.ShapeDtypeStruct(state.shape, jnp.bfloat16)
    return pl.pallas_call(
        settle_kernel,
        out_shape=(shape, shape),
        in_specs=[whole()] * 3,
        out_specs=(whole(), whole()),
        compiler_params=pltpu.CompilerParams(vmem_limit_bytes=VMEM_LIMIT),
        name="settle",
    )(parts, state, gain)


def on_device(
    prompt_states,
    decode_states,
    norm_gain,
    w_query,
    w_keyvalue,
    w_output,
    cache_pages,
    page_table,
    cache_len,
    dest_rank,
    dest_page,
):
    rank = lax.axis_index("tensor")
    section = lax.axis_index("section")
    count = lax.axis_size("tensor")
    pool = cache_pages[0]
    page_size, kv_width = pool.shape[1:]
    own_table = page_table[0]
    lengths = cache_len[0]
    each, width = decode_states.shape[1:]
    tokens = prompt_states.shape[1]
    q_cols = w_query.shape[1]
    kv_heads = kv_width // (2 * HD)
    shared = count // kv_heads if count > kv_heads else 1
    gain = norm_gain[None, :]

    if w_keyvalue.shape[1] < 2 * HD:
        other = swap_xor(w_keyvalue, 1)
        is_key = rank % 2 == 0
        w_pair = jnp.concatenate(
            [jnp.where(is_key, w_keyvalue, other), jnp.where(is_key, other, w_keyvalue)], axis=1
        )
    else:
        w_pair = w_keyvalue

    half = tokens // 2
    ready = normalize(prompt_states[0], gain)
    pieces = [ready[:half], ready[half:]]
    pages = jnp.broadcast_to(own_table[:, :1], (each, HD)).astype(jnp.bfloat16)
    opened = opening(decode_states[0], gain, pages)
    heads = tuple(target // shared for target in range(count))
    parcels = make_parcels(own_table, pool, heads, 2 * HD)
    spread = along_grid if count == 8 else along_ring
    arrivals, opened, parcels, middle = spread(pieces, opened, parcels)
    blocks = [opened] + [swap_xor(opened, bits) for bits in range(1, count)]
    numbers = jnp.arange(count * each, dtype=jnp.int32)

    span = own_table.shape[1] * page_size
    parcels, blocks, _ = lax.optimization_barrier((parcels, blocks, middle))
    first_pages = jnp.concatenate([block[:, width:] for block in blocks])[:, 0].astype(jnp.int32)
    cache = lax.all_to_all(
        parcels.reshape(count, each * span, 2 * HD), "tensor", split_axis=0, concat_axis=0, tiled=True
    ).reshape(count * each, span, 2 * HD)

    products = [
        jnp.dot(rows, w_pair, preferred_element_type=jnp.float32) for _, _, rows in arrivals
    ]
    starts = jnp.stack([source * tokens + piece * half for source, piece, _ in arrivals])
    row_index = (starts[:, None] + jnp.arange(half, dtype=jnp.int32)[None, :]).reshape(-1)
    cosine, sine = rope_tables(row_index % PLEN)
    values = jnp.concatenate(products, axis=0)
    keys = values[:, :HD]
    keys = keys * cosine + jnp.roll(keys, HD // 2, axis=1) * sine
    prompt_kv = jnp.concatenate([keys, values[:, HD:]], axis=1).astype(jnp.bfloat16)
    sections = lax.axis_size("section")
    arrived = lax.ppermute(prompt_kv, "section", [(s, (s + 1) % sections) for s in range(sections)])

    anchor = (section + 1) % sections
    targets = lax.dynamic_index_in_dim(dest_rank, anchor, 0, keepdims=False)
    landing = lax.dynamic_index_in_dim(dest_page, anchor, 0, keepdims=False)[:, 0]
    rows_of = (rank ^ (numbers // each)) * each + numbers % each
    here = (rows_of[None, :] // each == targets[:, None]) & (first_pages[None, :] == landing[:, None])
    receivers = jnp.sum(jnp.where(here, rows_of[None, :], 0), axis=1)
    prompts = (receivers[starts // PLEN], starts % PLEN, arrived)
    held = (w_query, w_pair, w_output, cache)

    times = lengths[None, :] + jnp.arange(STEPS, dtype=jnp.int32)[:, None]
    cosine, sine = rope_tables(times.reshape(-1))
    cosine = cosine.reshape(STEPS, count * each, HD)
    sine = sine.reshape(STEPS, count * each, HD)
    chosen = (numbers[:, None] == rows_of[None, :]).astype(jnp.bfloat16)
    state = decode_states[0]
    outputs = []
    earlier = []
    for iteration in range(STEPS):
        parts, fresh, *fetched = step(
            blocks, chosen, lengths, cosine, sine, earlier, held, count, prompts
        )
        if iteration == 0:
            held, prompts = fetched, ()
        earlier.append(fresh)
        parts = lax.all_to_all(parts, "tensor", split_axis=0, concat_axis=0, tiled=True)
        state, normed = settle(parts, state, gain)
        outputs.append(state)
        if iteration + 1 < STEPS:
            blocks = [normed] + [swap_xor(normed, bits) for bits in range(1, count)]
    return jnp.stack(outputs)[:, None]


def solution(mesh):
    in_specs = (
        P(("groups", "section"), "tensor", None),
        P(("groups", "section"), "tensor", None),
        P(),
        P(None, "tensor"),
        P(None, "tensor"),
        P("tensor", None),
        P(("groups", "section"), "tensor", None, None),
        P(("groups", "section"), "tensor", None),
        P(("groups", "section"), None),
        P("groups", None),
        P("groups", None, None),
    )
    out_specs = P(None, ("groups", "section"), "tensor", None)
    return jax.shard_map(
        on_device, mesh=mesh, in_specs=in_specs, out_specs=out_specs, check_vma=False
    )
```

time: 385 us -> 330 us (0.86)
  blocking collectives: 187 us -> 68.6 us
  waiting for transfers between devices: 47.9 us -> 87.3 us
  starting transfers between devices: 55.3 us -> 93.3 us
  local copies, waits for them, and re-layouts: 33 us -> 8.17 us
  other arithmetic: 3.62 us -> 11.3 us
  matrix products: 14.2 us -> 18.5 us
    unnamed x1 -> x0, blocking collectives: 91.8 us -> none
    ppermute x14 -> x20, waiting for transfers between devices: 33.2 us -> 74.5 us  [the longest x8 74.4 us: cross(): return lax.ppermute(rows, 'tensor', [(r, r ^ 1) for r in range(8)])]
    all_gather x1 -> x0, blocking collectives: 31.8 us -> none  [on_device(): lax.all_gather(normalize(decode_states[0], gain), 'tensor', axis=0, tiled...]
    ppermute x14 -> x20, starting transfers between devices: 15.2 us -> 39.2 us  [the longest x12 23.2 us: shift(): return lax.ppermute(rows, 'tensor', pairs)]
    unnamed x53 -> x48, local copies, waits for them, and re-layouts: 28.7 us -> 5.76 us
    ppermute x21 -> x28, starting transfers between devices: 33.6 us -> 46.2 us  [swap_xor(): return lax.ppermute(value, 'tensor', [(s, s ^ mask) for s in range(count)])]
    select_n x2 -> x9, other arithmetic: 0.66 us -> 7.38 us  [the longest x6 7.34 us: pick(): jnp.where(z == 0, rows[0], jnp.where(z == 1, rows[1], jnp.where(z == 2, r...]
    pallas_call x3 -> x2, Pallas kernels: 15.3 us -> 9.11 us  [the longest x1 8.92 us: make_parcels(): pl.pallas_call(functools.partial(parcels_kernel, heads), out_shape=pltpu....]
  transfers between devices with their start and end apart: 37 -> 50, of which waited for: 16 -> 22; matrix products, arithmetic and copies ran while one was open for 5% -> 9% of each run, Pallas kernels for 3% -> 3%
where the time goes in v4:
time: 330 us; the launch traced here: 329 us
  starting transfers between devices  93.3 us (28%)
  waiting for transfers between devices  87.3 us (26%)
  blocking collectives  68.6 us (21%)
  Pallas kernels  41 us (12%)
  matrix products  18.5 us (6%)
  other arithmetic  11.3 us (3%)
  local copies, waits for them, and re-layouts  8.17 us (2%)
    ppermute x8, waiting for transfers between devices, cross(): return lax.ppermute(rows, 'tensor', [(r, r ^ 1) for r in range(8)])  74.4 us
    all_to_all x4, blocking collectives, on_device(): lax.all_to_all(parts, 'tensor', split_axis=0, concat_axis=0, tiled=True)  68.6 us
    ppermute x28, starting transfers between devices, swap_xor(): return lax.ppermute(value, 'tensor', [(s, s ^ mask) for s in range(count)])  46.2 us
    pallas_call x4, Pallas kernels, step(): pl.pallas_call(functools.partial(step_kernel, blocks, iteration), out_sha...  29.4 us
    ppermute x12, starting transfers between devices, shift(): return lax.ppermute(rows, 'tensor', pairs)  23.2 us
    dot_general x16, matrix products, on_device(): jnp.dot(rows, w_pair, preferred_element_type=jnp.float32)  18.5 us
    ppermute x8, starting transfers between devices, cross(): return lax.ppermute(rows, 'tensor', [(r, r ^ 1) for r in range(8)])  16 us
    ppermute x28, waiting for transfers between devices, swap_xor(): return lax.ppermute(value, 'tensor', [(s, s ^ mask) for s in range(count)])  12.5 us
  transfers between devices with their start and end apart: 50, of which 22 were waited for; matrix products, arithmetic and copies ran while one was open for 9% of the time, Pallas kernels for 3%

profile of v4, /device:TPU:0, one launch (start us, length us, event | category | flops | bytes accessed | tf_op | source)
XLA Modules:
  0.0 328.9 jit_solution(3280813722316487919)
XLA Ops:
  2.7 3.0 collective-permute-start.5
  7.1 5.4 %collective-permute-start.3 = (bf16[32,8192]{1,0:T(8,128)(2,1)S(1)}, bf16[32,8192]{1,0:T(8,128)(2,1)}, u32[]{:S(2)}, u32[]{:S(2)}) collective-permute-start(bf16[32,8192]{1,0:T(8,128)(2,1)S(1)} %get-tuple-element.77), channel_id=1, source_target_pairs={{0,4},{2,6},{4,8},{6,10},{8,12},{10,14},{1,5},{3,7},{5,9},{7,11},{... | collective-permute-start | bytes 1572872 | tf_op jit(solution)/shard_map/ppermute | solution.py:57
  15.1 3.4 %collective-permute-done.5 = bf16[32,8192]{1,0:T(8,128)(2,1)S(1)} collective-permute-done((bf16[32,8192]{1,0:T(8,128)(2,1)S(1)}, bf16[32,8192]{1,0:T(8,128)(2,1)S(1)}, u32[]{:S(2)}, u32[]{:S(2)}) %collective-permute-start.5) | collective-permute-done | bytes 524320 | tf_op jit(solution)/shard_map/ppermute | solution.py:60
  18.5 4.8 %collective-permute-start = (bf16[32,8192]{1,0:T(8,128)(2,1)S(1)}, bf16[32,8192]{1,0:T(8,128)(2,1)}, u32[]{:S(2)}, u32[]{:S(2)}) collective-permute-start(bf16[32,8192]{1,0:T(8,128)(2,1)S(1)} %get-tuple-element.67), channel_id=1, source_target_pairs={{0,4},{2,6},{4,8},{6,10},{8,12},{10,14},{1,5},{3,7},{5,9},{7,11},{... | collective-permute-start | bytes 1572872 | tf_op jit(solution)/shard_map/ppermute | solution.py:57
  23.6 2.2 copy-done.5
  25.8 8.9 %parcels.1 = bf16[8,64,16,256]{3,2,1,0:T(8,128)(2,1)} custom-call(s32[4,16]{1,0:T(4,128)S(1)} %bitcast.99, bf16[64,16,2048]{2,1,0:T(8,128)(2,1)S(1)} %bitcast.86), custom_call_target="tpu_custom_call" | custom-call | tf_op jit(solution)/shard_map/parcels/pallas_call | solution.py:176
  34.8 1.9 fusion.4
  36.7 1.6 collective-permute-start.12
  38.4 3.2 collective-permute-start.11
  41.6 1.5 collective-permute-start.13
  48.6 7.8 %collective-permute-done.15 = bf16[32,8192]{1,0:T(8,128)(2,1)S(1)} collective-permute-done((bf16[32,8192]{1,0:T(8,128)(2,1)S(1)}, bf16[32,8192]{1,0:T(8,128)(2,1)S(1)}, u32[]{:S(2)}, u32[]{:S(2)}) %collective-permute-start.15) | collective-permute-done | bytes 524320 | tf_op jit(solution)/shard_map/ppermute | solution.py:60
  56.4 4.1 %collective-permute-start.10 = (bf16[4,8320]{1,0:T(4,128)(2,1)S(1)}, bf16[4,8320]{1,0:T(4,128)(2,1)S(1)}, u32[]{:S(2)}, u32[]{:S(2)}) collective-permute-start(bf16[4,8320]{1,0:T(4,128)(2,1)S(1)} %opening.1.refs_0_), channel_id=1, source_target_pairs={{0,10},{2,8},{4,14},{6,12},{8,2},{10,0},{12,6},{14,4},{1,11},{3,9}... | collective-permute-start | bytes 199688 | tf_op jit(solution)/shard_map/ppermute | solution.py:27
  60.7 2.0 collective-permute-start.8
  68.4 1.5 collective-permute-start.16
  69.8 2.2 select_select_fusion.3
  74.8 7.8 %all-to-all-start = ((bf16[8,1024,256]{2,1,0:T(8,128)(2,1)}), bf16[8,1024,256]{2,1,0:T(8,128)(2,1)}, u32[]{:S(2)}, u32[]{:S(2)}) async-start(bf16[8,1024,256]{2,1,0:T(8,128)(2,1)} %bitcast.100), calls=%async_computation | async-start | bytes 8388608 | tf_op jit(solution)/shard_map/all_to_all | solution.py:447
  82.6 2.1 collective-permute-start.25
  87.7 3.8 %convolution_dynamic-update-slice_fusion.13 = f32[512,256]{1,0:T(8,128)} fusion(f32[512,256]{1,0:T(8,128)} %convolution_dynamic-update-slice_fusion.14, bf16[32,8192]{1,0:T(8,128)(2,1)S(1)} %select_select_fusion.5, bf16[8192,256]{1,0:T(8,128)(2,1)} %refs_16_.1), kind=kOutput, calls=%fused_computation.14 | convolution fusion | flops 134217728 | bytes 4751360 | tf_op jit(solution)/shard_map/dot_general | solution.py:452
  91.6 41.0 %collective-permute-done.25 = bf16[32,8192]{1,0:T(8,128)(2,1)S(1)} collective-permute-done((bf16[32,8192]{1,0:T(8,128)(2,1)S(1)}, bf16[32,8192]{1,0:T(8,128)(2,1)S(1)}, u32[]{:S(2)}, u32[]{:S(2)}) %collective-permute-start.25) | collective-permute-done | bytes 524320 | tf_op jit(solution)/shard_map/ppermute | solution.py:60
  134.8 2.5 collective-permute-start.26
  137.3 14.6 %collective-permute-done.21 = bf16[32,8192]{1,0:T(8,128)(2,1)S(1)} collective-permute-done((bf16[32,8192]{1,0:T(8,128)(2,1)S(1)}, bf16[32,8192]{1,0:T(8,128)(2,1)S(1)}, u32[]{:S(2)}, u32[]{:S(2)}) %collective-permute-start.21) | collective-permute-done | bytes 524320 | tf_op jit(solution)/shard_map/ppermute | solution.py:60
  152.1 5.9 %collective-permute-start.22 = (bf16[32,8192]{1,0:T(8,128)(2,1)S(1)}, bf16[32,8192]{1,0:T(8,128)(2,1)S(1)}, u32[]{:S(2)}, u32[]{:S(2)}) collective-permute-start(bf16[32,8192]{1,0:T(8,128)(2,1)S(1)} %select_select_fusion.4), channel_id=1, source_target_pairs={{0,2},{2,0},{4,6},{6,4},{8,10},{10,8},{12,14},{14,12},{1,3},{3,1},... | collective-permute-start | bytes 1572872 | tf_op jit(solution)/shard_map/ppermute | solution.py:60
  159.6 1.9 convolution_dynamic-update-slice_fusion.10
  162.3 7.7 %collective-permute-done.22 = bf16[32,8192]{1,0:T(8,128)(2,1)S(1)} collective-permute-done((bf16[32,8192]{1,0:T(8,128)(2,1)S(1)}, bf16[32,8192]{1,0:T(8,128)(2,1)S(1)}, u32[]{:S(2)}, u32[]{:S(2)}) %collective-permute-start.22) | collective-permute-done | bytes 524320 | tf_op jit(solution)/shard_map/ppermute | solution.py:60
  179.7 2.2 copy-done.4
  181.9 10.7 %decode_step.4 = (bf16[8,4,8192]{2,1,0:T(4,128)(2,1)S(1)}, bf16[32,256]{1,0:T(8,128)(2,1)S(1)}, bf16[8192,512]{1,0:T(8,128)(2,1)S(1)}, bf16[8192,256]{1,0:T(8,12...) custom-call(bf16[4,8320]{1,0:T(4,128)(2,1)S(1)} %opening.1.refs_0_, ...), custom_call_target="tpu_custom_call" | custom-call | flops 671088640 | bytes 25165824 | tf_op jit(solution)/shard_map/decode_step/pallas_call | solution.py:358
  192.6 21.2 %all_to_all.25.parts_ref = bf16[8,4,8192]{2,1,0:T(4,128)(2,1)S(1)} all-to-all(bf16[8,4,8192]{2,1,0:T(4,128)(2,1)S(1)} %get-tuple-element.85), channel_id=1, replica_groups=mesh['groups'=2,'tensor'=8,'section'=2] {'tensor'}, dimensions={0} | all-to-all | bytes 1048576 | tf_op jit(solution)/shard_map/all_to_all | solution.py:488
  214.1 2.4 collective-permute-start.34
  216.5 2.4 collective-permute-start.33
  218.9 2.9 collective-permute-start.31
  221.9 2.9 collective-permute-start.29
  225.3 2.2 collective-permute-done.32.refs_5_
  229.4 6.2 %decode_step.5 = (bf16[8,4,8192]{2,1,0:T(4,128)(2,1)S(1)}, bf16[32,256]{1,0:T(8,128)(2,1)S(1)}) custom-call(bf16[4,8192]{1,0:T(4,128)(2,1)S(1)} %get-tuple-element.87.refs_0_, bf16[4,8192]{1,0:T(4,128)(2,1)S(1)} %collective-permute-done.28.refs_1_, bf16[4,8192]{1,0:T(4,128)(2,1)S(1)} %collective-permute-done.29.refs_2_, ...), custom_call_target="tpu_custom_call" | custom-call | flops 671088640 | bytes 25165824 | tf_op jit(solution)/shard_map/decode_step/pallas_call | solution.py:358
  235.6 16.0 %all_to_all.26.parts_ref = bf16[8,4,8192]{2,1,0:T(4,128)(2,1)S(1)} all-to-all(bf16[8,4,8192]{2,1,0:T(4,128)(2,1)S(1)} %get-tuple-element.93), channel_id=1, replica_groups=mesh['groups'=2,'tensor'=8,'section'=2] {'tensor'}, dimensions={0} | all-to-all | bytes 1048576 | tf_op jit(solution)/shard_map/all_to_all | solution.py:488
  251.9 2.4 collective-permute-start.41
  254.3 2.4 collective-permute-start.40
  256.7 2.9 collective-permute-start.38
  259.7 2.9 collective-permute-start.36
  263.1 2.3 collective-permute-done.39.refs_5_
  267.2 6.2 %decode_step.6 = (bf16[8,4,8192]{2,1,0:T(4,128)(2,1)S(1)}, bf16[32,256]{1,0:T(8,128)(2,1)S(1)}) custom-call(bf16[4,8192]{1,0:T(4,128)(2,1)S(1)} %get-tuple-element.95.refs_0_, bf16[4,8192]{1,0:T(4,128)(2,1)S(1)} %collective-permute-done.35.refs_1_, bf16[4,8192]{1,0:T(4,128)(2,1)S(1)} %collective-permute-done.36.refs_2_, ...), custom_call_target="tpu_custom_call" | custom-call | flops 671088640 | bytes 25165824 | tf_op jit(solution)/shard_map/decode_step/pallas_call | solution.py:358
  273.4 15.9 %all_to_all.27.parts_ref = bf16[8,4,8192]{2,1,0:T(4,128)(2,1)S(1)} all-to-all(bf16[8,4,8192]{2,1,0:T(4,128)(2,1)S(1)} %get-tuple-element.97), channel_id=1, replica_groups=mesh['groups'=2,'tensor'=8,'section'=2] {'tensor'}, dimensions={0} | all-to-all | bytes 1048576 | tf_op jit(solution)/shard_map/all_to_all | solution.py:488
  289.6 2.4 collective-permute-start.48
  292.0 2.4 collective-permute-start.47
  294.4 2.9 collective-permute-start.45
  297.3 3.6 %collective-permute-start.43 = (bf16[4,8192]{1,0:T(4,128)(2,1)S(1)}, bf16[4,8192]{1,0:T(4,128)(2,1)S(1)}, u32[]{:S(2)}, u32[]{:S(2)}) collective-permute-start(bf16[4,8192]{1,0:T(4,128)(2,1)S(1)} %get-tuple-element.99.refs_0_), channel_id=1, source_target_pairs={{0,4},{2,6},{4,0},{6,2},{8,12},{10,14},{12,8},{14,10},{1,5},{3,7},... | collective-permute-start | bytes 196616 | tf_op jit(solution)/shard_map/ppermute | solution.py:27
  301.0 2.2 collective-permute-done.46.refs_5_
  305.3 6.3 %decode_step.7 = (bf16[8,4,8192]{2,1,0:T(4,128)(2,1)S(1)}, bf16[32,256]{1,0:T(8,128)(2,1)}) custom-call(bf16[4,8192]{1,0:T(4,128)(2,1)S(1)} %get-tuple-element.99.refs_0_, bf16[4,8192]{1,0:T(4,128)(2,1)S(1)} %collective-permute-done.42.refs_1_, bf16[4,8192]{1,0:T(4,128)(2,1)S(1)} %collective-permute-done.43.refs_2_, ...), custom_call_target="tpu_custom_call" | custom-call | flops 671088640 | bytes 25165824 | tf_op jit(solution)/shard_map/decode_step/pallas_call | solution.py:358
  311.5 15.5 %all_to_all.28.parts_ref = bf16[8,4,8192]{2,1,0:T(4,128)(2,1)S(1)} all-to-all(bf16[8,4,8192]{2,1,0:T(4,128)(2,1)S(1)} %get-tuple-element.101), channel_id=1, replica_groups=mesh['groups'=2,'tensor'=8,'section'=2] {'tensor'}, dimensions={0} | all-to-all | bytes 1048576 | tf_op jit(solution)/shard_map/all_to_all | solution.py:488
  (178 shorter events, 48.0 us)
Async XLA Ops:
  2.7 15.8 %collective-permute-start.5 = (bf16[32,8192]{1,0:T(8,128)(2,1)S(1)}, bf16[32,8192]{1,0:T(8,128)(2,1)S(1)}, u32[]{:S(2)}, u32[]{:S(2)}) collective-permute-start(bf16[32,8192]{1,0:T(8,128)(2,1)S(1)} %get-tuple-element.77), channel_id=1, source_target_pairs={{0,2},{2,0},{4,6},{6,4},{8,10},{10,8},{12,14},{14,12},{1,3},{3,1},... | collective-permute-start | bytes 1572872 | tf_op jit(solution)/shard_map/ppermute | solution.py:60
  5.8 30.9 %collective-permute-start.4 = (bf16[32,8192]{1,0:T(8,128)(2,1)S(1)}, bf16[32,8192]{1,0:T(8,128)(2,1)S(1)}, u32[]{:S(2)}, u32[]{:S(2)}) collective-permute-start(bf16[32,8192]{1,0:T(8,128)(2,1)S(1)} %get-tuple-element.77), channel_id=1, source_target_pairs={{4,0},{6,2},{8,4},{10,6},{12,8},{14,10},{5,1},{7,3},{9,5},{11,7},{... | collective-permute-start | bytes 1572872 | tf_op jit(solution)/shard_map/ppermute | solution.py:57
  7.1 29.6 %collective-permute-start.3 = (bf16[32,8192]{1,0:T(8,128)(2,1)S(1)}, bf16[32,8192]{1,0:T(8,128)(2,1)}, u32[]{:S(2)}, u32[]{:S(2)}) collective-permute-start(bf16[32,8192]{1,0:T(8,128)(2,1)S(1)} %get-tuple-element.77), channel_id=1, source_target_pairs={{0,4},{2,6},{4,8},{6,10},{8,12},{10,14},{1,5},{3,7},{5,9},{7,11},{... | collective-permute-start | bytes 1572872 | tf_op jit(solution)/shard_map/ppermute | solution.py:57
  12.5 24.2 %collective-permute-start.2 = (bf16[32,8192]{1,0:T(8,128)(2,1)S(1)}, bf16[32,8192]{1,0:T(8,128)(2,1)S(1)}, u32[]{:S(2)}, u32[]{:S(2)}) collective-permute-start(bf16[32,8192]{1,0:T(8,128)(2,1)S(1)} %get-tuple-element.67), channel_id=1, source_target_pairs={{0,2},{2,0},{4,6},{6,4},{8,10},{10,8},{12,14},{14,12},{1,3},{3,1},... | collective-permute-start | bytes 1572872 | tf_op jit(solution)/shard_map/ppermute | solution.py:60
  12.5 24.2 %collective-permute-start.1 = (bf16[32,8192]{1,0:T(8,128)(2,1)S(1)}, bf16[32,8192]{1,0:T(8,128)(2,1)S(1)}, u32[]{:S(2)}, u32[]{:S(2)}) collective-permute-start(bf16[32,8192]{1,0:T(8,128)(2,1)S(1)} %get-tuple-element.67), channel_id=1, source_target_pairs={{4,0},{6,2},{8,4},{10,6},{12,8},{14,10},{5,1},{7,3},{9,5},{11,7},{... | collective-permute-start | bytes 1572872 | tf_op jit(solution)/shard_map/ppermute | solution.py:57
  18.5 18.2 %collective-permute-start = (bf16[32,8192]{1,0:T(8,128)(2,1)S(1)}, bf16[32,8192]{1,0:T(8,128)(2,1)}, u32[]{:S(2)}, u32[]{:S(2)}) collective-permute-start(bf16[32,8192]{1,0:T(8,128)(2,1)S(1)} %get-tuple-element.67), channel_id=1, source_target_pairs={{0,4},{2,6},{4,8},{6,10},{8,12},{10,14},{1,5},{3,7},{5,9},{7,11},{... | collective-permute-start | bytes 1572872 | tf_op jit(solution)/shard_map/ppermute | solution.py:57
  36.7 27.4 %collective-permute-start.12 = (bf16[4,8320]{1,0:T(4,128)(2,1)S(1)}, bf16[4,8320]{1,0:T(4,128)(2,1)S(1)}, u32[]{:S(2)}, u32[]{:S(2)}) collective-permute-start(bf16[4,8320]{1,0:T(4,128)(2,1)S(1)} %opening.1.refs_0_), channel_id=1, source_target_pairs={{0,14},{2,12},{4,10},{6,8},{8,6},{10,4},{12,2},{14,0},{1,15},{3,13... | collective-permute-start | bytes 199688 | tf_op jit(solution)/shard_map/ppermute | solution.py:27
  38.4 26.7 %collective-permute-start.11 = (bf16[4,8320]{1,0:T(4,128)(2,1)S(1)}, bf16[4,8320]{1,0:T(4,128)(2,1)S(1)}, u32[]{:S(2)}, u32[]{:S(2)}) collective-permute-start(bf16[4,8320]{1,0:T(4,128)(2,1)S(1)} %opening.1.refs_0_), channel_id=1, source_target_pairs={{0,12},{2,14},{4,8},{6,10},{8,4},{10,6},{12,0},{14,2},{1,13},{3,15... | collective-permute-start | bytes 199688 | tf_op jit(solution)/shard_map/ppermute | solution.py:27
  41.6 19.0 %collective-permute-start.13 = (bf16[32,8192]{1,0:T(8,128)(2,1)}, bf16[32,8192]{1,0:T(8,128)(2,1)}, u32[]{:S(2)}, u32[]{:S(2)}) collective-permute-start(bf16[32,8192]{1,0:T(8,128)(2,1)} %collective-permute-done.3), channel_id=1, source_target_pairs={{4,8},{6,10},{8,12},{10,14},{5,9},{7,11},{9,13},{11,15},{20,24},{2... | collective-permute-start | bytes 1572872 | tf_op jit(solution)/shard_map/ppermute | solution.py:57
  43.0 17.6 %collective-permute-start.14 = (bf16[32,8192]{1,0:T(8,128)(2,1)S(1)}, bf16[32,8192]{1,0:T(8,128)(2,1)}, u32[]{:S(2)}, u32[]{:S(2)}) collective-permute-start(bf16[32,8192]{1,0:T(8,128)(2,1)S(1)} %collective-permute-done.4), channel_id=1, source_target_pairs={{4,0},{6,2},{8,4},{10,6},{5,1},{7,3},{9,5},{11,7},{20,16},{22,18},... | collective-permute-start | bytes 1572872 | tf_op jit(solution)/shard_map/ppermute | solution.py:57
  45.5 11.0 %collective-permute-start.15 = (bf16[32,8192]{1,0:T(8,128)(2,1)S(1)}, bf16[32,8192]{1,0:T(8,128)(2,1)S(1)}, u32[]{:S(2)}, u32[]{:S(2)}) collective-permute-start(bf16[32,8192]{1,0:T(8,128)(2,1)S(1)} %fusion.1), channel_id=1, source_target_pairs={{0,2},{2,0},{4,6},{6,4},{8,10},{10,8},{12,14},{14,12},{1,3},{3,1},... | collective-permute-start | bytes 1572872 | tf_op jit(solution)/shard_map/ppermute | solution.py:60
  56.4 9.1 %collective-permute-start.10 = (bf16[4,8320]{1,0:T(4,128)(2,1)S(1)}, bf16[4,8320]{1,0:T(4,128)(2,1)S(1)}, u32[]{:S(2)}, u32[]{:S(2)}) collective-permute-start(bf16[4,8320]{1,0:T(4,128)(2,1)S(1)} %opening.1.refs_0_), channel_id=1, source_target_pairs={{0,10},{2,8},{4,14},{6,12},{8,2},{10,0},{12,6},{14,4},{1,11},{3,9}... | collective-permute-start | bytes 199688 | tf_op jit(solution)/shard_map/ppermute | solution.py:27
  60.5 6.5 %collective-permute-start.9 = (bf16[4,8320]{1,0:T(4,128)(2,1)S(1)}, bf16[4,8320]{1,0:T(4,128)(2,1)S(1)}, u32[]{:S(2)}, u32[]{:S(2)}) collective-permute-start(bf16[4,8320]{1,0:T(4,128)(2,1)S(1)} %opening.1.refs_0_), channel_id=1, source_target_pairs={{0,8},{2,10},{4,12},{6,14},{8,0},{10,2},{12,4},{14,6},{1,9},{3,11}... | collective-permute-start | bytes 199688 | tf_op jit(solution)/shard_map/ppermute | solution.py:27
  60.7 7.7 %collective-permute-start.8 = (bf16[4,8320]{1,0:T(4,128)(2,1)S(1)}, bf16[4,8320]{1,0:T(4,128)(2,1)S(1)}, u32[]{:S(2)}, u32[]{:S(2)}) collective-permute-start(bf16[4,8320]{1,0:T(4,128)(2,1)S(1)} %opening.1.refs_0_), channel_id=1, source_target_pairs={{0,6},{2,4},{4,2},{6,0},{8,14},{10,12},{12,10},{14,8},{1,7},{3,5},... | collective-permute-start | bytes 199688 | tf_op jit(solution)/shard_map/ppermute | solution.py:27
  64.1 7.9 %collective-permute-start.7 = (bf16[4,8320]{1,0:T(4,128)(2,1)S(1)}, bf16[4,8320]{1,0:T(4,128)(2,1)S(1)}, u32[]{:S(2)}, u32[]{:S(2)}) collective-permute-start(bf16[4,8320]{1,0:T(4,128)(2,1)S(1)} %opening.1.refs_0_), channel_id=1, source_target_pairs={{0,4},{2,6},{4,0},{6,2},{8,12},{10,14},{12,8},{14,10},{1,5},{3,7},... | collective-permute-start | bytes 199688 | tf_op jit(solution)/shard_map/ppermute | solution.py:27
  65.0 8.3 %collective-permute-start.6 = (bf16[4,8320]{1,0:T(4,128)(2,1)S(1)}, bf16[4,8320]{1,0:T(4,128)(2,1)S(1)}, u32[]{:S(2)}, u32[]{:S(2)}) collective-permute-start(bf16[4,8320]{1,0:T(4,128)(2,1)S(1)} %opening.1.refs_0_), channel_id=1, source_target_pairs={{0,2},{2,0},{4,6},{6,4},{8,10},{10,8},{12,14},{14,12},{1,3},{3,1},... | collective-permute-start | bytes 199688 | tf_op jit(solution)/shard_map/ppermute | solution.py:27
  65.6 17.0 %collective-permute-start.18 = (bf16[32,8192]{1,0:T(8,128)(2,1)S(1)}, bf16[32,8192]{1,0:T(8,128)(2,1)}, u32[]{:S(2)}, u32[]{:S(2)}) collective-permute-start(bf16[32,8192]{1,0:T(8,128)(2,1)S(1)} %fusion), channel_id=1, source_target_pairs={{0,2},{2,0},{4,6},{6,4},{8,10},{10,8},{12,14},{14,12},{1,3},{3,1},... | collective-permute-start | bytes 1572872 | tf_op jit(solution)/shard_map/ppermute | solution.py:60
  67.1 17.6 %collective-permute-start.17 = (bf16[32,8192]{1,0:T(8,128)(2,1)S(1)}, bf16[32,8192]{1,0:T(8,128)(2,1)}, u32[]{:S(2)}, u32[]{:S(2)}) collective-permute-start(bf16[32,8192]{1,0:T(8,128)(2,1)S(1)} %collective-permute-done.1), channel_id=1, source_target_pairs={{4,0},{6,2},{8,4},{10,6},{5,1},{7,3},{9,5},{11,7},{20,16},{22,18},... | collective-permute-start | bytes 1572872 | tf_op jit(solution)/shard_map/ppermute | solution.py:57
  68.4 16.3 %collective-permute-start.16 = (bf16[32,8192]{1,0:T(8,128)(2,1)}, bf16[32,8192]{1,0:T(8,128)(2,1)}, u32[]{:S(2)}, u32[]{:S(2)}) collective-permute-start(bf16[32,8192]{1,0:T(8,128)(2,1)} %collective-permute-done), channel_id=1, source_target_pairs={{4,8},{6,10},{8,12},{10,14},{5,9},{7,11},{9,13},{11,15},{20,24},{2... | collective-permute-start | bytes 1572872 | tf_op jit(solution)/shard_map/ppermute | solution.py:57
  72.0 61.4 %collective-permute-start.24 = (bf16[32,8192]{1,0:T(8,128)(2,1)}, bf16[32,8192]{1,0:T(8,128)(2,1)}, u32[]{:S(2)}, u32[]{:S(2)}) collective-permute-start(bf16[32,8192]{1,0:T(8,128)(2,1)} %collective-permute-done.14), channel_id=1, source_target_pairs={{4,0},{6,2},{5,1},{7,3},{20,16},{22,18},{21,17},{23,19}} | collective-permute-start | bytes 1572872 | tf_op jit(solution)/shard_map/ppermute | solution.py:57
  73.3 60.1 %collective-permute-start.23 = (bf16[32,8192]{1,0:T(8,128)(2,1)}, bf16[32,8192]{1,0:T(8,128)(2,1)}, u32[]{:S(2)}, u32[]{:S(2)}) collective-permute-start(bf16[32,8192]{1,0:T(8,128)(2,1)} %collective-permute-done.13), channel_id=1, source_target_pairs={{8,12},{10,14},{9,13},{11,15},{24,28},{26,30},{25,29},{27,31}} | collective-permute-start | bytes 1572872 | tf_op jit(solution)/shard_map/ppermute | solution.py:57
  74.8 104.9 %all-to-all-start = ((bf16[8,1024,256]{2,1,0:T(8,128)(2,1)}), bf16[8,1024,256]{2,1,0:T(8,128)(2,1)}, u32[]{:S(2)}, u32[]{:S(2)}) async-start(bf16[8,1024,256]{2,1,0:T(8,128)(2,1)} %bitcast.100), calls=%async_computation | async-start | bytes 8388608 | tf_op jit(solution)/shard_map/all_to_all | solution.py:447
  82.6 50.0 %collective-permute-start.25 = (bf16[32,8192]{1,0:T(8,128)(2,1)S(1)}, bf16[32,8192]{1,0:T(8,128)(2,1)S(1)}, u32[]{:S(2)}, u32[]{:S(2)}) collective-permute-start(bf16[32,8192]{1,0:T(8,128)(2,1)S(1)} %copy-done.12), channel_id=1, source_target_pairs={{0,2},{2,0},{4,6},{6,4},{8,10},{10,8},{12,14},{14,12},{1,3},{3,1},... | collective-permute-start | bytes 1572872 | tf_op jit(solution)/shard_map/ppermute | solution.py:60
  84.7 67.2 %collective-permute-start.20 = (bf16[32,8192]{1,0:T(8,128)(2,1)}, bf16[32,8192]{1,0:T(8,128)(2,1)S(1)}, u32[]{:S(2)}, u32[]{:S(2)}) collective-permute-start(bf16[32,8192]{1,0:T(8,128)(2,1)} %collective-permute-done.17), channel_id=1, source_target_pairs={{4,0},{6,2},{5,1},{7,3},{20,16},{22,18},{21,17},{23,19}} | collective-permute-start | bytes 1572872 | tf_op jit(solution)/shard_map/ppermute | solution.py:57
  87.4 64.5 %collective-permute-start.21 = (bf16[32,8192]{1,0:T(8,128)(2,1)S(1)}, bf16[32,8192]{1,0:T(8,128)(2,1)S(1)}, u32[]{:S(2)}, u32[]{:S(2)}) collective-permute-start(bf16[32,8192]{1,0:T(8,128)(2,1)S(1)} %select_select_fusion.5), channel_id=1, source_target_pairs={{0,2},{2,0},{4,6},{6,4},{8,10},{10,8},{12,14},{14,12},{1,3},{3,1},... | collective-permute-start | bytes 1572872 | tf_op jit(solution)/shard_map/ppermute | solution.py:60
  132.6 19.3 %collective-permute-start.19 = (bf16[32,8192]{1,0:T(8,128)(2,1)}, bf16[32,8192]{1,0:T(8,128)(2,1)S(1)}, u32[]{:S(2)}, u32[]{:S(2)}) collective-permute-start(bf16[32,8192]{1,0:T(8,128)(2,1)} %collective-permute-done.16), channel_id=1, source_target_pairs={{8,12},{10,14},{9,13},{11,15},{24,28},{26,30},{25,29},{27,31}} | collective-permute-start | bytes 1572872 | tf_op jit(solution)/shard_map/ppermute | solution.py:57
  134.8 41.9 %collective-permute-start.26 = (bf16[32,8192]{1,0:T(8,128)(2,1)S(1)}, bf16[32,8192]{1,0:T(8,128)(2,1)S(1)}, u32[]{:S(2)}, u32[]{:S(2)}) collective-permute-start(bf16[32,8192]{1,0:T(8,128)(2,1)S(1)} %select_select_fusion.2), channel_id=1, source_target_pairs={{0,2},{2,0},{4,6},{6,4},{8,10},{10,8},{12,14},{14,12},{1,3},{3,1},... | collective-permute-start | bytes 1572872 | tf_op jit(solution)/shard_map/ppermute | solution.py:60
  152.1 17.9 %collective-permute-start.22 = (bf16[32,8192]{1,0:T(8,128)(2,1)S(1)}, bf16[32,8192]{1,0:T(8,128)(2,1)S(1)}, u32[]{:S(2)}, u32[]{:S(2)}) collective-permute-start(bf16[32,8192]{1,0:T(8,128)(2,1)S(1)} %select_select_fusion.4), channel_id=1, source_target_pairs={{0,2},{2,0},{4,6},{6,4},{8,10},{10,8},{12,14},{14,12},{1,3},{3,1},... | collective-permute-start | bytes 1572872 | tf_op jit(solution)/shard_map/ppermute | solution.py:60
  214.1 7.8 %collective-permute-start.34 = (bf16[4,8192]{1,0:T(4,128)(2,1)S(1)}, bf16[4,8192]{1,0:T(4,128)(2,1)S(1)}, u32[]{:S(2)}, u32[]{:S(2)}) collective-permute-start(bf16[4,8192]{1,0:T(4,128)(2,1)S(1)} %get-tuple-element.87.refs_0_), channel_id=1, source_target_pairs={{0,14},{2,12},{4,10},{6,8},{8,6},{10,4},{12,2},{14,0},{1,15},{3,13... | collective-permute-start | bytes 196616 | tf_op jit(solution)/shard_map/ppermute | solution.py:27
  216.5 8.2 %collective-permute-start.33 = (bf16[4,8192]{1,0:T(4,128)(2,1)S(1)}, bf16[4,8192]{1,0:T(4,128)(2,1)S(1)}, u32[]{:S(2)}, u32[]{:S(2)}) collective-permute-start(bf16[4,8192]{1,0:T(4,128)(2,1)S(1)} %get-tuple-element.87.refs_0_), channel_id=1, source_target_pairs={{0,12},{2,14},{4,8},{6,10},{8,4},{10,6},{12,0},{14,2},{1,13},{3,15... | collective-permute-start | bytes 196616 | tf_op jit(solution)/shard_map/ppermute | solution.py:27
  218.9 8.6 %collective-permute-start.32 = (bf16[4,8192]{1,0:T(4,128)(2,1)S(1)}, bf16[4,8192]{1,0:T(4,128)(2,1)S(1)}, u32[]{:S(2)}, u32[]{:S(2)}) collective-permute-start(bf16[4,8192]{1,0:T(4,128)(2,1)S(1)} %get-tuple-element.87.refs_0_), channel_id=1, source_target_pairs={{0,10},{2,8},{4,14},{6,12},{8,2},{10,0},{12,6},{14,4},{1,11},{3,9}... | collective-permute-start | bytes 196616 | tf_op jit(solution)/shard_map/ppermute | solution.py:27
  218.9 9.1 %collective-permute-start.31 = (bf16[4,8192]{1,0:T(4,128)(2,1)S(1)}, bf16[4,8192]{1,0:T(4,128)(2,1)S(1)}, u32[]{:S(2)}, u32[]{:S(2)}) collective-permute-start(bf16[4,8192]{1,0:T(4,128)(2,1)S(1)} %get-tuple-element.87.refs_0_), channel_id=1, source_target_pairs={{0,8},{2,10},{4,12},{6,14},{8,0},{10,2},{12,4},{14,6},{1,9},{3,11}... | collective-permute-start | bytes 196616 | tf_op jit(solution)/shard_map/ppermute | solution.py:27
  221.8 7.1 %collective-permute-start.30 = (bf16[4,8192]{1,0:T(4,128)(2,1)S(1)}, bf16[4,8192]{1,0:T(4,128)(2,1)S(1)}, u32[]{:S(2)}, u32[]{:S(2)}) collective-permute-start(bf16[4,8192]{1,0:T(4,128)(2,1)S(1)} %get-tuple-element.87.refs_0_), channel_id=1, source_target_pairs={{0,6},{2,4},{4,2},{6,0},{8,14},{10,12},{12,10},{14,8},{1,7},{3,5},... | collective-permute-start | bytes 196616 | tf_op jit(solution)/shard_map/ppermute | solution.py:27
  221.9 7.4 %collective-permute-start.29 = (bf16[4,8192]{1,0:T(4,128)(2,1)S(1)}, bf16[4,8192]{1,0:T(4,128)(2,1)S(1)}, u32[]{:S(2)}, u32[]{:S(2)}) collective-permute-start(bf16[4,8192]{1,0:T(4,128)(2,1)S(1)} %get-tuple-element.87.refs_0_), channel_id=1, source_target_pairs={{0,4},{2,6},{4,0},{6,2},{8,12},{10,14},{12,8},{14,10},{1,5},{3,7},... | collective-permute-start | bytes 196616 | tf_op jit(solution)/shard_map/ppermute | solution.py:27
  224.8 4.6 %collective-permute-start.28 = (bf16[4,8192]{1,0:T(4,128)(2,1)S(1)}, bf16[4,8192]{1,0:T(4,128)(2,1)S(1)}, u32[]{:S(2)}, u32[]{:S(2)}) collective-permute-start(bf16[4,8192]{1,0:T(4,128)(2,1)S(1)} %get-tuple-element.87.refs_0_), channel_id=1, source_target_pairs={{0,2},{2,0},{4,6},{6,4},{8,10},{10,8},{12,14},{14,12},{1,3},{3,1},... | collective-permute-start | bytes 196616 | tf_op jit(solution)/shard_map/ppermute | solution.py:27
  251.9 7.8 %collective-permute-start.41 = (bf16[4,8192]{1,0:T(4,128)(2,1)S(1)}, bf16[4,8192]{1,0:T(4,128)(2,1)S(1)}, u32[]{:S(2)}, u32[]{:S(2)}) collective-permute-start(bf16[4,8192]{1,0:T(4,128)(2,1)S(1)} %get-tuple-element.95.refs_0_), channel_id=1, source_target_pairs={{0,14},{2,12},{4,10},{6,8},{8,6},{10,4},{12,2},{14,0},{1,15},{3,13... | collective-permute-start | bytes 196616 | tf_op jit(solution)/shard_map/ppermute | solution.py:27
  254.3 8.2 %collective-permute-start.40 = (bf16[4,8192]{1,0:T(4,128)(2,1)S(1)}, bf16[4,8192]{1,0:T(4,128)(2,1)S(1)}, u32[]{:S(2)}, u32[]{:S(2)}) collective-permute-start(bf16[4,8192]{1,0:T(4,128)(2,1)S(1)} %get-tuple-element.95.refs_0_), channel_id=1, source_target_pairs={{0,12},{2,14},{4,8},{6,10},{8,4},{10,6},{12,0},{14,2},{1,13},{3,15... | collective-permute-start | bytes 196616 | tf_op jit(solution)/shard_map/ppermute | solution.py:27
  256.7 8.7 %collective-permute-start.39 = (bf16[4,8192]{1,0:T(4,128)(2,1)S(1)}, bf16[4,8192]{1,0:T(4,128)(2,1)S(1)}, u32[]{:S(2)}, u32[]{:S(2)}) collective-permute-start(bf16[4,8192]{1,0:T(4,128)(2,1)S(1)} %get-tuple-element.95.refs_0_), channel_id=1, source_target_pairs={{0,10},{2,8},{4,14},{6,12},{8,2},{10,0},{12,6},{14,4},{1,11},{3,9}... | collective-permute-start | bytes 196616 | tf_op jit(solution)/shard_map/ppermute | solution.py:27
  256.7 8.9 %collective-permute-start.38 = (bf16[4,8192]{1,0:T(4,128)(2,1)S(1)}, bf16[4,8192]{1,0:T(4,128)(2,1)S(1)}, u32[]{:S(2)}, u32[]{:S(2)}) collective-permute-start(bf16[4,8192]{1,0:T(4,128)(2,1)S(1)} %get-tuple-element.95.refs_0_), channel_id=1, source_target_pairs={{0,8},{2,10},{4,12},{6,14},{8,0},{10,2},{12,4},{14,6},{1,9},{3,11}... | collective-permute-start | bytes 196616 | tf_op jit(solution)/shard_map/ppermute | solution.py:27
  259.6 7.1 %collective-permute-start.37 = (bf16[4,8192]{1,0:T(4,128)(2,1)S(1)}, bf16[4,8192]{1,0:T(4,128)(2,1)S(1)}, u32[]{:S(2)}, u32[]{:S(2)}) collective-permute-start(bf16[4,8192]{1,0:T(4,128)(2,1)S(1)} %get-tuple-element.95.refs_0_), channel_id=1, source_target_pairs={{0,6},{2,4},{4,2},{6,0},{8,14},{10,12},{12,10},{14,8},{1,7},{3,5},... | collective-permute-start | bytes 196616 | tf_op jit(solution)/shard_map/ppermute | solution.py:27
  259.7 7.3 %collective-permute-start.36 = (bf16[4,8192]{1,0:T(4,128)(2,1)S(1)}, bf16[4,8192]{1,0:T(4,128)(2,1)S(1)}, u32[]{:S(2)}, u32[]{:S(2)}) collective-permute-start(bf16[4,8192]{1,0:T(4,128)(2,1)S(1)} %get-tuple-element.95.refs_0_), channel_id=1, source_target_pairs={{0,4},{2,6},{4,0},{6,2},{8,12},{10,14},{12,8},{14,10},{1,5},{3,7},... | collective-permute-start | bytes 196616 | tf_op jit(solution)/shard_map/ppermute | solution.py:27
  262.5 4.6 %collective-permute-start.35 = (bf16[4,8192]{1,0:T(4,128)(2,1)S(1)}, bf16[4,8192]{1,0:T(4,128)(2,1)S(1)}, u32[]{:S(2)}, u32[]{:S(2)}) collective-permute-start(bf16[4,8192]{1,0:T(4,128)(2,1)S(1)} %get-tuple-element.95.refs_0_), channel_id=1, source_target_pairs={{0,2},{2,0},{4,6},{6,4},{8,10},{10,8},{12,14},{14,12},{1,3},{3,1},... | collective-permute-start | bytes 196616 | tf_op jit(solution)/shard_map/ppermute | solution.py:27
  289.6 7.7 %collective-permute-start.48 = (bf16[4,8192]{1,0:T(4,128)(2,1)S(1)}, bf16[4,8192]{1,0:T(4,128)(2,1)S(1)}, u32[]{:S(2)}, u32[]{:S(2)}) collective-permute-start(bf16[4,8192]{1,0:T(4,128)(2,1)S(1)} %get-tuple-element.99.refs_0_), channel_id=1, source_target_pairs={{0,14},{2,12},{4,10},{6,8},{8,6},{10,4},{12,2},{14,0},{1,15},{3,13... | collective-permute-start | bytes 196616 | tf_op jit(solution)/shard_map/ppermute | solution.py:27
  292.0 8.9 %collective-permute-start.47 = (bf16[4,8192]{1,0:T(4,128)(2,1)S(1)}, bf16[4,8192]{1,0:T(4,128)(2,1)S(1)}, u32[]{:S(2)}, u32[]{:S(2)}) collective-permute-start(bf16[4,8192]{1,0:T(4,128)(2,1)S(1)} %get-tuple-element.99.refs_0_), channel_id=1, source_target_pairs={{0,12},{2,14},{4,8},{6,10},{8,4},{10,6},{12,0},{14,2},{1,13},{3,15... | collective-permute-start | bytes 196616 | tf_op jit(solution)/shard_map/ppermute | solution.py:27
  294.4 8.8 %collective-permute-start.46 = (bf16[4,8192]{1,0:T(4,128)(2,1)S(1)}, bf16[4,8192]{1,0:T(4,128)(2,1)S(1)}, u32[]{:S(2)}, u32[]{:S(2)}) collective-permute-start(bf16[4,8192]{1,0:T(4,128)(2,1)S(1)} %get-tuple-element.99.refs_0_), channel_id=1, source_target_pairs={{0,10},{2,8},{4,14},{6,12},{8,2},{10,0},{12,6},{14,4},{1,11},{3,9}... | collective-permute-start | bytes 196616 | tf_op jit(solution)/shard_map/ppermute | solution.py:27
  294.4 8.9 %collective-permute-start.45 = (bf16[4,8192]{1,0:T(4,128)(2,1)S(1)}, bf16[4,8192]{1,0:T(4,128)(2,1)S(1)}, u32[]{:S(2)}, u32[]{:S(2)}) collective-permute-start(bf16[4,8192]{1,0:T(4,128)(2,1)S(1)} %get-tuple-element.99.refs_0_), channel_id=1, source_target_pairs={{0,8},{2,10},{4,12},{6,14},{8,0},{10,2},{12,4},{14,6},{1,9},{3,11}... | collective-permute-start | bytes 196616 | tf_op jit(solution)/shard_map/ppermute | solution.py:27
  297.3 6.8 %collective-permute-start.44 = (bf16[4,8192]{1,0:T(4,128)(2,1)S(1)}, bf16[4,8192]{1,0:T(4,128)(2,1)S(1)}, u32[]{:S(2)}, u32[]{:S(2)}) collective-permute-start(bf16[4,8192]{1,0:T(4,128)(2,1)S(1)} %get-tuple-element.99.refs_0_), channel_id=1, source_target_pairs={{0,6},{2,4},{4,2},{6,0},{8,14},{10,12},{12,10},{14,8},{1,7},{3,5},... | collective-permute-start | bytes 196616 | tf_op jit(solution)/shard_map/ppermute | solution.py:27
  297.3 7.3 %collective-permute-start.43 = (bf16[4,8192]{1,0:T(4,128)(2,1)S(1)}, bf16[4,8192]{1,0:T(4,128)(2,1)S(1)}, u32[]{:S(2)}, u32[]{:S(2)}) collective-permute-start(bf16[4,8192]{1,0:T(4,128)(2,1)S(1)} %get-tuple-element.99.refs_0_), channel_id=1, source_target_pairs={{0,4},{2,6},{4,0},{6,2},{8,12},{10,14},{12,8},{14,10},{1,5},{3,7},... | collective-permute-start | bytes 196616 | tf_op jit(solution)/shard_map/ppermute | solution.py:27
  (26 other events, 371.4 us)
